TPU v7x, 128 devices: a whole 4x4x4 slice. The times are simulated.
128 devices in a mesh: row: 16 (over y, x), samp: 8 (over z, core).
Axes of the slice: x: 4, y: 4, z: 4, core: 2. Of those that a mesh axis runs over, the one named last changes fastest.
Arguments:
- fibres_first: float32 [16384, 16384], P('row', 'samp'), may hold values from -768 to 768
- fibres_second: float32 [16384, 16384], P('row', 'samp'), may hold values from -768 to 768
- index_first: int32 [16384, 2], P('samp'), may hold values from 0 to 16383, as said below
- index_second: int32 [16384, 2], P('samp'), may hold values from 0 to 16383, as said below
- factor_b: float32 [16384, 256], P('row'), may hold values from -6 to 6
- factor_c: float32 [16384, 256], P('row'), may hold values from -6 to 6
Outputs:
- factor_a: float32 [16384, 256], P('row')
- factor_b_new: float32 [16384, 256], P('row')
- weights: float32 [256], replicated
Inputs may be any that keep to these rules, and one draw needn't show every extreme that they name: `index_first`: in each aligned block of 128 samples and in each column, at most 16 indices fall into the range of one block of 1024 factor rows; in every block some range takes exactly 16. `index_second`: in each aligned block of 128 samples and in each column, at most 16 indices fall into the range of one block of 1024 factor rows; in every block some range takes exactly 16.
All inputs are finite; a program needn't handle non-finite values.
Results may differ from a plain program's by a relative error of at most 0.00017.
Values sent between devices are 32-bit elements; how exact they have to be, the bound alone decides.
No kernel may reach another device: no remote copies, remote signals or barrier semaphores. Data moves between devices by JAX's collectives and lax.ppermute only.
A program may use at most 128 MiB of HBM per device.

v0:
```python
import jax
import jax.numpy as jnp
from jax import lax
from jax.experimental import pallas as pl
from jax.experimental.pallas import tpu as pltpu
from jax.sharding import PartitionSpec as P

F32, BF16 = jnp.float32, jnp.bfloat16
CAP = 16
BLOCK = 128
HIGHEST = lax.Precision.HIGHEST
VMEM = pl.BlockSpec(memory_space=pltpu.VMEM)
CORE = [(i, i ^ 1) for i in range(8)]
FAR_FIRST = (2, 1, 3)


def in_plane(down, right):
    return [(row, (row // 4 + down) % 4 * 4 + (row + right) % 4) for row in range(16)]


def along_z(step):
    return [(2 * z + c, (2 * z + 2 * step) % 8 + c) for z in range(4) for c in range(2)]


def call(kernel, out, *args, flops=0, size=0, specs=None, **kwargs):
    return pl.pallas_call(
        kernel,
        out_shape=out,
        in_specs=specs or [VMEM] * len(args),
        out_specs=jax.tree.map(lambda _: VMEM, out),
        cost_estimate=pl.CostEstimate(flops=flops, bytes_accessed=size, transcendentals=0),
        compiler_params=pltpu.CompilerParams(vmem_limit_bytes=32 * 2**20),
        **kwargs,
    )(*args)


def shape(*dims, dtype=F32):
    return jax.ShapeDtypeStruct(dims, dtype)


def dot(a, b, dims=(1, 0)):
    return lax.dot_general(a, b, (((dims[0],), (dims[1],)), ((), ())), precision=HIGHEST, preferred_element_type=F32)


def bf16_dot(a, b):
    return jnp.dot(a, b, preferred_element_type=F32)


def halves(x):
    high = x.astype(BF16)
    return high, (x - high.astype(F32)).astype(BF16)


def pick(onehot, x):
    high, low = halves(x)
    return bf16_dot(onehot, high) + bf16_dot(onehot, low)


def position():
    samp = lax.axis_index("samp")
    return lax.shift_right_logical(samp, 1), lax.bitwise_and(samp, 1)


def quarter(place, step):
    return lax.bitwise_and(place + step + 4, 3)


def place_in_row():
    row = lax.axis_index("row")
    return lax.bitwise_and(row, 3), lax.shift_right_logical(row, 2)


def slots_of(index_ref, column, height):
    blocks = index_ref.shape[1] // BLOCK
    wanted = [index_ref[column : column + 1, t * BLOCK : (t + 1) * BLOCK] for t in range(blocks)]
    local = jnp.concatenate(wanted, axis=0) - lax.axis_index("row") * height
    inside = (local >= 0) & (local < height)
    before = lax.broadcasted_iota(jnp.int32, (BLOCK, BLOCK), 0) < lax.broadcasted_iota(jnp.int32, (BLOCK, BLOCK), 1)
    slot = bf16_dot(jnp.where(inside, 1.0, 0.0).astype(BF16), jnp.where(before, 1.0, 0.0).astype(BF16))
    slot = jnp.where(inside, slot.astype(jnp.int32), -1)
    which = lax.broadcasted_iota(jnp.int32, (blocks, CAP, BLOCK), 1)
    wanted = jnp.where(slot[:, None, :] == which, local[:, None, :] + 1, 0)
    row = jnp.sum(wanted.astype(F32), axis=2, keepdims=True).astype(jnp.int32).reshape(blocks * CAP, 1) - 1
    return jnp.where(row == lax.broadcasted_iota(jnp.int32, (blocks * CAP, height), 1), 1.0, 0.0).astype(BF16)


def select_into(out_ref, part, onehot, rows):
    picked = pick(onehot, rows)
    out_ref[:, part * CAP : (part + 1) * CAP, :] = picked.reshape(-1, CAP, picked.shape[-1])


def first_select_kernel(index_hbm, b_hbm, c_hbm, out_ref, index_out, index_ref, b_ref, c_ref, sems):
    pairs = ((index_hbm, index_ref), (b_hbm, b_ref), (c_hbm, c_ref))
    copies = [pltpu.make_async_copy(src, dst, sems.at[n]) for n, (src, dst) in enumerate(pairs)]
    for copy in copies:
        copy.start()
    copies[0].wait()
    index_out[...] = index_ref[...]
    onehots = [slots_of(index_ref, column, b_ref.shape[0]) for column in range(2)]
    for column, rows in enumerate((b_ref, c_ref)):
        copies[column + 1].wait()
        select_into(out_ref, column, onehots[column], rows[...])


def first_select(index, b, c):
    args = [pltpu.with_memory_space_constraint(x, pltpu.HBM) for x in (index, b, c)]
    return call(
        first_select_kernel,
        (shape(index.shape[1] // BLOCK, 2 * CAP, b.shape[1]), shape(*index.shape, dtype=jnp.int32)),
        *args,
        specs=[pl.BlockSpec(memory_space=pltpu.HBM)] * 3,
        scratch_shapes=[pltpu.VMEM(x.shape, x.dtype) for x in (index, b, c)] + [pltpu.SemaphoreType.DMA((3,))],
        flops=10**9,
        size=2**21,
    )


def place_of(index, height):
    eye = lax.broadcasted_iota(jnp.int32, (BLOCK, BLOCK), 0) == lax.broadcasted_iota(jnp.int32, (BLOCK, BLOCK), 1)
    before = lax.broadcasted_iota(jnp.int32, (BLOCK, BLOCK), 1) < lax.broadcasted_iota(jnp.int32, (BLOCK, BLOCK), 0)
    owner = lax.shift_right_logical(index, height.bit_length() - 1)
    owner = jnp.broadcast_to(owner.astype(F32), (BLOCK, BLOCK))
    column = jnp.sum(jnp.where(eye, owner, 0.0), axis=1, keepdims=True)
    slot = jnp.sum(jnp.where((owner == column) & before, 1.0, 0.0), axis=1, keepdims=True)
    return column.astype(jnp.int32), slot.astype(jnp.int32)


def placed_rows(index_ref, column, got, height):
    owners, slots, rank = got.shape
    me = pl.multiple_of(lax.axis_index("row") * BLOCK, BLOCK)
    owner, slot = place_of(index_ref[column : column + 1, pl.ds(me, BLOCK)], height)
    target = owner * slots + column * CAP + slot
    onehot = target == lax.broadcasted_iota(jnp.int32, (BLOCK, owners * slots), 1)
    return pick(jnp.where(onehot, 1.0, 0.0).astype(BF16), got.reshape(owners * slots, rank))


def first_khatri_kernel(height, index_ref, got_ref, out_ref):
    got = got_ref[...]
    rows = [placed_rows(index_ref, column, got, height) for column in range(2)]
    out_ref[...] = rows[0] * rows[1]


def column_scale(got_ref, at, count):
    squares = jnp.sum(got_ref[:, at : at + 8, :], axis=0)
    return jnp.sqrt(squares[0:1, :] / count + 1e-6)


def second_khatri_kernel(height, index_ref, got_ref, out_ref, scale_ref):
    got = got_ref[...]
    scale = column_scale(got_ref, 2 * CAP, height * got_ref.shape[0])
    scale_ref[...] = jnp.broadcast_to(scale, scale_ref.shape)
    rows = placed_rows(index_ref, 0, got, height) / scale
    out_ref[...] = rows * placed_rows(index_ref, 1, got, height)


GROUP = 4


def invert_block(tiles):
    sub = lax.broadcasted_iota(jnp.int32, (8, 128), 0)
    lane = lax.broadcasted_iota(jnp.int32, (8, 128), 1)
    wide = lambda part: jnp.broadcast_to(part, (8, 128))

    def group(_, tiles):
        tiles = list(tiles)
        for j in range(GROUP):
            t = tiles[j]
            cols = [wide(t[:, 8 * j + k : 8 * j + k + 1]) for k in range(8)]
            in_panel = (lane >= 8 * j) & (lane < 8 * j + 8)
            rows = jnp.where(in_panel, jnp.where(lane == sub + 8 * j, 1.0, 0.0), t)
            for k in range(8):
                inverse = 1.0 / wide(cols[k][k : k + 1, :])
                here = sub == k
                factor = jnp.where(here, 0.0, cols[k])
                row = wide(rows[k : k + 1, :]) * inverse
                rows = jnp.where(here, row, rows - factor * row)
                for m in range(k + 1, 8):
                    entry = wide(cols[m][k : k + 1, :]) * inverse
                    cols[m] = jnp.where(here, entry, cols[m] - factor * entry)
            spread_rows = [wide(rows[k : k + 1, :]) for k in range(8)]
            for i in list(range(j + 1, len(tiles))) + list(range(j)):
                t = tiles[i]
                kept = jnp.where(in_panel, 0.0, t)
                for k in range(8):
                    kept = kept - wide(t[:, 8 * j + k : 8 * j + k + 1]) * spread_rows[k]
                tiles[i] = kept
            tiles[j] = rows
        tiles = [pltpu.roll(t, 128 - 8 * GROUP, 1) for t in tiles]
        return tuple(tiles[GROUP:] + tiles[:GROUP])

    return jnp.concatenate(lax.fori_loop(0, len(tiles) // GROUP, group, tuple(tiles)), axis=0)


def first_inverse_kernel(*refs):
    pieces, (a_ref, w_ref, rest_ref, gram_ref) = refs[:4], refs[4:]
    z, _ = position()
    rows = pieces[0].shape[0]
    for step, piece in enumerate(pieces):
        gram_ref[pl.ds(pl.multiple_of(quarter(z, -step) * rows, rows), rows), :] = piece[...]
    h = gram_ref.shape[0] // 2
    a_ref[...] = invert_block([gram_ref[8 * i : 8 * i + 8, :h] for i in range(h // 8)])
    w_ref[...] = dot(a_ref[...], gram_ref[:h, h:])
    rest_ref[...] = gram_ref[h:, h:] - dot(gram_ref[h:, :h], w_ref[...])


def second_inverse_kernel(a_ref, w_ref, rest_ref, out_ref):
    h = a_ref.shape[0]
    s = invert_block([rest_ref[8 * i : 8 * i + 8, :] for i in range(h // 8)])
    ws = dot(w_ref[...], s)
    out_ref[h:, h:] = s
    out_ref[:h, h:] = -ws
    out_ref[h:, :h] = -ws.T
    out_ref[:h, :h] = a_ref[...] + dot(ws, w_ref[...], (1, 1))


def join_kernel(place, a, b, c, d, out_ref):
    for step, piece in enumerate((a, b, c, d)):
        at = pl.multiple_of(quarter(place(), -step) * BLOCK, BLOCK)
        out_ref[pl.ds(at, BLOCK), :] = piece[...]


def joined(pieces, place):
    rows, rank = pieces[0].shape
    return call(lambda *refs: join_kernel(place, *refs), shape(4 * rows, rank), *pieces, size=2**20)


DIAGONALS = (0, -1, 1, 2)


def split_kernel(fibres_ref, *refs):
    outs, (held, sems) = refs[:8], refs[8:]
    x, y = place_in_row()
    _, _, rows, _ = held.shape
    copies = []
    for n, beside in enumerate(DIAGONALS):
        for half in range(2):
            copies.append([])
            for place in range(4):
                at = pl.multiple_of((4 * place + quarter(x - y + 4, place + beside)) * BLOCK, BLOCK)
                source = fibres_ref.at[half * rows : (half + 1) * rows, pl.ds(at, BLOCK)]
                target = held.at[n, half, :, place * BLOCK : (place + 1) * BLOCK]
                copies[-1].append(pltpu.make_async_copy(source, target, sems.at[n, half, place]))
                copies[-1][-1].start()
    for n in range(4):
        for half in range(2):
            for copy in copies[2 * n + half]:
                copy.wait()
            mine = slice(half * rows, (half + 1) * rows)
            outs[2 * n][mine, :], outs[2 * n + 1][mine, :] = halves(held[n, half])


def split(fibres):
    rows, samples = fibres.shape
    depth = samples // 4
    return call(
        split_kernel,
        (shape(rows, depth, dtype=BF16),) * 8,
        pltpu.with_memory_space_constraint(fibres, pltpu.HBM),
        specs=[pl.BlockSpec(memory_space=pltpu.HBM)],
        scratch_shapes=[pltpu.VMEM((4, 2, rows // 2, depth), F32), pltpu.SemaphoreType.DMA((4, 2, 4))],
        flops=4 * fibres.size,
        size=8 * fibres.size,
    )


def three_dots(high, low, khatri_high, khatri_low):
    return bf16_dot(high, khatri_high) + (bf16_dot(high, khatri_low) + bf16_dot(low, khatri_high))


def gram_of(high, low):
    t = lambda a, b: lax.dot_general(a, b, (((0,), (0,)), ((), ())), preferred_element_type=F32)
    cross = t(high, low)
    return t(high, high) + (cross + cross.T)


def piece_kernel(high_ref, low_ref, khatri_ref, *refs):
    so_far, (total_ref, gram_ref) = refs[:-2], refs[-2:]
    khatri = halves(khatri_ref[...])
    total, gram = three_dots(high_ref[...], low_ref[...], *khatri), gram_of(*khatri)
    total_ref[...] = total + so_far[0][...] if so_far else total
    gram_ref[...] = gram + so_far[1][...] if so_far else gram


def half_of(high_ref, low_ref, khatri, total_ref, core, out_ref):
    rows = high_ref.shape[0] // 2
    mine = pl.ds(pl.multiple_of(core * rows, rows), rows)
    total = three_dots(high_ref[mine, :], low_ref[mine, :], *khatri) + total_ref[mine, :]
    for place in range(4):
        out_ref[place, :BLOCK, :] = total[place * BLOCK : (place + 1) * BLOCK]


def given_kernel(high_ref, low_ref, khatri_ref, total_ref, gram_ref, out_ref):
    _, core = position()
    khatri = halves(khatri_ref[...])
    half_of(high_ref, low_ref, khatri, total_ref, 1 - core, out_ref)
    gram = gram_of(*khatri) + gram_ref[...]
    rows = gram.shape[0] // 4
    for place in range(4):
        out_ref[place, BLOCK:, :] = gram[place * rows : (place + 1) * rows]


def kept_kernel(high_ref, low_ref, khatri_ref, total_ref, given_ref, out_ref):
    _, core = position()
    half_of(high_ref, low_ref, halves(khatri_ref[...]), total_ref, core, out_ref)
    out_ref[:, BLOCK:, :] = given_ref[:, BLOCK:, :]


def pair_kernel(kept_ref, given_ref, *outs):
    z, _ = position()
    for step, out_ref in enumerate(outs):
        place = quarter(z, step)
        out_ref[...] = kept_ref[place] + given_ref[place]


def quarter_kernel(a, b, c, d, product_ref, gram_ref):
    total = (a[...] + b[...]) + (c[...] + d[...])
    product_ref[...] = total[:BLOCK]
    gram_ref[...] = total[BLOCK:]


def from_z(own):
    got = {step: lax.ppermute(own, "samp", along_z(step)) for step in FAR_FIRST}
    return [own, got[1], got[2], got[3]]


def sums_over_row_group(fibres, block, aside):
    rank = block.shape[1]
    rows, samples = fibres.shape
    depth = samples // 4
    flops = 6 * rows * depth * rank
    near = {step: lax.ppermute(block, "row", in_plane(step, step)) for step in FAR_FIRST}
    piece = joined([block, near[1], near[2], near[3]], lambda: place_in_row()[1])
    fibres, piece = lax.optimization_barrier((fibres, piece))
    parts = split(fibres)
    moves = {-1: (0, 1), 1: (0, -1), 2: (2, 0)}
    pieces = {beside: lax.ppermute(piece, "row", in_plane(*move)) for beside, move in moves.items()}
    pieces[0] = piece
    state = ()
    for n, beside in enumerate(DIAGONALS[:3]):
        high, low = parts[2 * n : 2 * n + 2]
        out = (shape(rows, rank), shape(rank, rank))
        state = call(piece_kernel, out, high, low, pieces[beside], *state, flops=flops, size=2**22)
        if n == 0:
            state, extra = lax.optimization_barrier((state, aside(piece)))
    total, gram = state
    high, low = parts[6:]
    out = shape(4, BLOCK + rank // 4, rank)
    given = call(given_kernel, out, high, low, pieces[2], total, gram, flops=flops, size=2**21)
    got = lax.ppermute(given, "samp", CORE)
    kept = call(kept_kernel, out, high, low, pieces[2], total, given, flops=flops // 2, size=2**21)
    return kept, got, extra


def summed(fibres, block, aside):
    rank = block.shape[1]
    kept, got, extra = sums_over_row_group(fibres, block, aside)
    rows = kept.shape[1]
    pairs = call(pair_kernel, (shape(rows, rank),) * 4, kept, got, size=2**21)
    parts = [pairs[0]] + [lax.ppermute(pairs[step], "samp", along_z(step)) for step in FAR_FIRST]
    product, gram = call(quarter_kernel, (shape(BLOCK, rank), shape(rank // 4, rank)), *parts, size=2**20)
    h = rank // 2
    first = call(
        first_inverse_kernel,
        (shape(h, h),) * 3,
        *from_z(gram),
        scratch_shapes=[pltpu.VMEM((rank, rank), F32)],
        flops=10**11,
        size=2**19,
    )
    first, pieces = lax.optimization_barrier((first, from_z(product)))
    mine = joined(pieces, lambda: position()[0])
    other = lax.ppermute(mine, "samp", CORE)
    inverse = call(second_inverse_kernel, shape(rank, rank), *first, flops=10**11, size=2**19)
    return mine, other, inverse, extra


def solve_into(out_ref, mine_ref, other_ref, inverse_ref):
    _, core = position()
    inverse = halves(inverse_ref[...])
    rows = mine_ref.shape[0]
    for owner, ref in ((core, mine_ref), (1 - core, other_ref)):
        out_ref[pl.ds(pl.multiple_of(owner * rows, rows), rows), :] = three_dots(*halves(ref[...]), *inverse)


def select_kernel(index_ref, c_ref, out_ref):
    select_into(out_ref, 0, slots_of(index_ref, 1, c_ref.shape[0]), c_ref[...])


def first_solve_kernel(mine_ref, other_ref, inverse_ref, index_ref, chosen_ref, solved_ref, out_ref):
    solve_into(solved_ref, mine_ref, other_ref, inverse_ref)
    solved = solved_ref[...]
    peers, _, rank = out_ref.shape
    squares = jnp.sum(solved * solved, axis=0, keepdims=True)
    out_ref[:, 2 * CAP :, :] = jnp.broadcast_to(squares[None], (peers, 8, rank))
    out_ref[:, CAP : 2 * CAP, :] = chosen_ref[...]
    select_into(out_ref, 0, slots_of(index_ref, 0, solved.shape[0]), solved)


def second_solve_kernel(mine_ref, other_ref, inverse_ref, solved_ref, out_ref):
    solve_into(solved_ref, mine_ref, other_ref, inverse_ref)
    solved = solved_ref[...]
    out_ref[...] = jnp.broadcast_to(jnp.sum(solved * solved, axis=0, keepdims=True)[None], out_ref.shape)


def finish_kernel(solved_ref, got_ref, out_ref, scale_ref):
    scale = column_scale(got_ref, 0, solved_ref.shape[0] * got_ref.shape[0])
    scale_ref[...] = jnp.broadcast_to(scale, scale_ref.shape)
    out_ref[...] = solved_ref[...] / scale


def exchange(rows):
    return lax.all_to_all(rows, "row", 0, 0, tiled=True)


def shards(fibres_first, fibres_second, index_first, index_second, factor_b, factor_c):
    height, rank = factor_b.shape
    peers = index_first.shape[0] // BLOCK
    first, second = index_first.T, index_second.T

    sent, first = first_select(first, factor_b, factor_c)
    got = exchange(sent)
    block = call(lambda *refs: first_khatri_kernel(height, *refs), shape(BLOCK, rank), first, got, flops=10**8, size=2**22)

    def choose(piece):
        index, rows, _ = lax.optimization_barrier((second, factor_c, piece))
        return call(select_kernel, shape(peers, CAP, rank), index, rows, flops=10**9, size=2**21)

    mine, other, inverse, chosen = summed(fibres_first, block, choose)
    solved, sent = call(
        first_solve_kernel,
        (shape(height, rank), shape(peers, 2 * CAP + 8, rank)),
        mine,
        other,
        inverse,
        second,
        chosen,
        flops=10**9,
        size=2**21,
    )
    block, scale = call(
        lambda *refs: second_khatri_kernel(height, *refs),
        (shape(BLOCK, rank), shape(8, rank)),
        second,
        exchange(sent),
        flops=10**8,
        size=2**22,
    )

    def normalise(piece):
        rows, _ = lax.optimization_barrier((solved, piece))
        return rows / scale[:1]

    mine, other, inverse, factor_a = summed(fibres_second, block, normalise)
    solved, sent = call(
        second_solve_kernel,
        (shape(height, rank), shape(peers, 8, rank)),
        mine,
        other,
        inverse,
        flops=10**9,
        size=2**21,
    )
    factor_b_new, weights = call(finish_kernel, (shape(height, rank), shape(8, rank)), solved, exchange(sent), size=2**21)
    return (factor_a, factor_b_new, weights[0])


def solution(mesh):
    placed = (P("row", "samp"), P("row", "samp"), P("samp", None), P("samp", None), P("row", None), P("row", None))
    return jax.shard_map(
        shards,
        mesh=mesh,
        in_specs=placed,
        out_specs=(P("row", None), P("row", None), P()),
        check_vma=False,
    )
```

profile of v0, /device:TPU:0, one launch (start us, length us, event | category | flops | bytes accessed | tf_op | source)
XLA Modules:
  0.0 184.4 jit_solution(6454274457252129659)
XLA Ops:
  0.7 2.7 %shard_map.85 = (f32[16,32,256]{2,1,0:T(8,128)S(1)}, s32[2,2048]{1,0:T(2,128)S(1)}) custom-call(s32[2,2048]{1,0:T(2,128)} %bitcast.9, f32[1024,256]{1,0:T(8,128)} %b_hbm.1, f32[1024,256]{1,0:T(8,128)} %c_ref), custom_call_target="tpu_custom_call" | custom-call | flops 1000000000 | bytes 2097152 | tf_op jit(solution)/shard_map/pallas_call | solution.py:26
  3.4 18.5 %all_to_all.15.refs_1_ = f32[16,32,256]{2,1,0:T(8,128)S(1)} all-to-all(f32[16,32,256]{2,1,0:T(8,128)S(1)} %get-tuple-element.87), channel_id=1, replica_groups=mesh['row'=16,'samp'=8] {'row'}, dimensions={0} | all-to-all | bytes 1048576 | tf_op jit(solution)/shard_map/all_to_all | solution.py:412
  22.4 3.5 %collective-permute-start.1 = (f32[128,256]{1,0:T(8,128)S(1)}, f32[128,256]{1,0:T(8,128)S(1)}, u32[]{:S(2)}, u32[]{:S(2)}) collective-permute-start(f32[128,256]{1,0:T(8,128)S(1)} %shard_map.86.refs_0_), channel_id=1, source_target_pairs={{0,80},{8,88},{16,64},{24,72},{32,112},{40,120},{48,96},{56,104},{... | collective-permute-start | bytes 393224 | tf_op jit(solution)/shard_map/ppermute | solution.py:331
  25.9 2.4 %collective-permute-start.2 = (f32[128,256]{1,0:T(8,128)S(1)}, f32[128,256]{1,0:T(8,128)S(1)}, u32[]{:S(2)}, u32[]{:S(2)}) collective-permute-start(f32[128,256]{1,0:T(8,128)S(1)} %shard_map.86.refs_0_), channel_id=1, source_target_pairs={{0,120},{8,96},{16,104},{24,112},{32,24},{40,0},{48,8},{56,16},{64... | collective-permute-start | bytes 393224 | tf_op jit(solution)/shard_map/ppermute | solution.py:331
  28.3 4.8 %collective-permute-done.refs_1_ = f32[128,256]{1,0:T(8,128)S(1)} collective-permute-done((f32[128,256]{1,0:T(8,128)S(1)}, f32[128,256]{1,0:T(8,128)S(1)}, u32[]{:S(2)}, u32[]{:S(2)}) %collective-permute-start) | collective-permute-done | bytes 131104 | tf_op jit(solution)/shard_map/ppermute | solution.py:331
  33.8 3.0 %collective-permute-start.4 = (f32[512,256]{1,0:T(8,128)S(1)}, f32[512,256]{1,0:T(8,128)S(1)}, u32[]{:S(2)}, u32[]{:S(2)}) collective-permute-start(f32[512,256]{1,0:T(8,128)S(1)} %shard_map.87.khatri_ref), channel_id=1, source_target_pairs={{0,24},{8,0},{16,8},{24,16},{32,56},{40,32},{48,40},{56,48},{64,88... | collective-permute-start | bytes 1572872 | tf_op jit(solution)/shard_map/ppermute | solution.py:336
  36.8 1.3 collective-permute-start.3
  38.1 3.9 %shard_map.88 = (bf16[1024,512]{1,0:T(8,128)(2,1)S(1)}, bf16[1024,512]{1,0:T(8,128)(2,1)S(1)}, bf16[1024,512]{1,0:T(8,128)(2,1)S(1)}, bf16[1024,512]{1,0:T(8,128...) custom-call(f32[1024,2048]{1,0:T(8,128)} %fibres_ref), custom_call_target="tpu_custom_call" | custom-call | flops 8388608 | bytes 16777216 | tf_op jit(solution)/shard_map/pallas_call | solution.py:26
  42.0 1.1 shard_map.89
  43.8 2.1 %collective-permute-done.5.khatri_ref = f32[512,256]{1,0:T(8,128)S(1)} collective-permute-done((f32[512,256]{1,0:T(8,128)S(1)}, f32[512,256]{1,0:T(8,128)S(1)}, u32[]{:S(2)}, u32[]{:S(2)}) %collective-permute-start.5) | collective-permute-done | bytes 524320 | tf_op jit(solution)/shard_map/ppermute | solution.py:336
  45.9 1.1 shard_map.91
  47.1 1.1 shard_map.92
  50.3 1.7 collective-permute-done.6.given_ref
  52.1 3.9 %collective-permute-start.7 = (f32[192,256]{1,0:T(8,128)S(1)}, f32[192,256]{1,0:T(8,128)S(1)}, u32[]{:S(2)}, u32[]{:S(2)}) collective-permute-start(f32[192,256]{1,0:T(8,128)S(1)} %get-tuple-element.109), channel_id=1, source_target_pairs={{0,4},{1,5},{2,6},{3,7},{4,0},{5,1},{6,2},{7,3},{8,12},{9,13},{10,... | collective-permute-start | bytes 589832 | tf_op jit(solution)/shard_map/ppermute | solution.py:359
  57.0 2.2 %collective-permute-start.9 = (f32[192,256]{1,0:T(8,128)S(1)}, f32[192,256]{1,0:T(8,128)S(1)}, u32[]{:S(2)}, u32[]{:S(2)}) collective-permute-start(f32[192,256]{1,0:T(8,128)S(1)} %get-tuple-element.111), channel_id=1, source_target_pairs={{0,6},{1,7},{2,0},{3,1},{4,2},{5,3},{6,4},{7,5},{8,14},{9,15},{10,... | collective-permute-start | bytes 589832 | tf_op jit(solution)/shard_map/ppermute | solution.py:359
  59.2 2.4 %collective-permute-done.7.b = f32[192,256]{1,0:T(8,128)S(1)} collective-permute-done((f32[192,256]{1,0:T(8,128)S(1)}, f32[192,256]{1,0:T(8,128)S(1)}, u32[]{:S(2)}, u32[]{:S(2)}) %collective-permute-start.7) | collective-permute-done | bytes 196640 | tf_op jit(solution)/shard_map/ppermute | solution.py:359
  61.7 3.7 %collective-permute-done.8.c = f32[192,256]{1,0:T(8,128)S(1)} collective-permute-done((f32[192,256]{1,0:T(8,128)S(1)}, f32[192,256]{1,0:T(8,128)S(1)}, u32[]{:S(2)}, u32[]{:S(2)}) %collective-permute-start.8) | collective-permute-done | bytes 196640 | tf_op jit(solution)/shard_map/ppermute | solution.py:359
  66.2 1.1 collective-permute-start.10
  67.3 3.1 %collective-permute-start.11 = (f32[64,256]{1,0:T(8,128)S(1)}, f32[64,256]{1,0:T(8,128)S(1)}, u32[]{:S(2)}, u32[]{:S(2)}) collective-permute-start(f32[64,256]{1,0:T(8,128)S(1)} %get-tuple-element.112.refs_0_), channel_id=1, source_target_pairs={{0,4},{1,5},{2,6},{3,7},{4,0},{5,1},{6,2},{7,3},{8,12},{9,13},{10,... | collective-permute-start | bytes 196616 | tf_op jit(solution)/shard_map/ppermute | solution.py:322
  71.0 1.5 collective-permute-start.13
  72.9 2.2 %collective-permute-start.15 = (f32[128,256]{1,0:T(8,128)S(1)}, f32[128,256]{1,0:T(8,128)S(1)}, u32[]{:S(2)}, u32[]{:S(2)}) collective-permute-start(f32[128,256]{1,0:T(8,128)S(1)} %get-tuple-element.117.refs_0_), channel_id=1, source_target_pairs={{0,6},{1,7},{2,0},{3,1},{4,2},{5,3},{6,4},{7,5},{8,14},{9,15},{10,... | collective-permute-start | bytes 393224 | tf_op jit(solution)/shard_map/ppermute | solution.py:322
  75.1 5.0 %shard_map.97 = (f32[128,128]{1,0:T(8,128)S(1)}, f32[128,128]{1,0:T(8,128)S(1)}, f32[128,128]{1,0:T(8,128)S(1)}) custom-call(f32[64,256]{1,0:T(8,128)S(1)} %get-tuple-element.112.refs_0_, f32[64,256]{1,0:T(8,128)S(1)} %collective-permute-done.10.refs_1_, f32[64,256]{1,0:T(8,128)S(1)} %collective-permute-done.11.refs_2_, ...), custom_call_target="tpu_custom_call" | custom-call | flops 99999997952 | bytes 524288 | tf_op jit(solution)/shard_map/pallas_call | solution.py:26
  80.4 5.0 %shard_map.99.inverse_ref = f32[256,256]{1,0:T(8,128)S(1)} custom-call(f32[128,128]{1,0:T(8,128)S(1)} %get-tuple-element.121.a_ref, f32[128,128]{1,0:T(8,128)S(1)} %get-tuple-element.122.w_ref, f32[128,128]{1,0:T(8,128)S(1)} %get-tuple-element.123.rest_ref), custom_call_target="tpu_custom_call" | custom-call | flops 99999997952 | bytes 524288 | tf_op jit(solution)/shard_map/pallas_call | solution.py:26
  85.4 1.8 %shard_map.100 = (f32[1024,256]{1,0:T(8,128)S(1)}, f32[16,40,256]{2,1,0:T(8,128)S(1)}) custom-call(f32[512,256]{1,0:T(8,128)S(1)} %shard_map.98.mine_ref, f32[512,256]{1,0:T(8,128)S(1)} %collective-permute-done.16.other_ref, f32[256,256]{1,0:T(8,128)S(1)} %shard_map.99.inverse_ref, s32[2,2048]{1,0:T(2,128)S(1)} %bitcast.5, ...), custom_call_target="tpu_custom_call" | custom-call | flops 1000000000 | bytes 2097152 | tf_op jit(solution)/shard_map/pallas_call | solution.py:26
  87.3 18.4 %all_to_all.16.refs_1_ = f32[16,40,256]{2,1,0:T(8,128)S(1)} all-to-all(f32[16,40,256]{2,1,0:T(8,128)S(1)} %get-tuple-element.125), channel_id=1, replica_groups=mesh['row'=16,'samp'=8] {'row'}, dimensions={0} | all-to-all | bytes 1310720 | tf_op jit(solution)/shard_map/all_to_all | solution.py:412
  106.6 3.7 %collective-permute-start.18 = (f32[128,256]{1,0:T(8,128)S(1)}, f32[128,256]{1,0:T(8,128)S(1)}, u32[]{:S(2)}, u32[]{:S(2)}) collective-permute-start(f32[128,256]{1,0:T(8,128)S(1)} %get-tuple-element.126.refs_0_), channel_id=1, source_target_pairs={{0,80},{8,88},{16,64},{24,72},{32,112},{40,120},{48,96},{56,104},{... | collective-permute-start | bytes 393224 | tf_op jit(solution)/shard_map/ppermute | solution.py:331
  110.2 2.1 %collective-permute-start.19 = (f32[128,256]{1,0:T(8,128)S(1)}, f32[128,256]{1,0:T(8,128)S(1)}, u32[]{:S(2)}, u32[]{:S(2)}) collective-permute-start(f32[128,256]{1,0:T(8,128)S(1)} %get-tuple-element.126.refs_0_), channel_id=1, source_target_pairs={{0,120},{8,96},{16,104},{24,112},{32,24},{40,0},{48,8},{56,16},{64... | collective-permute-start | bytes 393224 | tf_op jit(solution)/shard_map/ppermute | solution.py:331
  112.4 5.3 %collective-permute-done.17.refs_1_ = f32[128,256]{1,0:T(8,128)S(1)} collective-permute-done((f32[128,256]{1,0:T(8,128)S(1)}, f32[128,256]{1,0:T(8,128)S(1)}, u32[]{:S(2)}, u32[]{:S(2)}) %collective-permute-start.17) | collective-permute-done | bytes 131104 | tf_op jit(solution)/shard_map/ppermute | solution.py:331
  118.9 2.7 %collective-permute-start.21 = (f32[512,256]{1,0:T(8,128)S(1)}, f32[512,256]{1,0:T(8,128)S(1)}, u32[]{:S(2)}, u32[]{:S(2)}) collective-permute-start(f32[512,256]{1,0:T(8,128)S(1)} %shard_map.102.khatri_ref), channel_id=1, source_target_pairs={{0,24},{8,0},{16,8},{24,16},{32,56},{40,32},{48,40},{56,48},{64,88... | collective-permute-start | bytes 1572872 | tf_op jit(solution)/shard_map/ppermute | solution.py:336
  121.6 1.3 collective-permute-start.20
  122.9 3.9 %shard_map.103 = (bf16[1024,512]{1,0:T(8,128)(2,1)S(1)}, bf16[1024,512]{1,0:T(8,128)(2,1)S(1)}, bf16[1024,512]{1,0:T(8,128)(2,1)S(1)}, bf16[1024,512]{1,0:T(8,12...) custom-call(f32[1024,2048]{1,0:T(8,128)} %fibres_ref.1), custom_call_target="tpu_custom_call" | custom-call | flops 8388608 | bytes 16777216 | tf_op jit(solution)/shard_map/pallas_call | solution.py:26
  126.8 1.1 shard_map.104
  129.0 3.6 %collective-permute-done.22.khatri_ref = f32[512,256]{1,0:T(8,128)S(1)} collective-permute-done((f32[512,256]{1,0:T(8,128)S(1)}, f32[512,256]{1,0:T(8,128)S(1)}, u32[]{:S(2)}, u32[]{:S(2)}) %collective-permute-start.22) | collective-permute-done | bytes 524320 | tf_op jit(solution)/shard_map/ppermute | solution.py:336
  132.5 1.1 shard_map.105
  133.7 1.1 shard_map.106
  137.0 1.7 collective-permute-done.23.given_ref
  138.7 1.9 %collective-permute-start.24 = (f32[192,256]{1,0:T(8,128)S(1)}, f32[192,256]{1,0:T(8,128)S(1)}, u32[]{:S(2)}, u32[]{:S(2)}) collective-permute-start(f32[192,256]{1,0:T(8,128)S(1)} %get-tuple-element.150), channel_id=1, source_target_pairs={{0,4},{1,5},{2,6},{3,7},{4,0},{5,1},{6,2},{7,3},{8,12},{9,13},{10,... | collective-permute-start | bytes 589832 | tf_op jit(solution)/shard_map/ppermute | solution.py:359
  140.7 1.7 collective-permute-start.25
  142.3 1.6 collective-permute-start.26
  143.9 4.2 %collective-permute-done.24.b = f32[192,256]{1,0:T(8,128)S(1)} collective-permute-done((f32[192,256]{1,0:T(8,128)S(1)}, f32[192,256]{1,0:T(8,128)S(1)}, u32[]{:S(2)}, u32[]{:S(2)}) %collective-permute-start.24) | collective-permute-done | bytes 196640 | tf_op jit(solution)/shard_map/ppermute | solution.py:359
  148.1 3.4 %collective-permute-done.25.c = f32[192,256]{1,0:T(8,128)S(1)} collective-permute-done((f32[192,256]{1,0:T(8,128)S(1)}, f32[192,256]{1,0:T(8,128)S(1)}, u32[]{:S(2)}, u32[]{:S(2)}) %collective-permute-start.25) | collective-permute-done | bytes 196640 | tf_op jit(solution)/shard_map/ppermute | solution.py:359
  151.5 1.1 collective-permute-start.27
  152.6 3.1 %collective-permute-start.28 = (f32[64,256]{1,0:T(8,128)S(1)}, f32[64,256]{1,0:T(8,128)S(1)}, u32[]{:S(2)}, u32[]{:S(2)}) collective-permute-start(f32[64,256]{1,0:T(8,128)S(1)} %get-tuple-element.153.refs_0_), channel_id=1, source_target_pairs={{0,4},{1,5},{2,6},{3,7},{4,0},{5,1},{6,2},{7,3},{8,12},{9,13},{10,... | collective-permute-start | bytes 196616 | tf_op jit(solution)/shard_map/ppermute | solution.py:322
  156.1 1.6 collective-permute-start.30
  158.2 2.2 %collective-permute-start.32 = (f32[128,256]{1,0:T(8,128)S(1)}, f32[128,256]{1,0:T(8,128)S(1)}, u32[]{:S(2)}, u32[]{:S(2)}) collective-permute-start(f32[128,256]{1,0:T(8,128)S(1)} %get-tuple-element.158.refs_0_), channel_id=1, source_target_pairs={{0,6},{1,7},{2,0},{3,1},{4,2},{5,3},{6,4},{7,5},{8,14},{9,15},{10,... | collective-permute-start | bytes 393224 | tf_op jit(solution)/shard_map/ppermute | solution.py:322
  160.4 5.0 %shard_map.111 = (f32[128,128]{1,0:T(8,128)S(1)}, f32[128,128]{1,0:T(8,128)S(1)}, f32[128,128]{1,0:T(8,128)S(1)}) custom-call(f32[64,256]{1,0:T(8,128)S(1)} %get-tuple-element.153.refs_0_, f32[64,256]{1,0:T(8,128)S(1)} %collective-permute-done.27.refs_1_, f32[64,256]{1,0:T(8,128)S(1)} %collective-permute-done.28.refs_2_, ...), custom_call_target="tpu_custom_call" | custom-call | flops 99999997952 | bytes 524288 | tf_op jit(solution)/shard_map/pallas_call | solution.py:26
  165.7 5.0 %shard_map.113.inverse_ref = f32[256,256]{1,0:T(8,128)S(1)} custom-call(f32[128,128]{1,0:T(8,128)S(1)} %get-tuple-element.162.a_ref, f32[128,128]{1,0:T(8,128)S(1)} %get-tuple-element.163.w_ref, f32[128,128]{1,0:T(8,128)S(1)} %get-tuple-element.164.rest_ref), custom_call_target="tpu_custom_call" | custom-call | flops 99999997952 | bytes 524288 | tf_op jit(solution)/shard_map/pallas_call | solution.py:26
  171.5 11.3 %all_to_all.17.got_ref = f32[16,8,256]{2,1,0:T(8,128)S(1)} all-to-all(f32[16,8,256]{2,1,0:T(8,128)S(1)} %get-tuple-element.166), channel_id=1, replica_groups=mesh['row'=16,'samp'=8] {'row'}, dimensions={0} | all-to-all | bytes 262144 | tf_op jit(solution)/shard_map/all_to_all | solution.py:412
  (63 shorter events, 16.2 us)
Async XLA Ops:
  0.6 42.5 %copy-start = (s32[2048,2]{0,1:T(2,128)S(1)}, s32[2048,2]{0,1:T(2,128)}, u32[]{:S(2)}) copy-start(s32[2048,2]{0,1:T(2,128)} %param.9) | copy-start | bytes 49156
  0.6 42.5 %copy-start.2 = (f32[1024,256]{1,0:T(8,128)S(1)}, f32[1024,256]{1,0:T(8,128)}, u32[]{:S(2)}) copy-start(f32[1024,256]{1,0:T(8,128)} %c_ref) | copy-start | bytes 3145732
  22.3 10.8 %collective-permute-start = (f32[128,256]{1,0:T(8,128)S(1)}, f32[128,256]{1,0:T(8,128)S(1)}, u32[]{:S(2)}, u32[]{:S(2)}) collective-permute-start(f32[128,256]{1,0:T(8,128)S(1)} %shard_map.86.refs_0_), channel_id=1, source_target_pairs={{0,40},{8,48},{16,56},{24,32},{32,72},{40,80},{48,88},{56,64},{64,... | collective-permute-start | bytes 393224 | tf_op jit(solution)/shard_map/ppermute | solution.py:331
  22.4 10.7 %collective-permute-start.1 = (f32[128,256]{1,0:T(8,128)S(1)}, f32[128,256]{1,0:T(8,128)S(1)}, u32[]{:S(2)}, u32[]{:S(2)}) collective-permute-start(f32[128,256]{1,0:T(8,128)S(1)} %shard_map.86.refs_0_), channel_id=1, source_target_pairs={{0,80},{8,88},{16,64},{24,72},{32,112},{40,120},{48,96},{56,104},{... | collective-permute-start | bytes 393224 | tf_op jit(solution)/shard_map/ppermute | solution.py:331
  25.9 7.5 %collective-permute-start.2 = (f32[128,256]{1,0:T(8,128)S(1)}, f32[128,256]{1,0:T(8,128)S(1)}, u32[]{:S(2)}, u32[]{:S(2)}) collective-permute-start(f32[128,256]{1,0:T(8,128)S(1)} %shard_map.86.refs_0_), channel_id=1, source_target_pairs={{0,120},{8,96},{16,104},{24,112},{32,24},{40,0},{48,8},{56,16},{64... | collective-permute-start | bytes 393224 | tf_op jit(solution)/shard_map/ppermute | solution.py:331
  33.5 12.4 %collective-permute-start.5 = (f32[512,256]{1,0:T(8,128)S(1)}, f32[512,256]{1,0:T(8,128)S(1)}, u32[]{:S(2)}, u32[]{:S(2)}) collective-permute-start(f32[512,256]{1,0:T(8,128)S(1)} %shard_map.87.khatri_ref), channel_id=1, source_target_pairs={{0,8},{8,16},{16,24},{24,0},{32,40},{40,48},{48,56},{56,32},{64,72... | collective-permute-start | bytes 1572872 | tf_op jit(solution)/shard_map/ppermute | solution.py:336
  33.8 13.3 %collective-permute-start.4 = (f32[512,256]{1,0:T(8,128)S(1)}, f32[512,256]{1,0:T(8,128)S(1)}, u32[]{:S(2)}, u32[]{:S(2)}) collective-permute-start(f32[512,256]{1,0:T(8,128)S(1)} %shard_map.87.khatri_ref), channel_id=1, source_target_pairs={{0,24},{8,0},{16,8},{24,16},{32,56},{40,32},{48,40},{56,48},{64,88... | collective-permute-start | bytes 1572872 | tf_op jit(solution)/shard_map/ppermute | solution.py:336
  36.8 12.1 %collective-permute-start.3 = (f32[512,256]{1,0:T(8,128)S(1)}, f32[512,256]{1,0:T(8,128)S(1)}, u32[]{:S(2)}, u32[]{:S(2)}) collective-permute-start(f32[512,256]{1,0:T(8,128)S(1)} %shard_map.87.khatri_ref), channel_id=1, source_target_pairs={{0,64},{8,72},{16,80},{24,88},{32,96},{40,104},{48,112},{56,120},{... | collective-permute-start | bytes 1572872 | tf_op jit(solution)/shard_map/ppermute | solution.py:336
  49.6 2.4 %collective-permute-start.6 = (f32[4,192,256]{2,1,0:T(8,128)S(1)}, f32[4,192,256]{2,1,0:T(8,128)S(1)}, u32[]{:S(2)}, u32[]{:S(2)}) collective-permute-start(f32[4,192,256]{2,1,0:T(8,128)S(1)} %shard_map.93.given_ref), channel_id=1, source_target_pairs={{0,1},{1,0},{2,3},{3,2},{4,5},{5,4},{6,7},{7,6},{8,9},{9,8},{10,11... | collective-permute-start | bytes 2359304 | tf_op jit(solution)/shard_map/ppermute | solution.py:349
  52.1 9.6 %collective-permute-start.7 = (f32[192,256]{1,0:T(8,128)S(1)}, f32[192,256]{1,0:T(8,128)S(1)}, u32[]{:S(2)}, u32[]{:S(2)}) collective-permute-start(f32[192,256]{1,0:T(8,128)S(1)} %get-tuple-element.109), channel_id=1, source_target_pairs={{0,4},{1,5},{2,6},{3,7},{4,0},{5,1},{6,2},{7,3},{8,12},{9,13},{10,... | collective-permute-start | bytes 589832 | tf_op jit(solution)/shard_map/ppermute | solution.py:359
  56.0 9.4 %collective-permute-start.8 = (f32[192,256]{1,0:T(8,128)S(1)}, f32[192,256]{1,0:T(8,128)S(1)}, u32[]{:S(2)}, u32[]{:S(2)}) collective-permute-start(f32[192,256]{1,0:T(8,128)S(1)} %get-tuple-element.110), channel_id=1, source_target_pairs={{0,2},{1,3},{2,4},{3,5},{4,6},{5,7},{6,0},{7,1},{8,10},{9,11},{10,... | collective-permute-start | bytes 589832 | tf_op jit(solution)/shard_map/ppermute | solution.py:359
  57.0 9.1 %collective-permute-start.9 = (f32[192,256]{1,0:T(8,128)S(1)}, f32[192,256]{1,0:T(8,128)S(1)}, u32[]{:S(2)}, u32[]{:S(2)}) collective-permute-start(f32[192,256]{1,0:T(8,128)S(1)} %get-tuple-element.111), channel_id=1, source_target_pairs={{0,6},{1,7},{2,0},{3,1},{4,2},{5,3},{6,4},{7,5},{8,14},{9,15},{10,... | collective-permute-start | bytes 589832 | tf_op jit(solution)/shard_map/ppermute | solution.py:359
  66.2 6.7 %collective-permute-start.10 = (f32[64,256]{1,0:T(8,128)S(1)}, f32[64,256]{1,0:T(8,128)S(1)}, u32[]{:S(2)}, u32[]{:S(2)}) collective-permute-start(f32[64,256]{1,0:T(8,128)S(1)} %get-tuple-element.112.refs_0_), channel_id=1, source_target_pairs={{0,2},{1,3},{2,4},{3,5},{4,6},{5,7},{6,0},{7,1},{8,10},{9,11},{10,... | collective-permute-start | bytes 196616 | tf_op jit(solution)/shard_map/ppermute | solution.py:322
  67.3 7.8 %collective-permute-start.11 = (f32[64,256]{1,0:T(8,128)S(1)}, f32[64,256]{1,0:T(8,128)S(1)}, u32[]{:S(2)}, u32[]{:S(2)}) collective-permute-start(f32[64,256]{1,0:T(8,128)S(1)} %get-tuple-element.112.refs_0_), channel_id=1, source_target_pairs={{0,4},{1,5},{2,6},{3,7},{4,0},{5,1},{6,2},{7,3},{8,12},{9,13},{10,... | collective-permute-start | bytes 196616 | tf_op jit(solution)/shard_map/ppermute | solution.py:322
  70.4 4.7 %collective-permute-start.12 = (f32[64,256]{1,0:T(8,128)S(1)}, f32[64,256]{1,0:T(8,128)S(1)}, u32[]{:S(2)}, u32[]{:S(2)}) collective-permute-start(f32[64,256]{1,0:T(8,128)S(1)} %get-tuple-element.112.refs_0_), channel_id=1, source_target_pairs={{0,6},{1,7},{2,0},{3,1},{4,2},{5,3},{6,4},{7,5},{8,14},{9,15},{10,... | collective-permute-start | bytes 196616 | tf_op jit(solution)/shard_map/ppermute | solution.py:322
  71.0 9.1 %collective-permute-start.13 = (f32[128,256]{1,0:T(8,128)S(1)}, f32[128,256]{1,0:T(8,128)S(1)}, u32[]{:S(2)}, u32[]{:S(2)}) collective-permute-start(f32[128,256]{1,0:T(8,128)S(1)} %get-tuple-element.117.refs_0_), channel_id=1, source_target_pairs={{0,2},{1,3},{2,4},{3,5},{4,6},{5,7},{6,0},{7,1},{8,10},{9,11},{10,... | collective-permute-start | bytes 393224 | tf_op jit(solution)/shard_map/ppermute | solution.py:322
  72.4 7.7 %collective-permute-start.14 = (f32[128,256]{1,0:T(8,128)S(1)}, f32[128,256]{1,0:T(8,128)S(1)}, u32[]{:S(2)}, u32[]{:S(2)}) collective-permute-start(f32[128,256]{1,0:T(8,128)S(1)} %get-tuple-element.117.refs_0_), channel_id=1, source_target_pairs={{0,4},{1,5},{2,6},{3,7},{4,0},{5,1},{6,2},{7,3},{8,12},{9,13},{10,... | collective-permute-start | bytes 393224 | tf_op jit(solution)/shard_map/ppermute | solution.py:322
  72.9 7.4 %collective-permute-start.15 = (f32[128,256]{1,0:T(8,128)S(1)}, f32[128,256]{1,0:T(8,128)S(1)}, u32[]{:S(2)}, u32[]{:S(2)}) collective-permute-start(f32[128,256]{1,0:T(8,128)S(1)} %get-tuple-element.117.refs_0_), channel_id=1, source_target_pairs={{0,6},{1,7},{2,0},{3,1},{4,2},{5,3},{6,4},{7,5},{8,14},{9,15},{10,... | collective-permute-start | bytes 393224 | tf_op jit(solution)/shard_map/ppermute | solution.py:322
  80.3 5.1 %copy-start.1 = (s32[2048,2]{0,1:T(2,128)S(1)}, s32[2048,2]{0,1:T(2,128)}, u32[]{:S(2)}) copy-start(s32[2048,2]{0,1:T(2,128)} %param.9) | copy-start | bytes 49156
  80.4 5.1 %collective-permute-start.16 = (f32[512,256]{1,0:T(8,128)S(1)}, f32[512,256]{1,0:T(8,128)S(1)}, u32[]{:S(2)}, u32[]{:S(2)}) collective-permute-start(f32[512,256]{1,0:T(8,128)S(1)} %shard_map.98.mine_ref), channel_id=1, source_target_pairs={{0,1},{1,0},{2,3},{3,2},{4,5},{5,4},{6,7},{7,6},{8,9},{9,8},{10,11... | collective-permute-start | bytes 1572872 | tf_op jit(solution)/shard_map/ppermute | solution.py:372
  106.3 11.4 %collective-permute-start.17 = (f32[128,256]{1,0:T(8,128)S(1)}, f32[128,256]{1,0:T(8,128)S(1)}, u32[]{:S(2)}, u32[]{:S(2)}) collective-permute-start(f32[128,256]{1,0:T(8,128)S(1)} %get-tuple-element.126.refs_0_), channel_id=1, source_target_pairs={{0,40},{8,48},{16,56},{24,32},{32,72},{40,80},{48,88},{56,64},{64,... | collective-permute-start | bytes 393224 | tf_op jit(solution)/shard_map/ppermute | solution.py:331
  106.6 11.1 %collective-permute-start.18 = (f32[128,256]{1,0:T(8,128)S(1)}, f32[128,256]{1,0:T(8,128)S(1)}, u32[]{:S(2)}, u32[]{:S(2)}) collective-permute-start(f32[128,256]{1,0:T(8,128)S(1)} %get-tuple-element.126.refs_0_), channel_id=1, source_target_pairs={{0,80},{8,88},{16,64},{24,72},{32,112},{40,120},{48,96},{56,104},{... | collective-permute-start | bytes 393224 | tf_op jit(solution)/shard_map/ppermute | solution.py:331
  110.2 8.0 %collective-permute-start.19 = (f32[128,256]{1,0:T(8,128)S(1)}, f32[128,256]{1,0:T(8,128)S(1)}, u32[]{:S(2)}, u32[]{:S(2)}) collective-permute-start(f32[128,256]{1,0:T(8,128)S(1)} %get-tuple-element.126.refs_0_), channel_id=1, source_target_pairs={{0,120},{8,96},{16,104},{24,112},{32,24},{40,0},{48,8},{56,16},{64... | collective-permute-start | bytes 393224 | tf_op jit(solution)/shard_map/ppermute | solution.py:331
  118.3 14.2 %collective-permute-start.22 = (f32[512,256]{1,0:T(8,128)S(1)}, f32[512,256]{1,0:T(8,128)S(1)}, u32[]{:S(2)}, u32[]{:S(2)}) collective-permute-start(f32[512,256]{1,0:T(8,128)S(1)} %shard_map.102.khatri_ref), channel_id=1, source_target_pairs={{0,8},{8,16},{16,24},{24,0},{32,40},{40,48},{48,56},{56,32},{64,72... | collective-permute-start | bytes 1572872 | tf_op jit(solution)/shard_map/ppermute | solution.py:336
  118.9 14.7 %collective-permute-start.21 = (f32[512,256]{1,0:T(8,128)S(1)}, f32[512,256]{1,0:T(8,128)S(1)}, u32[]{:S(2)}, u32[]{:S(2)}) collective-permute-start(f32[512,256]{1,0:T(8,128)S(1)} %shard_map.102.khatri_ref), channel_id=1, source_target_pairs={{0,24},{8,0},{16,8},{24,16},{32,56},{40,32},{48,40},{56,48},{64,88... | collective-permute-start | bytes 1572872 | tf_op jit(solution)/shard_map/ppermute | solution.py:336
  121.6 14.0 %collective-permute-start.20 = (f32[512,256]{1,0:T(8,128)S(1)}, f32[512,256]{1,0:T(8,128)S(1)}, u32[]{:S(2)}, u32[]{:S(2)}) collective-permute-start(f32[512,256]{1,0:T(8,128)S(1)} %shard_map.102.khatri_ref), channel_id=1, source_target_pairs={{0,64},{8,72},{16,80},{24,88},{32,96},{40,104},{48,112},{56,120},{... | collective-permute-start | bytes 1572872 | tf_op jit(solution)/shard_map/ppermute | solution.py:336
  136.3 2.4 %collective-permute-start.23 = (f32[4,192,256]{2,1,0:T(8,128)S(1)}, f32[4,192,256]{2,1,0:T(8,128)S(1)}, u32[]{:S(2)}, u32[]{:S(2)}) collective-permute-start(f32[4,192,256]{2,1,0:T(8,128)S(1)} %shard_map.107.given_ref), channel_id=1, source_target_pairs={{0,1},{1,0},{2,3},{3,2},{4,5},{5,4},{6,7},{7,6},{8,9},{9,8},{10,11... | collective-permute-start | bytes 2359304 | tf_op jit(solution)/shard_map/ppermute | solution.py:349
  138.7 9.4 %collective-permute-start.24 = (f32[192,256]{1,0:T(8,128)S(1)}, f32[192,256]{1,0:T(8,128)S(1)}, u32[]{:S(2)}, u32[]{:S(2)}) collective-permute-start(f32[192,256]{1,0:T(8,128)S(1)} %get-tuple-element.150), channel_id=1, source_target_pairs={{0,4},{1,5},{2,6},{3,7},{4,0},{5,1},{6,2},{7,3},{8,12},{9,13},{10,... | collective-permute-start | bytes 589832 | tf_op jit(solution)/shard_map/ppermute | solution.py:359
  140.7 10.8 %collective-permute-start.25 = (f32[192,256]{1,0:T(8,128)S(1)}, f32[192,256]{1,0:T(8,128)S(1)}, u32[]{:S(2)}, u32[]{:S(2)}) collective-permute-start(f32[192,256]{1,0:T(8,128)S(1)} %get-tuple-element.151), channel_id=1, source_target_pairs={{0,2},{1,3},{2,4},{3,5},{4,6},{5,7},{6,0},{7,1},{8,10},{9,11},{10,... | collective-permute-start | bytes 589832 | tf_op jit(solution)/shard_map/ppermute | solution.py:359
  142.3 9.2 %collective-permute-start.26 = (f32[192,256]{1,0:T(8,128)S(1)}, f32[192,256]{1,0:T(8,128)S(1)}, u32[]{:S(2)}, u32[]{:S(2)}) collective-permute-start(f32[192,256]{1,0:T(8,128)S(1)} %get-tuple-element.152), channel_id=1, source_target_pairs={{0,6},{1,7},{2,0},{3,1},{4,2},{5,3},{6,4},{7,5},{8,14},{9,15},{10,... | collective-permute-start | bytes 589832 | tf_op jit(solution)/shard_map/ppermute | solution.py:359
  151.5 6.6 %collective-permute-start.27 = (f32[64,256]{1,0:T(8,128)S(1)}, f32[64,256]{1,0:T(8,128)S(1)}, u32[]{:S(2)}, u32[]{:S(2)}) collective-permute-start(f32[64,256]{1,0:T(8,128)S(1)} %get-tuple-element.153.refs_0_), channel_id=1, source_target_pairs={{0,2},{1,3},{2,4},{3,5},{4,6},{5,7},{6,0},{7,1},{8,10},{9,11},{10,... | collective-permute-start | bytes 196616 | tf_op jit(solution)/shard_map/ppermute | solution.py:322
  152.6 7.8 %collective-permute-start.28 = (f32[64,256]{1,0:T(8,128)S(1)}, f32[64,256]{1,0:T(8,128)S(1)}, u32[]{:S(2)}, u32[]{:S(2)}) collective-permute-start(f32[64,256]{1,0:T(8,128)S(1)} %get-tuple-element.153.refs_0_), channel_id=1, source_target_pairs={{0,4},{1,5},{2,6},{3,7},{4,0},{5,1},{6,2},{7,3},{8,12},{9,13},{10,... | collective-permute-start | bytes 196616 | tf_op jit(solution)/shard_map/ppermute | solution.py:322
  155.7 4.7 %collective-permute-start.29 = (f32[64,256]{1,0:T(8,128)S(1)}, f32[64,256]{1,0:T(8,128)S(1)}, u32[]{:S(2)}, u32[]{:S(2)}) collective-permute-start(f32[64,256]{1,0:T(8,128)S(1)} %get-tuple-element.153.refs_0_), channel_id=1, source_target_pairs={{0,6},{1,7},{2,0},{3,1},{4,2},{5,3},{6,4},{7,5},{8,14},{9,15},{10,... | collective-permute-start | bytes 196616 | tf_op jit(solution)/shard_map/ppermute | solution.py:322
  156.1 9.3 %collective-permute-start.30 = (f32[128,256]{1,0:T(8,128)S(1)}, f32[128,256]{1,0:T(8,128)S(1)}, u32[]{:S(2)}, u32[]{:S(2)}) collective-permute-start(f32[128,256]{1,0:T(8,128)S(1)} %get-tuple-element.158.refs_0_), channel_id=1, source_target_pairs={{0,2},{1,3},{2,4},{3,5},{4,6},{5,7},{6,0},{7,1},{8,10},{9,11},{10,... | collective-permute-start | bytes 393224 | tf_op jit(solution)/shard_map/ppermute | solution.py:322
  157.7 7.7 %collective-permute-start.31 = (f32[128,256]{1,0:T(8,128)S(1)}, f32[128,256]{1,0:T(8,128)S(1)}, u32[]{:S(2)}, u32[]{:S(2)}) collective-permute-start(f32[128,256]{1,0:T(8,128)S(1)} %get-tuple-element.158.refs_0_), channel_id=1, source_target_pairs={{0,4},{1,5},{2,6},{3,7},{4,0},{5,1},{6,2},{7,3},{8,12},{9,13},{10,... | collective-permute-start | bytes 393224 | tf_op jit(solution)/shard_map/ppermute | solution.py:322
  158.2 7.4 %collective-permute-start.32 = (f32[128,256]{1,0:T(8,128)S(1)}, f32[128,256]{1,0:T(8,128)S(1)}, u32[]{:S(2)}, u32[]{:S(2)}) collective-permute-start(f32[128,256]{1,0:T(8,128)S(1)} %get-tuple-element.158.refs_0_), channel_id=1, source_target_pairs={{0,6},{1,7},{2,0},{3,1},{4,2},{5,3},{6,4},{7,5},{8,14},{9,15},{10,... | collective-permute-start | bytes 393224 | tf_op jit(solution)/shard_map/ppermute | solution.py:322
  165.6 5.1 %collective-permute-start.33 = (f32[512,256]{1,0:T(8,128)S(1)}, f32[512,256]{1,0:T(8,128)S(1)}, u32[]{:S(2)}, u32[]{:S(2)}) collective-permute-start(f32[512,256]{1,0:T(8,128)S(1)} %shard_map.112.mine_ref), channel_id=1, source_target_pairs={{0,1},{1,0},{2,3},{3,2},{4,5},{5,4},{6,7},{7,6},{8,9},{9,8},{10,11... | collective-permute-start | bytes 1572872 | tf_op jit(solution)/shard_map/ppermute | solution.py:372
where the time goes:
time: 185 us; the launch traced here: 184 us
  starting transfers between devices  51.7 us (28%)
  blocking collectives  48.1 us (26%)
  Pallas kernels  45.6 us (25%)
  waiting for transfers between devices  36.4 us (20%)
    all_to_all x3, blocking collectives, exchange(): return lax.all_to_all(rows, 'row', 0, 0, tiled=True)  48.1 us
    pallas_call x31, Pallas kernels, call(): pl.pallas_call(kernel, out_shape=out, in_specs=specs or [VMEM] * len(args...  45.6 us
    ppermute x12, starting transfers between devices, from_z(): got = {step: lax.ppermute(own, 'samp', along_z(step)) for step in FAR_FIRST}  17.8 us
    ppermute x6, waiting for transfers between devices, summed(): lax.ppermute(pairs[step], 'samp', along_z(step))  14.5 us
    ppermute x6, starting transfers between devices, summed(): lax.ppermute(pairs[step], 'samp', along_z(step))  12.3 us
    ppermute x6, starting transfers between devices, sums_over_row_group(): lax.ppermute(block, 'row', in_plane(step, step))  12.1 us
    ppermute x6, waiting for transfers between devices, sums_over_row_group(): lax.ppermute(block, 'row', in_plane(step, step))  11 us
    ppermute x6, starting transfers between devices, sums_over_row_group(): lax.ppermute(piece, 'row', in_plane(*move))  9.16 us
  transfers between devices with their start and end apart: 34, of which 17 were waited for; matrix products, arithmetic and copies ran while one was open for 1% of the time, Pallas kernels for 20%

commit v1 on v0

--- a/solution.py
+++ b/solution.py
@@ -141,7 +141,7 @@
 
 
 def column_scale(got_ref, at, count):
-    squares = jnp.sum(got_ref[:, at : at + 8, :], axis=0)
+    squares = jnp.sum(got_ref[:, at : min(at + 8, got_ref.shape[1]), :], axis=0)
     return jnp.sqrt(squares[0:1, :] / count + 1e-6)
 
 
@@ -192,15 +192,19 @@
 
 
 def first_inverse_kernel(*refs):
-    pieces, (a_ref, w_ref, rest_ref, gram_ref) = refs[:4], refs[4:]
+    pieces, (a_ref, w_ref, rest_ref, p_ref, q_ref, r_ref) = refs[:4], refs[4:]
     z, _ = position()
-    rows = pieces[0].shape[0]
+    h = p_ref.shape[0]
+    rows, few = h // 4, h // 8
     for step, piece in enumerate(pieces):
-        gram_ref[pl.ds(pl.multiple_of(quarter(z, -step) * rows, rows), rows), :] = piece[...]
-    h = gram_ref.shape[0] // 2
-    a_ref[...] = invert_block([gram_ref[8 * i : 8 * i + 8, :h] for i in range(h // 8)])
-    w_ref[...] = dot(a_ref[...], gram_ref[:h, h:])
-    rest_ref[...] = gram_ref[h:, h:] - dot(gram_ref[h:, :h], w_ref[...])
+        place = quarter(z, -step)
+        at = pl.ds(pl.multiple_of(place * rows, rows), rows)
+        low = pl.multiple_of(place * few, few)
+        p_ref[at, :], r_ref[at, :] = piece[:rows, :h], piece[:rows, h:]
+        q_ref[pl.ds(low, few), :], q_ref[pl.ds(low + h // 2, few), :] = piece[rows:, :h], piece[rows:, h:]
+    a_ref[...] = invert_block([p_ref[8 * i : 8 * i + 8, :] for i in range(h // 8)])
+    w_ref[...] = dot(a_ref[...], q_ref[...])
+    rest_ref[...] = r_ref[...] - dot(q_ref[...], w_ref[...], (0, 0))
 
 
 def second_inverse_kernel(a_ref, w_ref, rest_ref, out_ref):
@@ -224,7 +228,7 @@
     return call(lambda *refs: join_kernel(place, *refs), shape(4 * rows, rank), *pieces, size=2**20)
 
 
-DIAGONALS = (0, -1, 1, 2)
+LINES = (0, -1, 1, 2)
 
 
 def split_kernel(fibres_ref, *refs):
@@ -232,11 +236,11 @@
     x, y = place_in_row()
     _, _, rows, _ = held.shape
     copies = []
-    for n, beside in enumerate(DIAGONALS):
+    for n, beside in enumerate(LINES):
         for half in range(2):
             copies.append([])
             for place in range(4):
-                at = pl.multiple_of((4 * place + quarter(x - y + 4, place + beside)) * BLOCK, BLOCK)
+                at = pl.multiple_of((4 * place + quarter(x - 2 * y + 8, 2 * place + beside)) * BLOCK, BLOCK)
                 source = fibres_ref.at[half * rows : (half + 1) * rows, pl.ds(at, BLOCK)]
                 target = held.at[n, half, :, place * BLOCK : (place + 1) * BLOCK]
                 copies[-1].append(pltpu.make_async_copy(source, target, sems.at[n, half, place]))
@@ -294,9 +298,14 @@
     khatri = halves(khatri_ref[...])
     half_of(high_ref, low_ref, khatri, total_ref, 1 - core, out_ref)
     gram = gram_of(*khatri) + gram_ref[...]
-    rows = gram.shape[0] // 4
+    h = gram.shape[0] // 2
+    rows, few = h // 4, h // 8
     for place in range(4):
-        out_ref[place, BLOCK:, :] = gram[place * rows : (place + 1) * rows]
+        at, low = slice(place * rows, (place + 1) * rows), place * few
+        out_ref[place, BLOCK : BLOCK + rows, :h] = gram[at, :h]
+        out_ref[place, BLOCK : BLOCK + rows, h:] = gram[h:, h:][at]
+        out_ref[place, BLOCK + rows :, :h] = gram[low : low + few, h:]
+        out_ref[place, BLOCK + rows :, h:] = gram[h // 2 + low : h // 2 + low + few, h:]
 
 
 def kept_kernel(high_ref, low_ref, khatri_ref, total_ref, given_ref, out_ref):
@@ -328,15 +337,15 @@
     rows, samples = fibres.shape
     depth = samples // 4
     flops = 6 * rows * depth * rank
-    near = {step: lax.ppermute(block, "row", in_plane(step, step)) for step in FAR_FIRST}
+    near = {step: lax.ppermute(block, "row", in_plane(step, 2 * step)) for step in FAR_FIRST}
     piece = joined([block, near[1], near[2], near[3]], lambda: place_in_row()[1])
     fibres, piece = lax.optimization_barrier((fibres, piece))
     parts = split(fibres)
-    moves = {-1: (0, 1), 1: (0, -1), 2: (2, 0)}
+    moves = {-1: (0, 1), 1: (0, -1), 2: (1, 0)}
     pieces = {beside: lax.ppermute(piece, "row", in_plane(*move)) for beside, move in moves.items()}
     pieces[0] = piece
     state = ()
-    for n, beside in enumerate(DIAGONALS[:3]):
+    for n, beside in enumerate(LINES[:3]):
         high, low = parts[2 * n : 2 * n + 2]
         out = (shape(rows, rank), shape(rank, rank))
         state = call(piece_kernel, out, high, low, pieces[beside], *state, flops=flops, size=2**22)
@@ -344,7 +353,7 @@
             state, extra = lax.optimization_barrier((state, aside(piece)))
     total, gram = state
     high, low = parts[6:]
-    out = shape(4, BLOCK + rank // 4, rank)
+    out = shape(4, BLOCK + 3 * rank // 16, rank)
     given = call(given_kernel, out, high, low, pieces[2], total, gram, flops=flops, size=2**21)
     got = lax.ppermute(given, "samp", CORE)
     kept = call(kept_kernel, out, high, low, pieces[2], total, given, flops=flops // 2, size=2**21)
@@ -357,13 +366,13 @@
     rows = kept.shape[1]
     pairs = call(pair_kernel, (shape(rows, rank),) * 4, kept, got, size=2**21)
     parts = [pairs[0]] + [lax.ppermute(pairs[step], "samp", along_z(step)) for step in FAR_FIRST]
-    product, gram = call(quarter_kernel, (shape(BLOCK, rank), shape(rank // 4, rank)), *parts, size=2**20)
+    product, gram = call(quarter_kernel, (shape(BLOCK, rank), shape(3 * rank // 16, rank)), *parts, size=2**20)
     h = rank // 2
     first = call(
         first_inverse_kernel,
         (shape(h, h),) * 3,
         *from_z(gram),
-        scratch_shapes=[pltpu.VMEM((rank, rank), F32)],
+        scratch_shapes=[pltpu.VMEM((h, h), F32)] * 3,
         flops=10**11,
         size=2**19,
     )
@@ -382,18 +391,19 @@
         out_ref[pl.ds(pl.multiple_of(owner * rows, rows), rows), :] = three_dots(*halves(ref[...]), *inverse)
 
 
-def select_kernel(index_ref, c_ref, out_ref):
+def select_kernel(index_ref, c_ref, out_ref, slots_ref):
     select_into(out_ref, 0, slots_of(index_ref, 1, c_ref.shape[0]), c_ref[...])
-
-
-def first_solve_kernel(mine_ref, other_ref, inverse_ref, index_ref, chosen_ref, solved_ref, out_ref):
+    slots_ref[...] = slots_of(index_ref, 0, c_ref.shape[0])
+
+
+def first_solve_kernel(mine_ref, other_ref, inverse_ref, chosen_ref, slots_ref, solved_ref, out_ref):
     solve_into(solved_ref, mine_ref, other_ref, inverse_ref)
     solved = solved_ref[...]
     peers, _, rank = out_ref.shape
     squares = jnp.sum(solved * solved, axis=0, keepdims=True)
     out_ref[:, 2 * CAP :, :] = jnp.broadcast_to(squares[None], (peers, 8, rank))
     out_ref[:, CAP : 2 * CAP, :] = chosen_ref[...]
-    select_into(out_ref, 0, slots_of(index_ref, 0, solved.shape[0]), solved)
+    select_into(out_ref, 0, slots_ref[...], solved)
 
 
 def second_solve_kernel(mine_ref, other_ref, inverse_ref, solved_ref, out_ref):
@@ -423,7 +433,8 @@
 
     def choose(piece):
         index, rows, _ = lax.optimization_barrier((second, factor_c, piece))
-        return call(select_kernel, shape(peers, CAP, rank), index, rows, flops=10**9, size=2**21)
+        out = (shape(peers, CAP, rank), shape(peers * CAP, height, dtype=BF16))
+        return call(select_kernel, out, index, rows, flops=10**9, size=2**21)
 
     mine, other, inverse, chosen = summed(fibres_first, block, choose)
     solved, sent = call(
@@ -432,8 +443,7 @@
         mine,
         other,
         inverse,
-        second,
-        chosen,
+        *chosen,
         flops=10**9,
         size=2**21,
     )
@@ -453,7 +463,7 @@
     mine, other, inverse, factor_a = summed(fibres_second, block, normalise)
     solved, sent = call(
         second_solve_kernel,
-        (shape(height, rank), shape(peers, 8, rank)),
+        (shape(height, rank), shape(peers, 1, rank)),
         mine,
         other,
         inverse,

time: 185 us -> 180 us (0.973)
  waiting for transfers between devices: 36.4 us -> 32.4 us
  transfers between devices with their start and end apart: 34 -> 34, of which waited for: 17 -> 15; matrix products, arithmetic and copies ran while one was open for 1% -> 1% of each run, Pallas kernels for 20% -> 20%
where the time goes in v1:
time: 180 us
  starting transfers between devices  51.7 us (29%)
  blocking collectives  47.3 us (26%)
  Pallas kernels  45.6 us (25%)
  waiting for transfers between devices  32.4 us (18%)
    all_to_all x3, blocking collectives, exchange(): return lax.all_to_all(rows, 'row', 0, 0, tiled=True)  47.3 us
    pallas_call x31, Pallas kernels, call(): pl.pallas_call(kernel, out_shape=out, in_specs=specs or [VMEM] * len(args...  45.6 us
    ppermute x12, starting transfers between devices, from_z(): got = {step: lax.ppermute(own, 'samp', along_z(step)) for step in FAR_FIRST}  17.8 us
    ppermute x6, waiting for transfers between devices, summed(): lax.ppermute(pairs[step], 'samp', along_z(step))  12.9 us
    ppermute x6, starting transfers between devices, summed(): lax.ppermute(pairs[step], 'samp', along_z(step))  12.5 us
    ppermute x6, starting transfers between devices, sums_over_row_group(): lax.ppermute(block, 'row', in_plane(step, 2 * step))  12 us
    ppermute x6, waiting for transfers between devices, sums_over_row_group(): lax.ppermute(block, 'row', in_plane(step, 2 * step))  9.5 us
    ppermute x6, starting transfers between devices, sums_over_row_group(): lax.ppermute(piece, 'row', in_plane(*move))  9.04 us
  transfers between devices with their start and end apart: 34, of which 15 were waited for; matrix products, arithmetic and copies ran while one was open for 1% of the time, Pallas kernels for 20%

profile of v1, /device:TPU:0, one launch (start us, length us, event | category | flops | bytes accessed | tf_op | source)
XLA Modules:
  0.0 179.7 jit_solution(14322885109055654895)
XLA Ops:
  0.7 2.7 %shard_map.85 = (f32[16,32,256]{2,1,0:T(8,128)S(1)}, s32[2,2048]{1,0:T(2,128)S(1)}) custom-call(s32[2,2048]{1,0:T(2,128)} %bitcast.8, f32[1024,256]{1,0:T(8,128)} %b_hbm.1, f32[1024,256]{1,0:T(8,128)} %c_ref), custom_call_target="tpu_custom_call" | custom-call | flops 1000000000 | bytes 2097152 | tf_op jit(solution)/shard_map/pallas_call | solution.py:26
  3.4 18.5 %all_to_all.15.refs_1_ = f32[16,32,256]{2,1,0:T(8,128)S(1)} all-to-all(f32[16,32,256]{2,1,0:T(8,128)S(1)} %get-tuple-element.90), channel_id=1, replica_groups=mesh['row'=16,'samp'=8] {'row'}, dimensions={0} | all-to-all | bytes 1048576 | tf_op jit(solution)/shard_map/all_to_all | solution.py:422
  23.3 1.9 %collective-permute-start.1 = (f32[128,256]{1,0:T(8,128)S(1)}, f32[128,256]{1,0:T(8,128)S(1)}, u32[]{:S(2)}, u32[]{:S(2)}) collective-permute-start(f32[128,256]{1,0:T(8,128)S(1)} %shard_map.86.refs_0_), channel_id=1, source_target_pairs={{0,64},{8,72},{16,80},{24,88},{32,96},{40,104},{48,112},{56,120},{... | collective-permute-start | bytes 393224 | tf_op jit(solution)/shard_map/ppermute | solution.py:340
  25.2 3.1 %collective-permute-start.2 = (f32[128,256]{1,0:T(8,128)S(1)}, f32[128,256]{1,0:T(8,128)S(1)}, u32[]{:S(2)}, u32[]{:S(2)}) collective-permute-start(f32[128,256]{1,0:T(8,128)S(1)} %shard_map.86.refs_0_), channel_id=1, source_target_pairs={{0,112},{8,120},{16,96},{24,104},{32,16},{40,24},{48,0},{56,8},{64... | collective-permute-start | bytes 393224 | tf_op jit(solution)/shard_map/ppermute | solution.py:340
  28.3 3.9 %collective-permute-done.refs_1_ = f32[128,256]{1,0:T(8,128)S(1)} collective-permute-done((f32[128,256]{1,0:T(8,128)S(1)}, f32[128,256]{1,0:T(8,128)S(1)}, u32[]{:S(2)}, u32[]{:S(2)}) %collective-permute-start) | collective-permute-done | bytes 131104 | tf_op jit(solution)/shard_map/ppermute | solution.py:340
  33.4 2.6 %collective-permute-start.4 = (f32[512,256]{1,0:T(8,128)S(1)}, f32[512,256]{1,0:T(8,128)S(1)}, u32[]{:S(2)}, u32[]{:S(2)}) collective-permute-start(f32[512,256]{1,0:T(8,128)S(1)} %shard_map.87.khatri_ref), channel_id=1, source_target_pairs={{0,24},{8,0},{16,8},{24,16},{32,56},{40,32},{48,40},{56,48},{64,88... | collective-permute-start | bytes 1572872 | tf_op jit(solution)/shard_map/ppermute | solution.py:345
  35.9 1.5 collective-permute-start.3
  37.5 3.9 %shard_map.88 = (bf16[1024,512]{1,0:T(8,128)(2,1)S(1)}, bf16[1024,512]{1,0:T(8,128)(2,1)S(1)}, bf16[1024,512]{1,0:T(8,128)(2,1)S(1)}, bf16[1024,512]{1,0:T(8,128...) custom-call(f32[1024,2048]{1,0:T(8,128)} %fibres_ref), custom_call_target="tpu_custom_call" | custom-call | flops 8388608 | bytes 16777216 | tf_op jit(solution)/shard_map/pallas_call | solution.py:26
  41.4 1.1 shard_map.89
  43.4 1.8 %collective-permute-done.5.khatri_ref = f32[512,256]{1,0:T(8,128)S(1)} collective-permute-done((f32[512,256]{1,0:T(8,128)S(1)}, f32[512,256]{1,0:T(8,128)S(1)}, u32[]{:S(2)}, u32[]{:S(2)}) %collective-permute-start.5) | collective-permute-done | bytes 524320 | tf_op jit(solution)/shard_map/ppermute | solution.py:345
  45.2 1.1 shard_map.91
  46.4 1.1 shard_map.92
  49.3 1.6 collective-permute-done.6.given_ref
  51.0 4.0 %collective-permute-start.7 = (f32[176,256]{1,0:T(8,128)S(1)}, f32[176,256]{1,0:T(8,128)S(1)}, u32[]{:S(2)}, u32[]{:S(2)}) collective-permute-start(f32[176,256]{1,0:T(8,128)S(1)} %get-tuple-element.114), channel_id=1, source_target_pairs={{0,4},{1,5},{2,6},{3,7},{4,0},{5,1},{6,2},{7,3},{8,12},{9,13},{10,... | collective-permute-start | bytes 540680 | tf_op jit(solution)/shard_map/ppermute | solution.py:368
  56.0 2.2 %collective-permute-start.9 = (f32[176,256]{1,0:T(8,128)S(1)}, f32[176,256]{1,0:T(8,128)S(1)}, u32[]{:S(2)}, u32[]{:S(2)}) collective-permute-start(f32[176,256]{1,0:T(8,128)S(1)} %get-tuple-element.116), channel_id=1, source_target_pairs={{0,6},{1,7},{2,0},{3,1},{4,2},{5,3},{6,4},{7,5},{8,14},{9,15},{10,... | collective-permute-start | bytes 540680 | tf_op jit(solution)/shard_map/ppermute | solution.py:368
  58.2 2.1 %collective-permute-done.7.b = f32[176,256]{1,0:T(8,128)S(1)} collective-permute-done((f32[176,256]{1,0:T(8,128)S(1)}, f32[176,256]{1,0:T(8,128)S(1)}, u32[]{:S(2)}, u32[]{:S(2)}) %collective-permute-start.7) | collective-permute-done | bytes 180256 | tf_op jit(solution)/shard_map/ppermute | solution.py:368
  60.3 3.4 %collective-permute-done.8.c = f32[176,256]{1,0:T(8,128)S(1)} collective-permute-done((f32[176,256]{1,0:T(8,128)S(1)}, f32[176,256]{1,0:T(8,128)S(1)}, u32[]{:S(2)}, u32[]{:S(2)}) %collective-permute-start.8) | collective-permute-done | bytes 180256 | tf_op jit(solution)/shard_map/ppermute | solution.py:368
  64.4 1.1 collective-permute-start.10
  65.6 3.1 %collective-permute-start.11 = (f32[48,256]{1,0:T(8,128)S(1)}, f32[48,256]{1,0:T(8,128)S(1)}, u32[]{:S(2)}, u32[]{:S(2)}) collective-permute-start(f32[48,256]{1,0:T(8,128)S(1)} %get-tuple-element.117.refs_0_), channel_id=1, source_target_pairs={{0,4},{1,5},{2,6},{3,7},{4,0},{5,1},{6,2},{7,3},{8,12},{9,13},{10,... | collective-permute-start | bytes 147464 | tf_op jit(solution)/shard_map/ppermute | solution.py:331
  69.2 1.5 collective-permute-start.13
  71.1 2.2 %collective-permute-start.15 = (f32[128,256]{1,0:T(8,128)S(1)}, f32[128,256]{1,0:T(8,128)S(1)}, u32[]{:S(2)}, u32[]{:S(2)}) collective-permute-start(f32[128,256]{1,0:T(8,128)S(1)} %get-tuple-element.122.refs_0_), channel_id=1, source_target_pairs={{0,6},{1,7},{2,0},{3,1},{4,2},{5,3},{6,4},{7,5},{8,14},{9,15},{10,... | collective-permute-start | bytes 393224 | tf_op jit(solution)/shard_map/ppermute | solution.py:331
  73.4 5.0 %shard_map.97 = (f32[128,128]{1,0:T(8,128)S(1)}, f32[128,128]{1,0:T(8,128)S(1)}, f32[128,128]{1,0:T(8,128)S(1)}) custom-call(f32[48,256]{1,0:T(8,128)S(1)} %get-tuple-element.117.refs_0_, f32[48,256]{1,0:T(8,128)S(1)} %collective-permute-done.10.refs_1_, f32[48,256]{1,0:T(8,128)S(1)} %collective-permute-done.11.refs_2_, ...), custom_call_target="tpu_custom_call" | custom-call | flops 99999997952 | bytes 524288 | tf_op jit(solution)/shard_map/pallas_call | solution.py:26
  78.5 5.0 %shard_map.99.inverse_ref = f32[256,256]{1,0:T(8,128)S(1)} custom-call(f32[128,128]{1,0:T(8,128)S(1)} %get-tuple-element.126.a_ref, f32[128,128]{1,0:T(8,128)S(1)} %get-tuple-element.127.w_ref, f32[128,128]{1,0:T(8,128)S(1)} %get-tuple-element.128.rest_ref), custom_call_target="tpu_custom_call" | custom-call | flops 99999997952 | bytes 524288 | tf_op jit(solution)/shard_map/pallas_call | solution.py:26
  83.5 1.8 shard_map.100
  85.2 18.5 %all_to_all.16.refs_1_ = f32[16,40,256]{2,1,0:T(8,128)S(1)} all-to-all(f32[16,40,256]{2,1,0:T(8,128)S(1)} %get-tuple-element.131), channel_id=1, replica_groups=mesh['row'=16,'samp'=8] {'row'}, dimensions={0} | all-to-all | bytes 1310720 | tf_op jit(solution)/shard_map/all_to_all | solution.py:422
  104.4 1.3 collective-permute-start.17
  105.6 2.1 %collective-permute-start.18 = (f32[128,256]{1,0:T(8,128)S(1)}, f32[128,256]{1,0:T(8,128)S(1)}, u32[]{:S(2)}, u32[]{:S(2)}) collective-permute-start(f32[128,256]{1,0:T(8,128)S(1)} %get-tuple-element.132.refs_0_), channel_id=1, source_target_pairs={{0,64},{8,72},{16,80},{24,88},{32,96},{40,104},{48,112},{56,120},{... | collective-permute-start | bytes 393224 | tf_op jit(solution)/shard_map/ppermute | solution.py:340
  107.7 2.7 %collective-permute-start.19 = (f32[128,256]{1,0:T(8,128)S(1)}, f32[128,256]{1,0:T(8,128)S(1)}, u32[]{:S(2)}, u32[]{:S(2)}) collective-permute-start(f32[128,256]{1,0:T(8,128)S(1)} %get-tuple-element.132.refs_0_), channel_id=1, source_target_pairs={{0,112},{8,120},{16,96},{24,104},{32,16},{40,24},{48,0},{56,8},{64... | collective-permute-start | bytes 393224 | tf_op jit(solution)/shard_map/ppermute | solution.py:340
  110.4 4.7 %collective-permute-done.17.refs_1_ = f32[128,256]{1,0:T(8,128)S(1)} collective-permute-done((f32[128,256]{1,0:T(8,128)S(1)}, f32[128,256]{1,0:T(8,128)S(1)}, u32[]{:S(2)}, u32[]{:S(2)}) %collective-permute-start.17) | collective-permute-done | bytes 131104 | tf_op jit(solution)/shard_map/ppermute | solution.py:340
  115.9 3.1 %collective-permute-start.21 = (f32[512,256]{1,0:T(8,128)S(1)}, f32[512,256]{1,0:T(8,128)S(1)}, u32[]{:S(2)}, u32[]{:S(2)}) collective-permute-start(f32[512,256]{1,0:T(8,128)S(1)} %shard_map.102.khatri_ref), channel_id=1, source_target_pairs={{0,24},{8,0},{16,8},{24,16},{32,56},{40,32},{48,40},{56,48},{64,88... | collective-permute-start | bytes 1572872 | tf_op jit(solution)/shard_map/ppermute | solution.py:345
  119.9 3.9 %shard_map.103 = (bf16[1024,512]{1,0:T(8,128)(2,1)S(1)}, bf16[1024,512]{1,0:T(8,128)(2,1)S(1)}, bf16[1024,512]{1,0:T(8,128)(2,1)S(1)}, bf16[1024,512]{1,0:T(8,12...) custom-call(f32[1024,2048]{1,0:T(8,128)} %fibres_ref.1), custom_call_target="tpu_custom_call" | custom-call | flops 8388608 | bytes 16777216 | tf_op jit(solution)/shard_map/pallas_call | solution.py:26
  123.8 1.1 shard_map.104
  126.0 4.1 %collective-permute-done.22.khatri_ref = f32[512,256]{1,0:T(8,128)S(1)} collective-permute-done((f32[512,256]{1,0:T(8,128)S(1)}, f32[512,256]{1,0:T(8,128)S(1)}, u32[]{:S(2)}, u32[]{:S(2)}) %collective-permute-start.22) | collective-permute-done | bytes 524320 | tf_op jit(solution)/shard_map/ppermute | solution.py:345
  130.1 1.1 shard_map.105
  131.2 1.1 shard_map.106
  134.2 1.6 collective-permute-done.23.given_ref
  135.8 2.1 %collective-permute-start.24 = (f32[176,256]{1,0:T(8,128)S(1)}, f32[176,256]{1,0:T(8,128)S(1)}, u32[]{:S(2)}, u32[]{:S(2)}) collective-permute-start(f32[176,256]{1,0:T(8,128)S(1)} %get-tuple-element.156), channel_id=1, source_target_pairs={{0,4},{1,5},{2,6},{3,7},{4,0},{5,1},{6,2},{7,3},{8,12},{9,13},{10,... | collective-permute-start | bytes 540680 | tf_op jit(solution)/shard_map/ppermute | solution.py:368
  137.9 1.5 collective-permute-start.25
  139.4 1.7 collective-permute-start.26
  141.2 3.6 %collective-permute-done.24.b = f32[176,256]{1,0:T(8,128)S(1)} collective-permute-done((f32[176,256]{1,0:T(8,128)S(1)}, f32[176,256]{1,0:T(8,128)S(1)}, u32[]{:S(2)}, u32[]{:S(2)}) %collective-permute-start.24) | collective-permute-done | bytes 180256 | tf_op jit(solution)/shard_map/ppermute | solution.py:368
  144.8 3.0 %collective-permute-done.25.c = f32[176,256]{1,0:T(8,128)S(1)} collective-permute-done((f32[176,256]{1,0:T(8,128)S(1)}, f32[176,256]{1,0:T(8,128)S(1)}, u32[]{:S(2)}, u32[]{:S(2)}) %collective-permute-start.25) | collective-permute-done | bytes 180256 | tf_op jit(solution)/shard_map/ppermute | solution.py:368
  147.9 1.1 collective-permute-start.27
  149.0 3.1 %collective-permute-start.28 = (f32[48,256]{1,0:T(8,128)S(1)}, f32[48,256]{1,0:T(8,128)S(1)}, u32[]{:S(2)}, u32[]{:S(2)}) collective-permute-start(f32[48,256]{1,0:T(8,128)S(1)} %get-tuple-element.159.refs_0_), channel_id=1, source_target_pairs={{0,4},{1,5},{2,6},{3,7},{4,0},{5,1},{6,2},{7,3},{8,12},{9,13},{10,... | collective-permute-start | bytes 147464 | tf_op jit(solution)/shard_map/ppermute | solution.py:331
  152.6 1.5 collective-permute-start.30
  154.6 2.2 %collective-permute-start.32 = (f32[128,256]{1,0:T(8,128)S(1)}, f32[128,256]{1,0:T(8,128)S(1)}, u32[]{:S(2)}, u32[]{:S(2)}) collective-permute-start(f32[128,256]{1,0:T(8,128)S(1)} %get-tuple-element.164.refs_0_), channel_id=1, source_target_pairs={{0,6},{1,7},{2,0},{3,1},{4,2},{5,3},{6,4},{7,5},{8,14},{9,15},{10,... | collective-permute-start | bytes 393224 | tf_op jit(solution)/shard_map/ppermute | solution.py:331
  156.8 5.0 %shard_map.111 = (f32[128,128]{1,0:T(8,128)S(1)}, f32[128,128]{1,0:T(8,128)S(1)}, f32[128,128]{1,0:T(8,128)S(1)}) custom-call(f32[48,256]{1,0:T(8,128)S(1)} %get-tuple-element.159.refs_0_, f32[48,256]{1,0:T(8,128)S(1)} %collective-permute-done.27.refs_1_, f32[48,256]{1,0:T(8,128)S(1)} %collective-permute-done.28.refs_2_, ...), custom_call_target="tpu_custom_call" | custom-call | flops 99999997952 | bytes 524288 | tf_op jit(solution)/shard_map/pallas_call | solution.py:26
  162.0 5.0 %shard_map.113.inverse_ref = f32[256,256]{1,0:T(8,128)S(1)} custom-call(f32[128,128]{1,0:T(8,128)S(1)} %get-tuple-element.168.a_ref, f32[128,128]{1,0:T(8,128)S(1)} %get-tuple-element.169.w_ref, f32[128,128]{1,0:T(8,128)S(1)} %get-tuple-element.170.rest_ref), custom_call_target="tpu_custom_call" | custom-call | flops 99999997952 | bytes 524288 | tf_op jit(solution)/shard_map/pallas_call | solution.py:26
  167.8 10.3 %all_to_all.17.got_ref = f32[16,1,256]{2,1,0:T(1,128)S(1)} all-to-all(f32[16,1,256]{2,1,0:T(1,128)S(1)} %get-tuple-element.172), channel_id=1, replica_groups=mesh['row'=16,'samp'=8] {'row'}, dimensions={0} | all-to-all | bytes 32768 | tf_op jit(solution)/shard_map/all_to_all | solution.py:422
  (63 shorter events, 17.1 us)
Async XLA Ops:
  0.6 41.9 %copy-start = (s32[2048,2]{0,1:T(2,128)S(1)}, s32[2048,2]{0,1:T(2,128)}, u32[]{:S(2)}) copy-start(s32[2048,2]{0,1:T(2,128)} %param.9) | copy-start | bytes 49156
  0.6 41.9 %copy-start.2 = (f32[1024,256]{1,0:T(8,128)S(1)}, f32[1024,256]{1,0:T(8,128)}, u32[]{:S(2)}) copy-start(f32[1024,256]{1,0:T(8,128)} %c_ref) | copy-start | bytes 3145732
  22.3 9.9 %collective-permute-start = (f32[128,256]{1,0:T(8,128)S(1)}, f32[128,256]{1,0:T(8,128)S(1)}, u32[]{:S(2)}, u32[]{:S(2)}) collective-permute-start(f32[128,256]{1,0:T(8,128)S(1)} %shard_map.86.refs_0_), channel_id=1, source_target_pairs={{0,48},{8,56},{16,32},{24,40},{32,80},{40,88},{48,64},{56,72},{64,... | collective-permute-start | bytes 393224 | tf_op jit(solution)/shard_map/ppermute | solution.py:340
  23.3 8.9 %collective-permute-start.1 = (f32[128,256]{1,0:T(8,128)S(1)}, f32[128,256]{1,0:T(8,128)S(1)}, u32[]{:S(2)}, u32[]{:S(2)}) collective-permute-start(f32[128,256]{1,0:T(8,128)S(1)} %shard_map.86.refs_0_), channel_id=1, source_target_pairs={{0,64},{8,72},{16,80},{24,88},{32,96},{40,104},{48,112},{56,120},{... | collective-permute-start | bytes 393224 | tf_op jit(solution)/shard_map/ppermute | solution.py:340
  25.2 7.4 %collective-permute-start.2 = (f32[128,256]{1,0:T(8,128)S(1)}, f32[128,256]{1,0:T(8,128)S(1)}, u32[]{:S(2)}, u32[]{:S(2)}) collective-permute-start(f32[128,256]{1,0:T(8,128)S(1)} %shard_map.86.refs_0_), channel_id=1, source_target_pairs={{0,112},{8,120},{16,96},{24,104},{32,16},{40,24},{48,0},{56,8},{64... | collective-permute-start | bytes 393224 | tf_op jit(solution)/shard_map/ppermute | solution.py:340
  32.6 12.6 %collective-permute-start.5 = (f32[512,256]{1,0:T(8,128)S(1)}, f32[512,256]{1,0:T(8,128)S(1)}, u32[]{:S(2)}, u32[]{:S(2)}) collective-permute-start(f32[512,256]{1,0:T(8,128)S(1)} %shard_map.87.khatri_ref), channel_id=1, source_target_pairs={{0,8},{8,16},{16,24},{24,0},{32,40},{40,48},{48,56},{56,32},{64,72... | collective-permute-start | bytes 1572872 | tf_op jit(solution)/shard_map/ppermute | solution.py:345
  33.4 13.0 %collective-permute-start.4 = (f32[512,256]{1,0:T(8,128)S(1)}, f32[512,256]{1,0:T(8,128)S(1)}, u32[]{:S(2)}, u32[]{:S(2)}) collective-permute-start(f32[512,256]{1,0:T(8,128)S(1)} %shard_map.87.khatri_ref), channel_id=1, source_target_pairs={{0,24},{8,0},{16,8},{24,16},{32,56},{40,32},{48,40},{56,48},{64,88... | collective-permute-start | bytes 1572872 | tf_op jit(solution)/shard_map/ppermute | solution.py:345
  35.9 12.0 %collective-permute-start.3 = (f32[512,256]{1,0:T(8,128)S(1)}, f32[512,256]{1,0:T(8,128)S(1)}, u32[]{:S(2)}, u32[]{:S(2)}) collective-permute-start(f32[512,256]{1,0:T(8,128)S(1)} %shard_map.87.khatri_ref), channel_id=1, source_target_pairs={{0,32},{8,40},{16,48},{24,56},{32,64},{40,72},{48,80},{56,88},{64,... | collective-permute-start | bytes 1572872 | tf_op jit(solution)/shard_map/ppermute | solution.py:345
  48.6 2.3 %collective-permute-start.6 = (f32[4,176,256]{2,1,0:T(8,128)S(1)}, f32[4,176,256]{2,1,0:T(8,128)S(1)}, u32[]{:S(2)}, u32[]{:S(2)}) collective-permute-start(f32[4,176,256]{2,1,0:T(8,128)S(1)} %shard_map.93.given_ref), channel_id=1, source_target_pairs={{0,1},{1,0},{2,3},{3,2},{4,5},{5,4},{6,7},{7,6},{8,9},{9,8},{10,11... | collective-permute-start | bytes 2162696 | tf_op jit(solution)/shard_map/ppermute | solution.py:358
  51.0 9.3 %collective-permute-start.7 = (f32[176,256]{1,0:T(8,128)S(1)}, f32[176,256]{1,0:T(8,128)S(1)}, u32[]{:S(2)}, u32[]{:S(2)}) collective-permute-start(f32[176,256]{1,0:T(8,128)S(1)} %get-tuple-element.114), channel_id=1, source_target_pairs={{0,4},{1,5},{2,6},{3,7},{4,0},{5,1},{6,2},{7,3},{8,12},{9,13},{10,... | collective-permute-start | bytes 540680 | tf_op jit(solution)/shard_map/ppermute | solution.py:368
  54.9 8.7 %collective-permute-start.8 = (f32[176,256]{1,0:T(8,128)S(1)}, f32[176,256]{1,0:T(8,128)S(1)}, u32[]{:S(2)}, u32[]{:S(2)}) collective-permute-start(f32[176,256]{1,0:T(8,128)S(1)} %get-tuple-element.115), channel_id=1, source_target_pairs={{0,2},{1,3},{2,4},{3,5},{4,6},{5,7},{6,0},{7,1},{8,10},{9,11},{10,... | collective-permute-start | bytes 540680 | tf_op jit(solution)/shard_map/ppermute | solution.py:368
  56.0 8.4 %collective-permute-start.9 = (f32[176,256]{1,0:T(8,128)S(1)}, f32[176,256]{1,0:T(8,128)S(1)}, u32[]{:S(2)}, u32[]{:S(2)}) collective-permute-start(f32[176,256]{1,0:T(8,128)S(1)} %get-tuple-element.116), channel_id=1, source_target_pairs={{0,6},{1,7},{2,0},{3,1},{4,2},{5,3},{6,4},{7,5},{8,14},{9,15},{10,... | collective-permute-start | bytes 540680 | tf_op jit(solution)/shard_map/ppermute | solution.py:368
  64.4 6.7 %collective-permute-start.10 = (f32[48,256]{1,0:T(8,128)S(1)}, f32[48,256]{1,0:T(8,128)S(1)}, u32[]{:S(2)}, u32[]{:S(2)}) collective-permute-start(f32[48,256]{1,0:T(8,128)S(1)} %get-tuple-element.117.refs_0_), channel_id=1, source_target_pairs={{0,2},{1,3},{2,4},{3,5},{4,6},{5,7},{6,0},{7,1},{8,10},{9,11},{10,... | collective-permute-start | bytes 147464 | tf_op jit(solution)/shard_map/ppermute | solution.py:331
  65.6 7.8 %collective-permute-start.11 = (f32[48,256]{1,0:T(8,128)S(1)}, f32[48,256]{1,0:T(8,128)S(1)}, u32[]{:S(2)}, u32[]{:S(2)}) collective-permute-start(f32[48,256]{1,0:T(8,128)S(1)} %get-tuple-element.117.refs_0_), channel_id=1, source_target_pairs={{0,4},{1,5},{2,6},{3,7},{4,0},{5,1},{6,2},{7,3},{8,12},{9,13},{10,... | collective-permute-start | bytes 147464 | tf_op jit(solution)/shard_map/ppermute | solution.py:331
  68.6 4.7 %collective-permute-start.12 = (f32[48,256]{1,0:T(8,128)S(1)}, f32[48,256]{1,0:T(8,128)S(1)}, u32[]{:S(2)}, u32[]{:S(2)}) collective-permute-start(f32[48,256]{1,0:T(8,128)S(1)} %get-tuple-element.117.refs_0_), channel_id=1, source_target_pairs={{0,6},{1,7},{2,0},{3,1},{4,2},{5,3},{6,4},{7,5},{8,14},{9,15},{10,... | collective-permute-start | bytes 147464 | tf_op jit(solution)/shard_map/ppermute | solution.py:331
  69.2 9.1 %collective-permute-start.13 = (f32[128,256]{1,0:T(8,128)S(1)}, f32[128,256]{1,0:T(8,128)S(1)}, u32[]{:S(2)}, u32[]{:S(2)}) collective-permute-start(f32[128,256]{1,0:T(8,128)S(1)} %get-tuple-element.122.refs_0_), channel_id=1, source_target_pairs={{0,2},{1,3},{2,4},{3,5},{4,6},{5,7},{6,0},{7,1},{8,10},{9,11},{10,... | collective-permute-start | bytes 393224 | tf_op jit(solution)/shard_map/ppermute | solution.py:331
  70.7 7.7 %collective-permute-start.14 = (f32[128,256]{1,0:T(8,128)S(1)}, f32[128,256]{1,0:T(8,128)S(1)}, u32[]{:S(2)}, u32[]{:S(2)}) collective-permute-start(f32[128,256]{1,0:T(8,128)S(1)} %get-tuple-element.122.refs_0_), channel_id=1, source_target_pairs={{0,4},{1,5},{2,6},{3,7},{4,0},{5,1},{6,2},{7,3},{8,12},{9,13},{10,... | collective-permute-start | bytes 393224 | tf_op jit(solution)/shard_map/ppermute | solution.py:331
  71.1 7.2 %collective-permute-start.15 = (f32[128,256]{1,0:T(8,128)S(1)}, f32[128,256]{1,0:T(8,128)S(1)}, u32[]{:S(2)}, u32[]{:S(2)}) collective-permute-start(f32[128,256]{1,0:T(8,128)S(1)} %get-tuple-element.122.refs_0_), channel_id=1, source_target_pairs={{0,6},{1,7},{2,0},{3,1},{4,2},{5,3},{6,4},{7,5},{8,14},{9,15},{10,... | collective-permute-start | bytes 393224 | tf_op jit(solution)/shard_map/ppermute | solution.py:331
  78.4 25.4 %copy-start.1 = (s32[2048,2]{0,1:T(2,128)S(1)}, s32[2048,2]{0,1:T(2,128)}, u32[]{:S(2)}) copy-start(s32[2048,2]{0,1:T(2,128)} %param.9) | copy-start | bytes 49156
  78.4 5.1 %collective-permute-start.16 = (f32[512,256]{1,0:T(8,128)S(1)}, f32[512,256]{1,0:T(8,128)S(1)}, u32[]{:S(2)}, u32[]{:S(2)}) collective-permute-start(f32[512,256]{1,0:T(8,128)S(1)} %shard_map.98.mine_ref), channel_id=1, source_target_pairs={{0,1},{1,0},{2,3},{3,2},{4,5},{5,4},{6,7},{7,6},{8,9},{9,8},{10,11... | collective-permute-start | bytes 1572872 | tf_op jit(solution)/shard_map/ppermute | solution.py:381
  104.4 10.7 %collective-permute-start.17 = (f32[128,256]{1,0:T(8,128)S(1)}, f32[128,256]{1,0:T(8,128)S(1)}, u32[]{:S(2)}, u32[]{:S(2)}) collective-permute-start(f32[128,256]{1,0:T(8,128)S(1)} %get-tuple-element.132.refs_0_), channel_id=1, source_target_pairs={{0,48},{8,56},{16,32},{24,40},{32,80},{40,88},{48,64},{56,72},{64,... | collective-permute-start | bytes 393224 | tf_op jit(solution)/shard_map/ppermute | solution.py:340
  105.6 10.0 %collective-permute-start.18 = (f32[128,256]{1,0:T(8,128)S(1)}, f32[128,256]{1,0:T(8,128)S(1)}, u32[]{:S(2)}, u32[]{:S(2)}) collective-permute-start(f32[128,256]{1,0:T(8,128)S(1)} %get-tuple-element.132.refs_0_), channel_id=1, source_target_pairs={{0,64},{8,72},{16,80},{24,88},{32,96},{40,104},{48,112},{56,120},{... | collective-permute-start | bytes 393224 | tf_op jit(solution)/shard_map/ppermute | solution.py:340
  107.7 7.9 %collective-permute-start.19 = (f32[128,256]{1,0:T(8,128)S(1)}, f32[128,256]{1,0:T(8,128)S(1)}, u32[]{:S(2)}, u32[]{:S(2)}) collective-permute-start(f32[128,256]{1,0:T(8,128)S(1)} %get-tuple-element.132.refs_0_), channel_id=1, source_target_pairs={{0,112},{8,120},{16,96},{24,104},{32,16},{40,24},{48,0},{56,8},{64... | collective-permute-start | bytes 393224 | tf_op jit(solution)/shard_map/ppermute | solution.py:340
  115.7 14.4 %collective-permute-start.22 = (f32[512,256]{1,0:T(8,128)S(1)}, f32[512,256]{1,0:T(8,128)S(1)}, u32[]{:S(2)}, u32[]{:S(2)}) collective-permute-start(f32[512,256]{1,0:T(8,128)S(1)} %shard_map.102.khatri_ref), channel_id=1, source_target_pairs={{0,8},{8,16},{16,24},{24,0},{32,40},{40,48},{48,56},{56,32},{64,72... | collective-permute-start | bytes 1572872 | tf_op jit(solution)/shard_map/ppermute | solution.py:345
  115.9 15.3 %collective-permute-start.21 = (f32[512,256]{1,0:T(8,128)S(1)}, f32[512,256]{1,0:T(8,128)S(1)}, u32[]{:S(2)}, u32[]{:S(2)}) collective-permute-start(f32[512,256]{1,0:T(8,128)S(1)} %shard_map.102.khatri_ref), channel_id=1, source_target_pairs={{0,24},{8,0},{16,8},{24,16},{32,56},{40,32},{48,40},{56,48},{64,88... | collective-permute-start | bytes 1572872 | tf_op jit(solution)/shard_map/ppermute | solution.py:345
  119.0 13.8 %collective-permute-start.20 = (f32[512,256]{1,0:T(8,128)S(1)}, f32[512,256]{1,0:T(8,128)S(1)}, u32[]{:S(2)}, u32[]{:S(2)}) collective-permute-start(f32[512,256]{1,0:T(8,128)S(1)} %shard_map.102.khatri_ref), channel_id=1, source_target_pairs={{0,32},{8,40},{16,48},{24,56},{32,64},{40,72},{48,80},{56,88},{64,... | collective-permute-start | bytes 1572872 | tf_op jit(solution)/shard_map/ppermute | solution.py:345
  133.5 2.3 %collective-permute-start.23 = (f32[4,176,256]{2,1,0:T(8,128)S(1)}, f32[4,176,256]{2,1,0:T(8,128)S(1)}, u32[]{:S(2)}, u32[]{:S(2)}) collective-permute-start(f32[4,176,256]{2,1,0:T(8,128)S(1)} %shard_map.107.given_ref), channel_id=1, source_target_pairs={{0,1},{1,0},{2,3},{3,2},{4,5},{5,4},{6,7},{7,6},{8,9},{9,8},{10,11... | collective-permute-start | bytes 2162696 | tf_op jit(solution)/shard_map/ppermute | solution.py:358
  135.8 9.0 %collective-permute-start.24 = (f32[176,256]{1,0:T(8,128)S(1)}, f32[176,256]{1,0:T(8,128)S(1)}, u32[]{:S(2)}, u32[]{:S(2)}) collective-permute-start(f32[176,256]{1,0:T(8,128)S(1)} %get-tuple-element.156), channel_id=1, source_target_pairs={{0,4},{1,5},{2,6},{3,7},{4,0},{5,1},{6,2},{7,3},{8,12},{9,13},{10,... | collective-permute-start | bytes 540680 | tf_op jit(solution)/shard_map/ppermute | solution.py:368
  137.9 9.9 %collective-permute-start.25 = (f32[176,256]{1,0:T(8,128)S(1)}, f32[176,256]{1,0:T(8,128)S(1)}, u32[]{:S(2)}, u32[]{:S(2)}) collective-permute-start(f32[176,256]{1,0:T(8,128)S(1)} %get-tuple-element.157), channel_id=1, source_target_pairs={{0,2},{1,3},{2,4},{3,5},{4,6},{5,7},{6,0},{7,1},{8,10},{9,11},{10,... | collective-permute-start | bytes 540680 | tf_op jit(solution)/shard_map/ppermute | solution.py:368
  139.4 8.4 %collective-permute-start.26 = (f32[176,256]{1,0:T(8,128)S(1)}, f32[176,256]{1,0:T(8,128)S(1)}, u32[]{:S(2)}, u32[]{:S(2)}) collective-permute-start(f32[176,256]{1,0:T(8,128)S(1)} %get-tuple-element.158), channel_id=1, source_target_pairs={{0,6},{1,7},{2,0},{3,1},{4,2},{5,3},{6,4},{7,5},{8,14},{9,15},{10,... | collective-permute-start | bytes 540680 | tf_op jit(solution)/shard_map/ppermute | solution.py:368
  147.9 6.7 %collective-permute-start.27 = (f32[48,256]{1,0:T(8,128)S(1)}, f32[48,256]{1,0:T(8,128)S(1)}, u32[]{:S(2)}, u32[]{:S(2)}) collective-permute-start(f32[48,256]{1,0:T(8,128)S(1)} %get-tuple-element.159.refs_0_), channel_id=1, source_target_pairs={{0,2},{1,3},{2,4},{3,5},{4,6},{5,7},{6,0},{7,1},{8,10},{9,11},{10,... | collective-permute-start | bytes 147464 | tf_op jit(solution)/shard_map/ppermute | solution.py:331
  149.0 7.8 %collective-permute-start.28 = (f32[48,256]{1,0:T(8,128)S(1)}, f32[48,256]{1,0:T(8,128)S(1)}, u32[]{:S(2)}, u32[]{:S(2)}) collective-permute-start(f32[48,256]{1,0:T(8,128)S(1)} %get-tuple-element.159.refs_0_), channel_id=1, source_target_pairs={{0,4},{1,5},{2,6},{3,7},{4,0},{5,1},{6,2},{7,3},{8,12},{9,13},{10,... | collective-permute-start | bytes 147464 | tf_op jit(solution)/shard_map/ppermute | solution.py:331
  152.1 4.7 %collective-permute-start.29 = (f32[48,256]{1,0:T(8,128)S(1)}, f32[48,256]{1,0:T(8,128)S(1)}, u32[]{:S(2)}, u32[]{:S(2)}) collective-permute-start(f32[48,256]{1,0:T(8,128)S(1)} %get-tuple-element.159.refs_0_), channel_id=1, source_target_pairs={{0,6},{1,7},{2,0},{3,1},{4,2},{5,3},{6,4},{7,5},{8,14},{9,15},{10,... | collective-permute-start | bytes 147464 | tf_op jit(solution)/shard_map/ppermute | solution.py:331
  152.6 9.1 %collective-permute-start.30 = (f32[128,256]{1,0:T(8,128)S(1)}, f32[128,256]{1,0:T(8,128)S(1)}, u32[]{:S(2)}, u32[]{:S(2)}) collective-permute-start(f32[128,256]{1,0:T(8,128)S(1)} %get-tuple-element.164.refs_0_), channel_id=1, source_target_pairs={{0,2},{1,3},{2,4},{3,5},{4,6},{5,7},{6,0},{7,1},{8,10},{9,11},{10,... | collective-permute-start | bytes 393224 | tf_op jit(solution)/shard_map/ppermute | solution.py:331
  154.1 7.7 %collective-permute-start.31 = (f32[128,256]{1,0:T(8,128)S(1)}, f32[128,256]{1,0:T(8,128)S(1)}, u32[]{:S(2)}, u32[]{:S(2)}) collective-permute-start(f32[128,256]{1,0:T(8,128)S(1)} %get-tuple-element.164.refs_0_), channel_id=1, source_target_pairs={{0,4},{1,5},{2,6},{3,7},{4,0},{5,1},{6,2},{7,3},{8,12},{9,13},{10,... | collective-permute-start | bytes 393224 | tf_op jit(solution)/shard_map/ppermute | solution.py:331
  154.6 7.3 %collective-permute-start.32 = (f32[128,256]{1,0:T(8,128)S(1)}, f32[128,256]{1,0:T(8,128)S(1)}, u32[]{:S(2)}, u32[]{:S(2)}) collective-permute-start(f32[128,256]{1,0:T(8,128)S(1)} %get-tuple-element.164.refs_0_), channel_id=1, source_target_pairs={{0,6},{1,7},{2,0},{3,1},{4,2},{5,3},{6,4},{7,5},{8,14},{9,15},{10,... | collective-permute-start | bytes 393224 | tf_op jit(solution)/shard_map/ppermute | solution.py:331
  161.9 5.1 %collective-permute-start.33 = (f32[512,256]{1,0:T(8,128)S(1)}, f32[512,256]{1,0:T(8,128)S(1)}, u32[]{:S(2)}, u32[]{:S(2)}) collective-permute-start(f32[512,256]{1,0:T(8,128)S(1)} %shard_map.112.mine_ref), channel_id=1, source_target_pairs={{0,1},{1,0},{2,3},{3,2},{4,5},{5,4},{6,7},{7,6},{8,9},{9,8},{10,11... | collective-permute-start | bytes 1572872 | tf_op jit(solution)/shard_map/ppermute | solution.py:381

commit v2 on v1

--- a/solution.py
+++ b/solution.py
@@ -149,7 +149,7 @@
     got = got_ref[...]
     scale = column_scale(got_ref, 2 * CAP, height * got_ref.shape[0])
     scale_ref[...] = jnp.broadcast_to(scale, scale_ref.shape)
-    rows = placed_rows(index_ref, 0, got, height) / scale
+    rows = placed_rows(index_ref, 0, got, height) * (1.0 / scale)
     out_ref[...] = rows * placed_rows(index_ref, 1, got, height)
 
 
@@ -277,18 +277,22 @@
     return t(high, high) + (cross + cross.T)
 
 
+def half_of(ref, core):
+    rows = ref.shape[0] // 2
+    return ref[pl.ds(pl.multiple_of(core * rows, rows), rows), :]
+
+
 def piece_kernel(high_ref, low_ref, khatri_ref, *refs):
     so_far, (total_ref, gram_ref) = refs[:-2], refs[-2:]
+    _, core = position()
     khatri = halves(khatri_ref[...])
-    total, gram = three_dots(high_ref[...], low_ref[...], *khatri), gram_of(*khatri)
+    total = three_dots(half_of(high_ref, 1 - core), half_of(low_ref, 1 - core), *khatri)
+    gram = gram_of(*khatri)
     total_ref[...] = total + so_far[0][...] if so_far else total
     gram_ref[...] = gram + so_far[1][...] if so_far else gram
 
 
-def half_of(high_ref, low_ref, khatri, total_ref, core, out_ref):
-    rows = high_ref.shape[0] // 2
-    mine = pl.ds(pl.multiple_of(core * rows, rows), rows)
-    total = three_dots(high_ref[mine, :], low_ref[mine, :], *khatri) + total_ref[mine, :]
+def by_quarters(out_ref, total):
     for place in range(4):
         out_ref[place, :BLOCK, :] = total[place * BLOCK : (place + 1) * BLOCK]
 
@@ -296,7 +300,7 @@
 def given_kernel(high_ref, low_ref, khatri_ref, total_ref, gram_ref, out_ref):
     _, core = position()
     khatri = halves(khatri_ref[...])
-    half_of(high_ref, low_ref, khatri, total_ref, 1 - core, out_ref)
+    by_quarters(out_ref, three_dots(half_of(high_ref, 1 - core), half_of(low_ref, 1 - core), *khatri) + total_ref[...])
     gram = gram_of(*khatri) + gram_ref[...]
     h = gram.shape[0] // 2
     rows, few = h // 4, h // 8
@@ -308,9 +312,14 @@
         out_ref[place, BLOCK + rows :, h:] = gram[h // 2 + low : h // 2 + low + few, h:]
 
 
-def kept_kernel(high_ref, low_ref, khatri_ref, total_ref, given_ref, out_ref):
+def kept_kernel(*refs):
+    parts, pieces, (given_ref, out_ref) = refs[:8], refs[8:12], refs[12:]
     _, core = position()
-    half_of(high_ref, low_ref, halves(khatri_ref[...]), total_ref, core, out_ref)
+    total = None
+    for n, khatri_ref in enumerate(pieces):
+        part = three_dots(half_of(parts[2 * n], core), half_of(parts[2 * n + 1], core), *halves(khatri_ref[...]))
+        total = part if total is None else total + part
+    by_quarters(out_ref, total)
     out_ref[:, BLOCK:, :] = given_ref[:, BLOCK:, :]
 
 
@@ -347,8 +356,8 @@
     state = ()
     for n, beside in enumerate(LINES[:3]):
         high, low = parts[2 * n : 2 * n + 2]
-        out = (shape(rows, rank), shape(rank, rank))
-        state = call(piece_kernel, out, high, low, pieces[beside], *state, flops=flops, size=2**22)
+        out = (shape(rows // 2, rank), shape(rank, rank))
+        state = call(piece_kernel, out, high, low, pieces[beside], *state, flops=flops // 2, size=2**21)
         if n == 0:
             state, extra = lax.optimization_barrier((state, aside(piece)))
     total, gram = state
@@ -356,15 +365,14 @@
     out = shape(4, BLOCK + 3 * rank // 16, rank)
     given = call(given_kernel, out, high, low, pieces[2], total, gram, flops=flops, size=2**21)
     got = lax.ppermute(given, "samp", CORE)
-    kept = call(kept_kernel, out, high, low, pieces[2], total, given, flops=flops // 2, size=2**21)
+    kept = call(kept_kernel, out, *parts, *[pieces[beside] for beside in LINES], given, flops=2 * flops, size=2**23)
     return kept, got, extra
 
 
 def summed(fibres, block, aside):
     rank = block.shape[1]
     kept, got, extra = sums_over_row_group(fibres, block, aside)
-    rows = kept.shape[1]
-    pairs = call(pair_kernel, (shape(rows, rank),) * 4, kept, got, size=2**21)
+    pairs = call(pair_kernel, (shape(*kept.shape[1:]),) * 4, kept, got, size=2**21)
     parts = [pairs[0]] + [lax.ppermute(pairs[step], "samp", along_z(step)) for step in FAR_FIRST]
     product, gram = call(quarter_kernel, (shape(BLOCK, rank), shape(3 * rank // 16, rank)), *parts, size=2**20)
     h = rank // 2
@@ -414,8 +422,8 @@
 
 def finish_kernel(solved_ref, got_ref, out_ref, scale_ref):
     scale = column_scale(got_ref, 0, solved_ref.shape[0] * got_ref.shape[0])
-    scale_ref[...] = jnp.broadcast_to(scale, scale_ref.shape)
-    out_ref[...] = solved_ref[...] / scale
+    scale_ref[...] = scale
+    out_ref[...] = solved_ref[...] * (1.0 / scale)
 
 
 def exchange(rows):
@@ -470,8 +478,8 @@
         flops=10**9,
         size=2**21,
     )
-    factor_b_new, weights = call(finish_kernel, (shape(height, rank), shape(8, rank)), solved, exchange(sent), size=2**21)
-    return (factor_a, factor_b_new, weights[0])
+    factor_b_new, weights = call(finish_kernel, (shape(height, rank), shape(1, rank)), solved, exchange(sent), size=2**21)
+    return (factor_a, factor_b_new, weights.reshape(rank))
 
 
 def solution(mesh):

time: 180 us -> 180 us (level)
  waiting for transfers between devices: 32.4 us -> 40.7 us
  starting transfers between devices: 51.7 us -> 44.9 us
    ppermute x6, waiting for transfers between devices: 9.5 us -> 13.9 us  [sums_over_row_group(): lax.ppermute(block, 'row', in_plane(step, 2 * step))]
    ppermute x12, waiting for transfers between devices: 0.08 us -> 3.35 us  [from_z(): got = {step: lax.ppermute(own, 'samp', along_z(step)) for step in FAR_FIRST}]
    ppermute x6, waiting for transfers between devices: 6.73 us -> 9.45 us  [sums_over_row_group(): lax.ppermute(piece, 'row', in_plane(*move))]
    ppermute x2, waiting for transfers between devices: 3.18 us -> 0.75 us  [sums_over_row_group(): got = lax.ppermute(given, 'samp', CORE)]
    ppermute x6, starting transfers between devices: 9.04 us -> 6.62 us  [sums_over_row_group(): lax.ppermute(piece, 'row', in_plane(*move))]
    ppermute x6, starting transfers between devices: 12 us -> 9.59 us  [sums_over_row_group(): lax.ppermute(block, 'row', in_plane(step, 2 * step))]
    ppermute x12, starting transfers between devices: 17.8 us -> 16 us  [from_z(): got = {step: lax.ppermute(own, 'samp', along_z(step)) for step in FAR_FIRST}]
  transfers between devices with their start and end apart: 34 -> 34, of which waited for: 15 -> 23; matrix products, arithmetic and copies ran while one was open for 1% -> 1% of each run, Pallas kernels for 20% -> 20%
where the time goes in v2:
time: 180 us
  blocking collectives  46.3 us (26%)
  Pallas kernels  45.6 us (25%)
  starting transfers between devices  44.9 us (25%)
  waiting for transfers between devices  40.7 us (23%)
    all_to_all x3, blocking collectives, exchange(): return lax.all_to_all(rows, 'row', 0, 0, tiled=True)  46.3 us
    pallas_call x31, Pallas kernels, call(): pl.pallas_call(kernel, out_shape=out, in_specs=specs or [VMEM] * len(args...  45.6 us
    ppermute x12, starting transfers between devices, from_z(): got = {step: lax.ppermute(own, 'samp', along_z(step)) for step in FAR_FIRST}  16 us
    ppermute x6, waiting for transfers between devices, sums_over_row_group(): lax.ppermute(block, 'row', in_plane(step, 2 * step))  13.9 us
    ppermute x6, waiting for transfers between devices, summed(): lax.ppermute(pairs[step], 'samp', along_z(step))  13.3 us
    ppermute x6, starting transfers between devices, summed(): lax.ppermute(pairs[step], 'samp', along_z(step))  12.2 us
    ppermute x6, starting transfers between devices, sums_over_row_group(): lax.ppermute(block, 'row', in_plane(step, 2 * step))  9.59 us
    ppermute x6, waiting for transfers between devices, sums_over_row_group(): lax.ppermute(piece, 'row', in_plane(*move))  9.45 us
  transfers between devices with their start and end apart: 34, of which 23 were waited for; matrix products, arithmetic and copies ran while one was open for 1% of the time, Pallas kernels for 20%

profile of v2, /device:TPU:0, one launch (start us, length us, event | category | flops | bytes accessed | tf_op | source)
XLA Modules:
  0.0 179.7 jit_solution(4406223761922093933)
XLA Ops:
  0.7 2.7 %shard_map.85 = (f32[16,32,256]{2,1,0:T(8,128)S(1)}, s32[2,2048]{1,0:T(2,128)S(1)}) custom-call(s32[2,2048]{1,0:T(2,128)} %bitcast.7, f32[1024,256]{1,0:T(8,128)} %b_hbm.1, f32[1024,256]{1,0:T(8,128)} %c_ref), custom_call_target="tpu_custom_call" | custom-call | flops 1000000000 | bytes 2097152 | tf_op jit(solution)/shard_map/pallas_call | solution.py:26
  3.4 18.5 %all_to_all.15.refs_1_ = f32[16,32,256]{2,1,0:T(8,128)S(1)} all-to-all(f32[16,32,256]{2,1,0:T(8,128)S(1)} %get-tuple-element.90), channel_id=1, replica_groups=mesh['row'=16,'samp'=8] {'row'}, dimensions={0} | all-to-all | bytes 1048576 | tf_op jit(solution)/shard_map/all_to_all | solution.py:430
  22.3 1.4 collective-permute-start.2
  23.8 1.6 collective-permute-start.1
  25.4 1.7 collective-permute-start
  27.1 3.9 %collective-permute-done.2.refs_3_ = f32[128,256]{1,0:T(8,128)S(1)} collective-permute-done((f32[128,256]{1,0:T(8,128)S(1)}, f32[128,256]{1,0:T(8,128)S(1)}, u32[]{:S(2)}, u32[]{:S(2)}) %collective-permute-start.2) | collective-permute-done | bytes 131104 | tf_op jit(solution)/shard_map/ppermute | solution.py:349
  31.6 2.3 %collective-permute-done.refs_1_ = f32[128,256]{1,0:T(8,128)S(1)} collective-permute-done((f32[128,256]{1,0:T(8,128)S(1)}, f32[128,256]{1,0:T(8,128)S(1)}, u32[]{:S(2)}, u32[]{:S(2)}) %collective-permute-start) | collective-permute-done | bytes 131104 | tf_op jit(solution)/shard_map/ppermute | solution.py:349
  34.5 2.8 %collective-permute-start.4 = (f32[512,256]{1,0:T(8,128)S(1)}, f32[512,256]{1,0:T(8,128)S(1)}, u32[]{:S(2)}, u32[]{:S(2)}) collective-permute-start(f32[512,256]{1,0:T(8,128)S(1)} %shard_map.87.khatri_ref.refs_8_), channel_id=1, source_target_pairs={{0,24},{8,0},{16,8},{24,16},{32,56},{40,32},{48,40},{56,48},{64,88... | collective-permute-start | bytes 1572872 | tf_op jit(solution)/shard_map/ppermute | solution.py:354
  37.3 3.9 %shard_map.88 = (bf16[1024,512]{1,0:T(8,128)(2,1)S(1)}, bf16[1024,512]{1,0:T(8,128)(2,1)S(1)}, bf16[1024,512]{1,0:T(8,128)(2,1)S(1)}, bf16[1024,512]{1,0:T(8,128...) custom-call(f32[1024,2048]{1,0:T(8,128)} %fibres_ref), custom_call_target="tpu_custom_call" | custom-call | flops 8388608 | bytes 16777216 | tf_op jit(solution)/shard_map/pallas_call | solution.py:26
  42.8 3.2 %collective-permute-done.3.khatri_ref.refs_9_ = f32[512,256]{1,0:T(8,128)S(1)} collective-permute-done((f32[512,256]{1,0:T(8,128)S(1)}, f32[512,256]{1,0:T(8,128)S(1)}, u32[]{:S(2)}, u32[]{:S(2)}) %collective-permute-start.3) | collective-permute-done | bytes 524320 | tf_op jit(solution)/shard_map/ppermute | solution.py:354
  47.5 1.2 collective-permute-done.5.khatri_ref.refs_11_
  49.5 1.8 shard_map.94.kept_ref
  51.8 4.0 %collective-permute-start.7 = (f32[176,256]{1,0:T(8,128)S(1)}, f32[176,256]{1,0:T(8,128)S(1)}, u32[]{:S(2)}, u32[]{:S(2)}) collective-permute-start(f32[176,256]{1,0:T(8,128)S(1)} %get-tuple-element.114), channel_id=1, source_target_pairs={{0,4},{1,5},{2,6},{3,7},{4,0},{5,1},{6,2},{7,3},{8,12},{9,13},{10,... | collective-permute-start | bytes 540680 | tf_op jit(solution)/shard_map/ppermute | solution.py:376
  55.8 1.0 collective-permute-start.8
  56.8 2.2 %collective-permute-start.9 = (f32[176,256]{1,0:T(8,128)S(1)}, f32[176,256]{1,0:T(8,128)S(1)}, u32[]{:S(2)}, u32[]{:S(2)}) collective-permute-start(f32[176,256]{1,0:T(8,128)S(1)} %get-tuple-element.116), channel_id=1, source_target_pairs={{0,6},{1,7},{2,0},{3,1},{4,2},{5,3},{6,4},{7,5},{8,14},{9,15},{10,... | collective-permute-start | bytes 540680 | tf_op jit(solution)/shard_map/ppermute | solution.py:376
  59.0 2.1 %collective-permute-done.7.b = f32[176,256]{1,0:T(8,128)S(1)} collective-permute-done((f32[176,256]{1,0:T(8,128)S(1)}, f32[176,256]{1,0:T(8,128)S(1)}, u32[]{:S(2)}, u32[]{:S(2)}) %collective-permute-start.7) | collective-permute-done | bytes 180256 | tf_op jit(solution)/shard_map/ppermute | solution.py:376
  61.1 3.4 %collective-permute-done.8.c = f32[176,256]{1,0:T(8,128)S(1)} collective-permute-done((f32[176,256]{1,0:T(8,128)S(1)}, f32[176,256]{1,0:T(8,128)S(1)}, u32[]{:S(2)}, u32[]{:S(2)}) %collective-permute-start.8) | collective-permute-done | bytes 180256 | tf_op jit(solution)/shard_map/ppermute | solution.py:376
  65.3 2.7 %collective-permute-start.12 = (f32[48,256]{1,0:T(8,128)S(1)}, f32[48,256]{1,0:T(8,128)S(1)}, u32[]{:S(2)}, u32[]{:S(2)}) collective-permute-start(f32[48,256]{1,0:T(8,128)S(1)} %get-tuple-element.117.refs_0_), channel_id=1, source_target_pairs={{0,6},{1,7},{2,0},{3,1},{4,2},{5,3},{6,4},{7,5},{8,14},{9,15},{10,... | collective-permute-start | bytes 147464 | tf_op jit(solution)/shard_map/ppermute | solution.py:340
  69.1 2.6 %collective-permute-start.15 = (f32[128,256]{1,0:T(8,128)S(1)}, f32[128,256]{1,0:T(8,128)S(1)}, u32[]{:S(2)}, u32[]{:S(2)}) collective-permute-start(f32[128,256]{1,0:T(8,128)S(1)} %get-tuple-element.122.refs_0_), channel_id=1, source_target_pairs={{0,6},{1,7},{2,0},{3,1},{4,2},{5,3},{6,4},{7,5},{8,14},{9,15},{10,... | collective-permute-start | bytes 393224 | tf_op jit(solution)/shard_map/ppermute | solution.py:340
  71.7 1.9 %collective-permute-start.14 = (f32[128,256]{1,0:T(8,128)S(1)}, f32[128,256]{1,0:T(8,128)S(1)}, u32[]{:S(2)}, u32[]{:S(2)}) collective-permute-start(f32[128,256]{1,0:T(8,128)S(1)} %get-tuple-element.122.refs_0_), channel_id=1, source_target_pairs={{0,4},{1,5},{2,6},{3,7},{4,0},{5,1},{6,2},{7,3},{8,12},{9,13},{10,... | collective-permute-start | bytes 393224 | tf_op jit(solution)/shard_map/ppermute | solution.py:340
  74.1 5.0 %shard_map.97 = (f32[128,128]{1,0:T(8,128)S(1)}, f32[128,128]{1,0:T(8,128)S(1)}, f32[128,128]{1,0:T(8,128)S(1)}) custom-call(f32[48,256]{1,0:T(8,128)S(1)} %get-tuple-element.117.refs_0_, f32[48,256]{1,0:T(8,128)S(1)} %collective-permute-done.10.refs_1_, f32[48,256]{1,0:T(8,128)S(1)} %collective-permute-done.11.refs_2_, ...), custom_call_target="tpu_custom_call" | custom-call | flops 99999997952 | bytes 524288 | tf_op jit(solution)/shard_map/pallas_call | solution.py:26
  80.2 5.0 %shard_map.99.inverse_ref = f32[256,256]{1,0:T(8,128)S(1)} custom-call(f32[128,128]{1,0:T(8,128)S(1)} %get-tuple-element.126.a_ref, f32[128,128]{1,0:T(8,128)S(1)} %get-tuple-element.127.w_ref, f32[128,128]{1,0:T(8,128)S(1)} %get-tuple-element.128.rest_ref), custom_call_target="tpu_custom_call" | custom-call | flops 99999997952 | bytes 524288 | tf_op jit(solution)/shard_map/pallas_call | solution.py:26
  85.2 1.8 shard_map.100
  86.9 17.0 %all_to_all.16.refs_1_ = f32[16,40,256]{2,1,0:T(8,128)S(1)} all-to-all(f32[16,40,256]{2,1,0:T(8,128)S(1)} %get-tuple-element.131), channel_id=1, replica_groups=mesh['row'=16,'samp'=8] {'row'}, dimensions={0} | all-to-all | bytes 1310720 | tf_op jit(solution)/shard_map/all_to_all | solution.py:430
  104.4 1.9 %collective-permute-start.19 = (f32[128,256]{1,0:T(8,128)S(1)}, f32[128,256]{1,0:T(8,128)S(1)}, u32[]{:S(2)}, u32[]{:S(2)}) collective-permute-start(f32[128,256]{1,0:T(8,128)S(1)} %get-tuple-element.132.refs_0_), channel_id=1, source_target_pairs={{0,112},{8,120},{16,96},{24,104},{32,16},{40,24},{48,0},{56,8},{64... | collective-permute-start | bytes 393224 | tf_op jit(solution)/shard_map/ppermute | solution.py:349
  106.3 1.5 collective-permute-start.18
  107.8 1.5 collective-permute-start.17
  109.3 2.9 %collective-permute-done.19.refs_3_ = f32[128,256]{1,0:T(8,128)S(1)} collective-permute-done((f32[128,256]{1,0:T(8,128)S(1)}, f32[128,256]{1,0:T(8,128)S(1)}, u32[]{:S(2)}, u32[]{:S(2)}) %collective-permute-start.19) | collective-permute-done | bytes 131104 | tf_op jit(solution)/shard_map/ppermute | solution.py:349
  112.8 3.6 %collective-permute-done.17.refs_1_ = f32[128,256]{1,0:T(8,128)S(1)} collective-permute-done((f32[128,256]{1,0:T(8,128)S(1)}, f32[128,256]{1,0:T(8,128)S(1)}, u32[]{:S(2)}, u32[]{:S(2)}) %collective-permute-start.17) | collective-permute-done | bytes 131104 | tf_op jit(solution)/shard_map/ppermute | solution.py:349
  117.1 2.6 %collective-permute-start.21 = (f32[512,256]{1,0:T(8,128)S(1)}, f32[512,256]{1,0:T(8,128)S(1)}, u32[]{:S(2)}, u32[]{:S(2)}) collective-permute-start(f32[512,256]{1,0:T(8,128)S(1)} %shard_map.102.khatri_ref.refs_8_), channel_id=1, source_target_pairs={{0,24},{8,0},{16,8},{24,16},{32,56},{40,32},{48,40},{56,48},{64,88... | collective-permute-start | bytes 1572872 | tf_op jit(solution)/shard_map/ppermute | solution.py:354
  119.7 3.9 %shard_map.103 = (bf16[1024,512]{1,0:T(8,128)(2,1)S(1)}, bf16[1024,512]{1,0:T(8,128)(2,1)S(1)}, bf16[1024,512]{1,0:T(8,128)(2,1)S(1)}, bf16[1024,512]{1,0:T(8,12...) custom-call(f32[1024,2048]{1,0:T(8,128)} %fibres_ref.1), custom_call_target="tpu_custom_call" | custom-call | flops 8388608 | bytes 16777216 | tf_op jit(solution)/shard_map/pallas_call | solution.py:26
  124.4 1.0 broadcast_divide_fusion
  125.4 3.8 %collective-permute-done.20.khatri_ref.refs_9_ = f32[512,256]{1,0:T(8,128)S(1)} collective-permute-done((f32[512,256]{1,0:T(8,128)S(1)}, f32[512,256]{1,0:T(8,128)S(1)}, u32[]{:S(2)}, u32[]{:S(2)}) %collective-permute-start.20) | collective-permute-done | bytes 524320 | tf_op jit(solution)/shard_map/ppermute | solution.py:354
  130.7 1.2 collective-permute-done.22.khatri_ref.refs_11_
  132.9 1.8 shard_map.108.kept_ref
  135.2 1.8 collective-permute-start.24
  136.9 0.9 collective-permute-start.25
  137.9 2.3 %collective-permute-start.26 = (f32[176,256]{1,0:T(8,128)S(1)}, f32[176,256]{1,0:T(8,128)S(1)}, u32[]{:S(2)}, u32[]{:S(2)}) collective-permute-start(f32[176,256]{1,0:T(8,128)S(1)} %get-tuple-element.158), channel_id=1, source_target_pairs={{0,6},{1,7},{2,0},{3,1},{4,2},{5,3},{6,4},{7,5},{8,14},{9,15},{10,... | collective-permute-start | bytes 540680 | tf_op jit(solution)/shard_map/ppermute | solution.py:376
  140.2 4.0 %collective-permute-done.24.b = f32[176,256]{1,0:T(8,128)S(1)} collective-permute-done((f32[176,256]{1,0:T(8,128)S(1)}, f32[176,256]{1,0:T(8,128)S(1)}, u32[]{:S(2)}, u32[]{:S(2)}) %collective-permute-start.24) | collective-permute-done | bytes 180256 | tf_op jit(solution)/shard_map/ppermute | solution.py:376
  144.2 3.0 %collective-permute-done.25.c = f32[176,256]{1,0:T(8,128)S(1)} collective-permute-done((f32[176,256]{1,0:T(8,128)S(1)}, f32[176,256]{1,0:T(8,128)S(1)}, u32[]{:S(2)}, u32[]{:S(2)}) %collective-permute-start.25) | collective-permute-done | bytes 180256 | tf_op jit(solution)/shard_map/ppermute | solution.py:376
  147.3 1.8 %collective-permute-start.29 = (f32[48,256]{1,0:T(8,128)S(1)}, f32[48,256]{1,0:T(8,128)S(1)}, u32[]{:S(2)}, u32[]{:S(2)}) collective-permute-start(f32[48,256]{1,0:T(8,128)S(1)} %get-tuple-element.159.refs_0_), channel_id=1, source_target_pairs={{0,6},{1,7},{2,0},{3,1},{4,2},{5,3},{6,4},{7,5},{8,14},{9,15},{10,... | collective-permute-start | bytes 147464 | tf_op jit(solution)/shard_map/ppermute | solution.py:340
  150.4 2.7 %collective-permute-start.32 = (f32[128,256]{1,0:T(8,128)S(1)}, f32[128,256]{1,0:T(8,128)S(1)}, u32[]{:S(2)}, u32[]{:S(2)}) collective-permute-start(f32[128,256]{1,0:T(8,128)S(1)} %get-tuple-element.164.refs_0_), channel_id=1, source_target_pairs={{0,6},{1,7},{2,0},{3,1},{4,2},{5,3},{6,4},{7,5},{8,14},{9,15},{10,... | collective-permute-start | bytes 393224 | tf_op jit(solution)/shard_map/ppermute | solution.py:340
  153.2 1.5 collective-permute-start.31
  155.2 5.0 %shard_map.111 = (f32[128,128]{1,0:T(8,128)S(1)}, f32[128,128]{1,0:T(8,128)S(1)}, f32[128,128]{1,0:T(8,128)S(1)}) custom-call(f32[48,256]{1,0:T(8,128)S(1)} %get-tuple-element.159.refs_0_, f32[48,256]{1,0:T(8,128)S(1)} %collective-permute-done.27.refs_1_, f32[48,256]{1,0:T(8,128)S(1)} %collective-permute-done.28.refs_2_, ...), custom_call_target="tpu_custom_call" | custom-call | flops 99999997952 | bytes 524288 | tf_op jit(solution)/shard_map/pallas_call | solution.py:26
  160.4 1.3 collective-permute-done.30.refs_1_
  161.9 5.0 %shard_map.113.inverse_ref = f32[256,256]{1,0:T(8,128)S(1)} custom-call(f32[128,128]{1,0:T(8,128)S(1)} %get-tuple-element.168.a_ref, f32[128,128]{1,0:T(8,128)S(1)} %get-tuple-element.169.w_ref, f32[128,128]{1,0:T(8,128)S(1)} %get-tuple-element.170.rest_ref), custom_call_target="tpu_custom_call" | custom-call | flops 99999997952 | bytes 524288 | tf_op jit(solution)/shard_map/pallas_call | solution.py:26
  167.7 10.9 %all_to_all.17.got_ref = f32[16,1,256]{2,1,0:T(1,128)S(1)} all-to-all(f32[16,1,256]{2,1,0:T(1,128)S(1)} %get-tuple-element.172), channel_id=1, replica_groups=mesh['row'=16,'samp'=8] {'row'}, dimensions={0} | all-to-all | bytes 32768 | tf_op jit(solution)/shard_map/all_to_all | solution.py:430
  178.6 1.1 shard_map.115
  (62 shorter events, 18.2 us)
Async XLA Ops:
  0.6 41.3 %copy-start = (s32[2048,2]{0,1:T(2,128)S(1)}, s32[2048,2]{0,1:T(2,128)}, u32[]{:S(2)}) copy-start(s32[2048,2]{0,1:T(2,128)} %param.9) | copy-start | bytes 49156
  0.6 41.3 %copy-start.2 = (f32[1024,256]{1,0:T(8,128)S(1)}, f32[1024,256]{1,0:T(8,128)}, u32[]{:S(2)}) copy-start(f32[1024,256]{1,0:T(8,128)} %c_ref) | copy-start | bytes 3145732
  22.3 8.6 %collective-permute-start.2 = (f32[128,256]{1,0:T(8,128)S(1)}, f32[128,256]{1,0:T(8,128)S(1)}, u32[]{:S(2)}, u32[]{:S(2)}) collective-permute-start(f32[128,256]{1,0:T(8,128)S(1)} %shard_map.86.refs_0_), channel_id=1, source_target_pairs={{0,112},{8,120},{16,96},{24,104},{32,16},{40,24},{48,0},{56,8},{64... | collective-permute-start | bytes 393224 | tf_op jit(solution)/shard_map/ppermute | solution.py:349
  23.8 7.9 %collective-permute-start.1 = (f32[128,256]{1,0:T(8,128)S(1)}, f32[128,256]{1,0:T(8,128)S(1)}, u32[]{:S(2)}, u32[]{:S(2)}) collective-permute-start(f32[128,256]{1,0:T(8,128)S(1)} %shard_map.86.refs_0_), channel_id=1, source_target_pairs={{0,64},{8,72},{16,80},{24,88},{32,96},{40,104},{48,112},{56,120},{... | collective-permute-start | bytes 393224 | tf_op jit(solution)/shard_map/ppermute | solution.py:349
  25.4 8.6 %collective-permute-start = (f32[128,256]{1,0:T(8,128)S(1)}, f32[128,256]{1,0:T(8,128)S(1)}, u32[]{:S(2)}, u32[]{:S(2)}) collective-permute-start(f32[128,256]{1,0:T(8,128)S(1)} %shard_map.86.refs_0_), channel_id=1, source_target_pairs={{0,48},{8,56},{16,32},{24,40},{32,80},{40,88},{48,64},{56,72},{64,... | collective-permute-start | bytes 393224 | tf_op jit(solution)/shard_map/ppermute | solution.py:349
  34.0 12.1 %collective-permute-start.3 = (f32[512,256]{1,0:T(8,128)S(1)}, f32[512,256]{1,0:T(8,128)S(1)}, u32[]{:S(2)}, u32[]{:S(2)}) collective-permute-start(f32[512,256]{1,0:T(8,128)S(1)} %shard_map.87.khatri_ref.refs_8_), channel_id=1, source_target_pairs={{0,8},{8,16},{16,24},{24,0},{32,40},{40,48},{48,56},{56,32},{64,72... | collective-permute-start | bytes 1572872 | tf_op jit(solution)/shard_map/ppermute | solution.py:354
  34.5 12.2 %collective-permute-start.4 = (f32[512,256]{1,0:T(8,128)S(1)}, f32[512,256]{1,0:T(8,128)S(1)}, u32[]{:S(2)}, u32[]{:S(2)}) collective-permute-start(f32[512,256]{1,0:T(8,128)S(1)} %shard_map.87.khatri_ref.refs_8_), channel_id=1, source_target_pairs={{0,24},{8,0},{16,8},{24,16},{32,56},{40,32},{48,40},{56,48},{64,88... | collective-permute-start | bytes 1572872 | tf_op jit(solution)/shard_map/ppermute | solution.py:354
  37.3 11.4 %collective-permute-start.5 = (f32[512,256]{1,0:T(8,128)S(1)}, f32[512,256]{1,0:T(8,128)S(1)}, u32[]{:S(2)}, u32[]{:S(2)}) collective-permute-start(f32[512,256]{1,0:T(8,128)S(1)} %shard_map.87.khatri_ref.refs_8_), channel_id=1, source_target_pairs={{0,32},{8,40},{16,48},{24,56},{32,64},{40,72},{48,80},{56,88},{64,... | collective-permute-start | bytes 1572872 | tf_op jit(solution)/shard_map/ppermute | solution.py:354
  49.5 2.3 %collective-permute-start.6 = (f32[4,176,256]{2,1,0:T(8,128)S(1)}, f32[4,176,256]{2,1,0:T(8,128)S(1)}, u32[]{:S(2)}, u32[]{:S(2)}) collective-permute-start(f32[4,176,256]{2,1,0:T(8,128)S(1)} %shard_map.93.refs_12_), channel_id=1, source_target_pairs={{0,1},{1,0},{2,3},{3,2},{4,5},{5,4},{6,7},{7,6},{8,9},{9,8},{10,11... | collective-permute-start | bytes 2162696 | tf_op jit(solution)/shard_map/ppermute | solution.py:367
  51.8 9.3 %collective-permute-start.7 = (f32[176,256]{1,0:T(8,128)S(1)}, f32[176,256]{1,0:T(8,128)S(1)}, u32[]{:S(2)}, u32[]{:S(2)}) collective-permute-start(f32[176,256]{1,0:T(8,128)S(1)} %get-tuple-element.114), channel_id=1, source_target_pairs={{0,4},{1,5},{2,6},{3,7},{4,0},{5,1},{6,2},{7,3},{8,12},{9,13},{10,... | collective-permute-start | bytes 540680 | tf_op jit(solution)/shard_map/ppermute | solution.py:376
  55.8 8.7 %collective-permute-start.8 = (f32[176,256]{1,0:T(8,128)S(1)}, f32[176,256]{1,0:T(8,128)S(1)}, u32[]{:S(2)}, u32[]{:S(2)}) collective-permute-start(f32[176,256]{1,0:T(8,128)S(1)} %get-tuple-element.115), channel_id=1, source_target_pairs={{0,2},{1,3},{2,4},{3,5},{4,6},{5,7},{6,0},{7,1},{8,10},{9,11},{10,... | collective-permute-start | bytes 540680 | tf_op jit(solution)/shard_map/ppermute | solution.py:376
  56.8 8.4 %collective-permute-start.9 = (f32[176,256]{1,0:T(8,128)S(1)}, f32[176,256]{1,0:T(8,128)S(1)}, u32[]{:S(2)}, u32[]{:S(2)}) collective-permute-start(f32[176,256]{1,0:T(8,128)S(1)} %get-tuple-element.116), channel_id=1, source_target_pairs={{0,6},{1,7},{2,0},{3,1},{4,2},{5,3},{6,4},{7,5},{8,14},{9,15},{10,... | collective-permute-start | bytes 540680 | tf_op jit(solution)/shard_map/ppermute | solution.py:376
  65.3 8.3 %collective-permute-start.12 = (f32[48,256]{1,0:T(8,128)S(1)}, f32[48,256]{1,0:T(8,128)S(1)}, u32[]{:S(2)}, u32[]{:S(2)}) collective-permute-start(f32[48,256]{1,0:T(8,128)S(1)} %get-tuple-element.117.refs_0_), channel_id=1, source_target_pairs={{0,6},{1,7},{2,0},{3,1},{4,2},{5,3},{6,4},{7,5},{8,14},{9,15},{10,... | collective-permute-start | bytes 147464 | tf_op jit(solution)/shard_map/ppermute | solution.py:340
  68.0 5.6 %collective-permute-start.11 = (f32[48,256]{1,0:T(8,128)S(1)}, f32[48,256]{1,0:T(8,128)S(1)}, u32[]{:S(2)}, u32[]{:S(2)}) collective-permute-start(f32[48,256]{1,0:T(8,128)S(1)} %get-tuple-element.117.refs_0_), channel_id=1, source_target_pairs={{0,4},{1,5},{2,6},{3,7},{4,0},{5,1},{6,2},{7,3},{8,12},{9,13},{10,... | collective-permute-start | bytes 147464 | tf_op jit(solution)/shard_map/ppermute | solution.py:340
  68.5 5.7 %collective-permute-start.10 = (f32[48,256]{1,0:T(8,128)S(1)}, f32[48,256]{1,0:T(8,128)S(1)}, u32[]{:S(2)}, u32[]{:S(2)}) collective-permute-start(f32[48,256]{1,0:T(8,128)S(1)} %get-tuple-element.117.refs_0_), channel_id=1, source_target_pairs={{0,2},{1,3},{2,4},{3,5},{4,6},{5,7},{6,0},{7,1},{8,10},{9,11},{10,... | collective-permute-start | bytes 147464 | tf_op jit(solution)/shard_map/ppermute | solution.py:340
  69.1 10.0 %collective-permute-start.15 = (f32[128,256]{1,0:T(8,128)S(1)}, f32[128,256]{1,0:T(8,128)S(1)}, u32[]{:S(2)}, u32[]{:S(2)}) collective-permute-start(f32[128,256]{1,0:T(8,128)S(1)} %get-tuple-element.122.refs_0_), channel_id=1, source_target_pairs={{0,6},{1,7},{2,0},{3,1},{4,2},{5,3},{6,4},{7,5},{8,14},{9,15},{10,... | collective-permute-start | bytes 393224 | tf_op jit(solution)/shard_map/ppermute | solution.py:340
  71.7 7.4 %collective-permute-start.14 = (f32[128,256]{1,0:T(8,128)S(1)}, f32[128,256]{1,0:T(8,128)S(1)}, u32[]{:S(2)}, u32[]{:S(2)}) collective-permute-start(f32[128,256]{1,0:T(8,128)S(1)} %get-tuple-element.122.refs_0_), channel_id=1, source_target_pairs={{0,4},{1,5},{2,6},{3,7},{4,0},{5,1},{6,2},{7,3},{8,12},{9,13},{10,... | collective-permute-start | bytes 393224 | tf_op jit(solution)/shard_map/ppermute | solution.py:340
  73.6 6.5 %collective-permute-start.13 = (f32[128,256]{1,0:T(8,128)S(1)}, f32[128,256]{1,0:T(8,128)S(1)}, u32[]{:S(2)}, u32[]{:S(2)}) collective-permute-start(f32[128,256]{1,0:T(8,128)S(1)} %get-tuple-element.122.refs_0_), channel_id=1, source_target_pairs={{0,2},{1,3},{2,4},{3,5},{4,6},{5,7},{6,0},{7,1},{8,10},{9,11},{10,... | collective-permute-start | bytes 393224 | tf_op jit(solution)/shard_map/ppermute | solution.py:340
  80.1 23.8 %copy-start.1 = (s32[2048,2]{0,1:T(2,128)S(1)}, s32[2048,2]{0,1:T(2,128)}, u32[]{:S(2)}) copy-start(s32[2048,2]{0,1:T(2,128)} %param.9) | copy-start | bytes 49156
  80.1 5.1 %collective-permute-start.16 = (f32[512,256]{1,0:T(8,128)S(1)}, f32[512,256]{1,0:T(8,128)S(1)}, u32[]{:S(2)}, u32[]{:S(2)}) collective-permute-start(f32[512,256]{1,0:T(8,128)S(1)} %shard_map.98.mine_ref), channel_id=1, source_target_pairs={{0,1},{1,0},{2,3},{3,2},{4,5},{5,4},{6,7},{7,6},{8,9},{9,8},{10,11... | collective-permute-start | bytes 1572872 | tf_op jit(solution)/shard_map/ppermute | solution.py:389
  104.4 7.7 %collective-permute-start.19 = (f32[128,256]{1,0:T(8,128)S(1)}, f32[128,256]{1,0:T(8,128)S(1)}, u32[]{:S(2)}, u32[]{:S(2)}) collective-permute-start(f32[128,256]{1,0:T(8,128)S(1)} %get-tuple-element.132.refs_0_), channel_id=1, source_target_pairs={{0,112},{8,120},{16,96},{24,104},{32,16},{40,24},{48,0},{56,8},{64... | collective-permute-start | bytes 393224 | tf_op jit(solution)/shard_map/ppermute | solution.py:349
  106.3 6.5 %collective-permute-start.18 = (f32[128,256]{1,0:T(8,128)S(1)}, f32[128,256]{1,0:T(8,128)S(1)}, u32[]{:S(2)}, u32[]{:S(2)}) collective-permute-start(f32[128,256]{1,0:T(8,128)S(1)} %get-tuple-element.132.refs_0_), channel_id=1, source_target_pairs={{0,64},{8,72},{16,80},{24,88},{32,96},{40,104},{48,112},{56,120},{... | collective-permute-start | bytes 393224 | tf_op jit(solution)/shard_map/ppermute | solution.py:349
  107.8 8.6 %collective-permute-start.17 = (f32[128,256]{1,0:T(8,128)S(1)}, f32[128,256]{1,0:T(8,128)S(1)}, u32[]{:S(2)}, u32[]{:S(2)}) collective-permute-start(f32[128,256]{1,0:T(8,128)S(1)} %get-tuple-element.132.refs_0_), channel_id=1, source_target_pairs={{0,48},{8,56},{16,32},{24,40},{32,80},{40,88},{48,64},{56,72},{64,... | collective-permute-start | bytes 393224 | tf_op jit(solution)/shard_map/ppermute | solution.py:349
  116.4 12.8 %collective-permute-start.20 = (f32[512,256]{1,0:T(8,128)S(1)}, f32[512,256]{1,0:T(8,128)S(1)}, u32[]{:S(2)}, u32[]{:S(2)}) collective-permute-start(f32[512,256]{1,0:T(8,128)S(1)} %shard_map.102.khatri_ref.refs_8_), channel_id=1, source_target_pairs={{0,8},{8,16},{16,24},{24,0},{32,40},{40,48},{48,56},{56,32},{64,72... | collective-permute-start | bytes 1572872 | tf_op jit(solution)/shard_map/ppermute | solution.py:354
  117.1 12.9 %collective-permute-start.21 = (f32[512,256]{1,0:T(8,128)S(1)}, f32[512,256]{1,0:T(8,128)S(1)}, u32[]{:S(2)}, u32[]{:S(2)}) collective-permute-start(f32[512,256]{1,0:T(8,128)S(1)} %shard_map.102.khatri_ref.refs_8_), channel_id=1, source_target_pairs={{0,24},{8,0},{16,8},{24,16},{32,56},{40,32},{48,40},{56,48},{64,88... | collective-permute-start | bytes 1572872 | tf_op jit(solution)/shard_map/ppermute | solution.py:354
  119.7 12.2 %collective-permute-start.22 = (f32[512,256]{1,0:T(8,128)S(1)}, f32[512,256]{1,0:T(8,128)S(1)}, u32[]{:S(2)}, u32[]{:S(2)}) collective-permute-start(f32[512,256]{1,0:T(8,128)S(1)} %shard_map.102.khatri_ref.refs_8_), channel_id=1, source_target_pairs={{0,32},{8,40},{16,48},{24,56},{32,64},{40,72},{48,80},{56,88},{64,... | collective-permute-start | bytes 1572872 | tf_op jit(solution)/shard_map/ppermute | solution.py:354
  132.6 2.5 %collective-permute-start.23 = (f32[4,176,256]{2,1,0:T(8,128)S(1)}, f32[4,176,256]{2,1,0:T(8,128)S(1)}, u32[]{:S(2)}, u32[]{:S(2)}) collective-permute-start(f32[4,176,256]{2,1,0:T(8,128)S(1)} %shard_map.107.refs_12_), channel_id=1, source_target_pairs={{0,1},{1,0},{2,3},{3,2},{4,5},{5,4},{6,7},{7,6},{8,9},{9,8},{10,11... | collective-permute-start | bytes 2162696 | tf_op jit(solution)/shard_map/ppermute | solution.py:367
  135.2 9.0 %collective-permute-start.24 = (f32[176,256]{1,0:T(8,128)S(1)}, f32[176,256]{1,0:T(8,128)S(1)}, u32[]{:S(2)}, u32[]{:S(2)}) collective-permute-start(f32[176,256]{1,0:T(8,128)S(1)} %get-tuple-element.156), channel_id=1, source_target_pairs={{0,4},{1,5},{2,6},{3,7},{4,0},{5,1},{6,2},{7,3},{8,12},{9,13},{10,... | collective-permute-start | bytes 540680 | tf_op jit(solution)/shard_map/ppermute | solution.py:376
  136.9 10.3 %collective-permute-start.25 = (f32[176,256]{1,0:T(8,128)S(1)}, f32[176,256]{1,0:T(8,128)S(1)}, u32[]{:S(2)}, u32[]{:S(2)}) collective-permute-start(f32[176,256]{1,0:T(8,128)S(1)} %get-tuple-element.157), channel_id=1, source_target_pairs={{0,2},{1,3},{2,4},{3,5},{4,6},{5,7},{6,0},{7,1},{8,10},{9,11},{10,... | collective-permute-start | bytes 540680 | tf_op jit(solution)/shard_map/ppermute | solution.py:376
  137.9 9.3 %collective-permute-start.26 = (f32[176,256]{1,0:T(8,128)S(1)}, f32[176,256]{1,0:T(8,128)S(1)}, u32[]{:S(2)}, u32[]{:S(2)}) collective-permute-start(f32[176,256]{1,0:T(8,128)S(1)} %get-tuple-element.158), channel_id=1, source_target_pairs={{0,6},{1,7},{2,0},{3,1},{4,2},{5,3},{6,4},{7,5},{8,14},{9,15},{10,... | collective-permute-start | bytes 540680 | tf_op jit(solution)/shard_map/ppermute | solution.py:376
  147.3 7.4 %collective-permute-start.29 = (f32[48,256]{1,0:T(8,128)S(1)}, f32[48,256]{1,0:T(8,128)S(1)}, u32[]{:S(2)}, u32[]{:S(2)}) collective-permute-start(f32[48,256]{1,0:T(8,128)S(1)} %get-tuple-element.159.refs_0_), channel_id=1, source_target_pairs={{0,6},{1,7},{2,0},{3,1},{4,2},{5,3},{6,4},{7,5},{8,14},{9,15},{10,... | collective-permute-start | bytes 147464 | tf_op jit(solution)/shard_map/ppermute | solution.py:340
  149.1 5.8 %collective-permute-start.28 = (f32[48,256]{1,0:T(8,128)S(1)}, f32[48,256]{1,0:T(8,128)S(1)}, u32[]{:S(2)}, u32[]{:S(2)}) collective-permute-start(f32[48,256]{1,0:T(8,128)S(1)} %get-tuple-element.159.refs_0_), channel_id=1, source_target_pairs={{0,4},{1,5},{2,6},{3,7},{4,0},{5,1},{6,2},{7,3},{8,12},{9,13},{10,... | collective-permute-start | bytes 147464 | tf_op jit(solution)/shard_map/ppermute | solution.py:340
  149.9 5.3 %collective-permute-start.27 = (f32[48,256]{1,0:T(8,128)S(1)}, f32[48,256]{1,0:T(8,128)S(1)}, u32[]{:S(2)}, u32[]{:S(2)}) collective-permute-start(f32[48,256]{1,0:T(8,128)S(1)} %get-tuple-element.159.refs_0_), channel_id=1, source_target_pairs={{0,2},{1,3},{2,4},{3,5},{4,6},{5,7},{6,0},{7,1},{8,10},{9,11},{10,... | collective-permute-start | bytes 147464 | tf_op jit(solution)/shard_map/ppermute | solution.py:340
  150.4 9.7 %collective-permute-start.32 = (f32[128,256]{1,0:T(8,128)S(1)}, f32[128,256]{1,0:T(8,128)S(1)}, u32[]{:S(2)}, u32[]{:S(2)}) collective-permute-start(f32[128,256]{1,0:T(8,128)S(1)} %get-tuple-element.164.refs_0_), channel_id=1, source_target_pairs={{0,6},{1,7},{2,0},{3,1},{4,2},{5,3},{6,4},{7,5},{8,14},{9,15},{10,... | collective-permute-start | bytes 393224 | tf_op jit(solution)/shard_map/ppermute | solution.py:340
  153.2 7.3 %collective-permute-start.31 = (f32[128,256]{1,0:T(8,128)S(1)}, f32[128,256]{1,0:T(8,128)S(1)}, u32[]{:S(2)}, u32[]{:S(2)}) collective-permute-start(f32[128,256]{1,0:T(8,128)S(1)} %get-tuple-element.164.refs_0_), channel_id=1, source_target_pairs={{0,4},{1,5},{2,6},{3,7},{4,0},{5,1},{6,2},{7,3},{8,12},{9,13},{10,... | collective-permute-start | bytes 393224 | tf_op jit(solution)/shard_map/ppermute | solution.py:340
  154.7 7.1 %collective-permute-start.30 = (f32[128,256]{1,0:T(8,128)S(1)}, f32[128,256]{1,0:T(8,128)S(1)}, u32[]{:S(2)}, u32[]{:S(2)}) collective-permute-start(f32[128,256]{1,0:T(8,128)S(1)} %get-tuple-element.164.refs_0_), channel_id=1, source_target_pairs={{0,2},{1,3},{2,4},{3,5},{4,6},{5,7},{6,0},{7,1},{8,10},{9,11},{10,... | collective-permute-start | bytes 393224 | tf_op jit(solution)/shard_map/ppermute | solution.py:340
  161.8 5.1 %collective-permute-start.33 = (f32[512,256]{1,0:T(8,128)S(1)}, f32[512,256]{1,0:T(8,128)S(1)}, u32[]{:S(2)}, u32[]{:S(2)}) collective-permute-start(f32[512,256]{1,0:T(8,128)S(1)} %shard_map.112.mine_ref), channel_id=1, source_target_pairs={{0,1},{1,0},{2,3},{3,2},{4,5},{5,4},{6,7},{7,6},{8,9},{9,8},{10,11... | collective-permute-start | bytes 1572872 | tf_op jit(solution)/shard_map/ppermute | solution.py:389

commit v3 on v2

--- a/solution.py
+++ b/solution.py
@@ -153,7 +153,7 @@
     out_ref[...] = rows * placed_rows(index_ref, 1, got, height)
 
 
-GROUP = 4
+GROUP = 8
 
 
 def invert_block(tiles):

time: 180 us -> 179 us (level)
  no operation moved by 1% of the time
where the time goes in v3:
time: 179 us
  blocking collectives  46.3 us (26%)
  starting transfers between devices  45 us (25%)
  Pallas kernels  44.4 us (25%)
  waiting for transfers between devices  41.4 us (23%)
    all_to_all x3, blocking collectives, exchange(): return lax.all_to_all(rows, 'row', 0, 0, tiled=True)  46.3 us
    pallas_call x31, Pallas kernels, call(): pl.pallas_call(kernel, out_shape=out, in_specs=specs or [VMEM] * len(args...  44.4 us
    ppermute x12, starting transfers between devices, from_z(): got = {step: lax.ppermute(own, 'samp', along_z(step)) for step in FAR_FIRST}  16 us
    ppermute x6, waiting for transfers between devices, sums_over_row_group(): lax.ppermute(block, 'row', in_plane(step, 2 * step))  13.9 us
    ppermute x6, waiting for transfers between devices, summed(): lax.ppermute(pairs[step], 'samp', along_z(step))  13.2 us
    ppermute x6, starting transfers between devices, summed(): lax.ppermute(pairs[step], 'samp', along_z(step))  12.2 us
    ppermute x6, starting transfers between devices, sums_over_row_group(): lax.ppermute(block, 'row', in_plane(step, 2 * step))  9.59 us
    ppermute x6, waiting for transfers between devices, sums_over_row_group(): lax.ppermute(piece, 'row', in_plane(*move))  9.45 us
  transfers between devices with their start and end apart: 34, of which 23 were waited for; matrix products, arithmetic and copies ran while one was open for 1% of the time, Pallas kernels for 20%

profile of v3, /device:TPU:0, one launch (start us, length us, event | category | flops | bytes accessed | tf_op | source)
XLA Modules:
  0.0 179.1 jit_solution(8634789147338691475)
XLA Ops:
  0.7 2.7 %shard_map.85 = (f32[16,32,256]{2,1,0:T(8,128)S(1)}, s32[2,2048]{1,0:T(2,128)S(1)}) custom-call(s32[2,2048]{1,0:T(2,128)} %bitcast.7, f32[1024,256]{1,0:T(8,128)} %b_hbm.1, f32[1024,256]{1,0:T(8,128)} %c_ref), custom_call_target="tpu_custom_call" | custom-call | flops 1000000000 | bytes 2097152 | tf_op jit(solution)/shard_map/pallas_call | solution.py:26
  3.4 18.5 %all_to_all.15.refs_1_ = f32[16,32,256]{2,1,0:T(8,128)S(1)} all-to-all(f32[16,32,256]{2,1,0:T(8,128)S(1)} %get-tuple-element.90), channel_id=1, replica_groups=mesh['row'=16,'samp'=8] {'row'}, dimensions={0} | all-to-all | bytes 1048576 | tf_op jit(solution)/shard_map/all_to_all | solution.py:430
  22.3 1.4 collective-permute-start.2
  23.8 1.6 collective-permute-start.1
  25.4 1.7 collective-permute-start
  27.1 3.9 %collective-permute-done.2.refs_3_ = f32[128,256]{1,0:T(8,128)S(1)} collective-permute-done((f32[128,256]{1,0:T(8,128)S(1)}, f32[128,256]{1,0:T(8,128)S(1)}, u32[]{:S(2)}, u32[]{:S(2)}) %collective-permute-start.2) | collective-permute-done | bytes 131104 | tf_op jit(solution)/shard_map/ppermute | solution.py:349
  31.6 2.3 %collective-permute-done.refs_1_ = f32[128,256]{1,0:T(8,128)S(1)} collective-permute-done((f32[128,256]{1,0:T(8,128)S(1)}, f32[128,256]{1,0:T(8,128)S(1)}, u32[]{:S(2)}, u32[]{:S(2)}) %collective-permute-start) | collective-permute-done | bytes 131104 | tf_op jit(solution)/shard_map/ppermute | solution.py:349
  34.5 2.8 %collective-permute-start.4 = (f32[512,256]{1,0:T(8,128)S(1)}, f32[512,256]{1,0:T(8,128)S(1)}, u32[]{:S(2)}, u32[]{:S(2)}) collective-permute-start(f32[512,256]{1,0:T(8,128)S(1)} %shard_map.87.khatri_ref.refs_8_), channel_id=1, source_target_pairs={{0,24},{8,0},{16,8},{24,16},{32,56},{40,32},{48,40},{56,48},{64,88... | collective-permute-start | bytes 1572872 | tf_op jit(solution)/shard_map/ppermute | solution.py:354
  37.3 3.9 %shard_map.88 = (bf16[1024,512]{1,0:T(8,128)(2,1)S(1)}, bf16[1024,512]{1,0:T(8,128)(2,1)S(1)}, bf16[1024,512]{1,0:T(8,128)(2,1)S(1)}, bf16[1024,512]{1,0:T(8,128...) custom-call(f32[1024,2048]{1,0:T(8,128)} %fibres_ref), custom_call_target="tpu_custom_call" | custom-call | flops 8388608 | bytes 16777216 | tf_op jit(solution)/shard_map/pallas_call | solution.py:26
  42.8 3.2 %collective-permute-done.3.khatri_ref.refs_9_ = f32[512,256]{1,0:T(8,128)S(1)} collective-permute-done((f32[512,256]{1,0:T(8,128)S(1)}, f32[512,256]{1,0:T(8,128)S(1)}, u32[]{:S(2)}, u32[]{:S(2)}) %collective-permute-start.3) | collective-permute-done | bytes 524320 | tf_op jit(solution)/shard_map/ppermute | solution.py:354
  47.5 1.2 collective-permute-done.5.khatri_ref.refs_11_
  49.5 1.8 %shard_map.94.kept_ref = f32[4,176,256]{2,1,0:T(8,128)S(1)} custom-call(bf16[1024,512]{1,0:T(8,128)(2,1)S(1)} %get-tuple-element.92.high_ref.refs_0_, bf16[1024,512]{1,0:T(8,128)(2,1)S(1)} %get-tuple-element.93.low_ref.refs_1_, bf16[1024,512]{1,0:T(8,128)(2,1)S(1)} %get-tuple-element.94.high_ref.refs_2_, ...), custom_call_target="tpu_custom_call" | custom-call | flops 1610612736 | bytes 8388608 | tf_op jit(solution)/shard_map/pallas_call | solution.py:26
  51.8 4.0 %collective-permute-start.7 = (f32[176,256]{1,0:T(8,128)S(1)}, f32[176,256]{1,0:T(8,128)S(1)}, u32[]{:S(2)}, u32[]{:S(2)}) collective-permute-start(f32[176,256]{1,0:T(8,128)S(1)} %get-tuple-element.114), channel_id=1, source_target_pairs={{0,4},{1,5},{2,6},{3,7},{4,0},{5,1},{6,2},{7,3},{8,12},{9,13},{10,... | collective-permute-start | bytes 540680 | tf_op jit(solution)/shard_map/ppermute | solution.py:376
  56.8 2.2 %collective-permute-start.9 = (f32[176,256]{1,0:T(8,128)S(1)}, f32[176,256]{1,0:T(8,128)S(1)}, u32[]{:S(2)}, u32[]{:S(2)}) collective-permute-start(f32[176,256]{1,0:T(8,128)S(1)} %get-tuple-element.116), channel_id=1, source_target_pairs={{0,6},{1,7},{2,0},{3,1},{4,2},{5,3},{6,4},{7,5},{8,14},{9,15},{10,... | collective-permute-start | bytes 540680 | tf_op jit(solution)/shard_map/ppermute | solution.py:376
  59.0 2.1 %collective-permute-done.7.b = f32[176,256]{1,0:T(8,128)S(1)} collective-permute-done((f32[176,256]{1,0:T(8,128)S(1)}, f32[176,256]{1,0:T(8,128)S(1)}, u32[]{:S(2)}, u32[]{:S(2)}) %collective-permute-start.7) | collective-permute-done | bytes 180256 | tf_op jit(solution)/shard_map/ppermute | solution.py:376
  61.1 3.4 %collective-permute-done.8.c = f32[176,256]{1,0:T(8,128)S(1)} collective-permute-done((f32[176,256]{1,0:T(8,128)S(1)}, f32[176,256]{1,0:T(8,128)S(1)}, u32[]{:S(2)}, u32[]{:S(2)}) %collective-permute-start.8) | collective-permute-done | bytes 180256 | tf_op jit(solution)/shard_map/ppermute | solution.py:376
  65.3 2.7 %collective-permute-start.12 = (f32[48,256]{1,0:T(8,128)S(1)}, f32[48,256]{1,0:T(8,128)S(1)}, u32[]{:S(2)}, u32[]{:S(2)}) collective-permute-start(f32[48,256]{1,0:T(8,128)S(1)} %get-tuple-element.117.refs_0_), channel_id=1, source_target_pairs={{0,6},{1,7},{2,0},{3,1},{4,2},{5,3},{6,4},{7,5},{8,14},{9,15},{10,... | collective-permute-start | bytes 147464 | tf_op jit(solution)/shard_map/ppermute | solution.py:340
  69.1 2.6 %collective-permute-start.15 = (f32[128,256]{1,0:T(8,128)S(1)}, f32[128,256]{1,0:T(8,128)S(1)}, u32[]{:S(2)}, u32[]{:S(2)}) collective-permute-start(f32[128,256]{1,0:T(8,128)S(1)} %get-tuple-element.122.refs_0_), channel_id=1, source_target_pairs={{0,6},{1,7},{2,0},{3,1},{4,2},{5,3},{6,4},{7,5},{8,14},{9,15},{10,... | collective-permute-start | bytes 393224 | tf_op jit(solution)/shard_map/ppermute | solution.py:340
  71.7 1.9 %collective-permute-start.14 = (f32[128,256]{1,0:T(8,128)S(1)}, f32[128,256]{1,0:T(8,128)S(1)}, u32[]{:S(2)}, u32[]{:S(2)}) collective-permute-start(f32[128,256]{1,0:T(8,128)S(1)} %get-tuple-element.122.refs_0_), channel_id=1, source_target_pairs={{0,4},{1,5},{2,6},{3,7},{4,0},{5,1},{6,2},{7,3},{8,12},{9,13},{10,... | collective-permute-start | bytes 393224 | tf_op jit(solution)/shard_map/ppermute | solution.py:340
  74.1 4.6 %shard_map.97 = (f32[128,128]{1,0:T(8,128)S(1)}, f32[128,128]{1,0:T(8,128)S(1)}, f32[128,128]{1,0:T(8,128)S(1)}) custom-call(f32[48,256]{1,0:T(8,128)S(1)} %get-tuple-element.117.refs_0_, f32[48,256]{1,0:T(8,128)S(1)} %collective-permute-done.10.refs_1_, f32[48,256]{1,0:T(8,128)S(1)} %collective-permute-done.11.refs_2_, ...), custom_call_target="tpu_custom_call" | custom-call | flops 99999997952 | bytes 524288 | tf_op jit(solution)/shard_map/pallas_call | solution.py:26
  78.8 1.2 collective-permute-done.13.refs_1_
  80.2 4.7 %shard_map.99.inverse_ref = f32[256,256]{1,0:T(8,128)S(1)} custom-call(f32[128,128]{1,0:T(8,128)S(1)} %get-tuple-element.126.a_ref, f32[128,128]{1,0:T(8,128)S(1)} %get-tuple-element.127.w_ref, f32[128,128]{1,0:T(8,128)S(1)} %get-tuple-element.128.rest_ref), custom_call_target="tpu_custom_call" | custom-call | flops 99999997952 | bytes 524288 | tf_op jit(solution)/shard_map/pallas_call | solution.py:26
  84.8 1.8 shard_map.100
  86.6 17.0 %all_to_all.16.refs_1_ = f32[16,40,256]{2,1,0:T(8,128)S(1)} all-to-all(f32[16,40,256]{2,1,0:T(8,128)S(1)} %get-tuple-element.131), channel_id=1, replica_groups=mesh['row'=16,'samp'=8] {'row'}, dimensions={0} | all-to-all | bytes 1310720 | tf_op jit(solution)/shard_map/all_to_all | solution.py:430
  104.1 1.9 %collective-permute-start.19 = (f32[128,256]{1,0:T(8,128)S(1)}, f32[128,256]{1,0:T(8,128)S(1)}, u32[]{:S(2)}, u32[]{:S(2)}) collective-permute-start(f32[128,256]{1,0:T(8,128)S(1)} %get-tuple-element.132.refs_0_), channel_id=1, source_target_pairs={{0,112},{8,120},{16,96},{24,104},{32,16},{40,24},{48,0},{56,8},{64... | collective-permute-start | bytes 393224 | tf_op jit(solution)/shard_map/ppermute | solution.py:349
  106.0 1.5 collective-permute-start.18
  107.5 1.5 collective-permute-start.17
  109.0 2.9 %collective-permute-done.19.refs_3_ = f32[128,256]{1,0:T(8,128)S(1)} collective-permute-done((f32[128,256]{1,0:T(8,128)S(1)}, f32[128,256]{1,0:T(8,128)S(1)}, u32[]{:S(2)}, u32[]{:S(2)}) %collective-permute-start.19) | collective-permute-done | bytes 131104 | tf_op jit(solution)/shard_map/ppermute | solution.py:349
  112.5 3.6 %collective-permute-done.17.refs_1_ = f32[128,256]{1,0:T(8,128)S(1)} collective-permute-done((f32[128,256]{1,0:T(8,128)S(1)}, f32[128,256]{1,0:T(8,128)S(1)}, u32[]{:S(2)}, u32[]{:S(2)}) %collective-permute-start.17) | collective-permute-done | bytes 131104 | tf_op jit(solution)/shard_map/ppermute | solution.py:349
  116.8 2.6 %collective-permute-start.21 = (f32[512,256]{1,0:T(8,128)S(1)}, f32[512,256]{1,0:T(8,128)S(1)}, u32[]{:S(2)}, u32[]{:S(2)}) collective-permute-start(f32[512,256]{1,0:T(8,128)S(1)} %shard_map.102.khatri_ref.refs_8_), channel_id=1, source_target_pairs={{0,24},{8,0},{16,8},{24,16},{32,56},{40,32},{48,40},{56,48},{64,88... | collective-permute-start | bytes 1572872 | tf_op jit(solution)/shard_map/ppermute | solution.py:354
  119.4 3.9 %shard_map.103 = (bf16[1024,512]{1,0:T(8,128)(2,1)S(1)}, bf16[1024,512]{1,0:T(8,128)(2,1)S(1)}, bf16[1024,512]{1,0:T(8,128)(2,1)S(1)}, bf16[1024,512]{1,0:T(8,12...) custom-call(f32[1024,2048]{1,0:T(8,128)} %fibres_ref.1), custom_call_target="tpu_custom_call" | custom-call | flops 8388608 | bytes 16777216 | tf_op jit(solution)/shard_map/pallas_call | solution.py:26
  124.0 1.0 broadcast_divide_fusion
  125.1 3.8 %collective-permute-done.20.khatri_ref.refs_9_ = f32[512,256]{1,0:T(8,128)S(1)} collective-permute-done((f32[512,256]{1,0:T(8,128)S(1)}, f32[512,256]{1,0:T(8,128)S(1)}, u32[]{:S(2)}, u32[]{:S(2)}) %collective-permute-start.20) | collective-permute-done | bytes 524320 | tf_op jit(solution)/shard_map/ppermute | solution.py:354
  130.4 1.2 collective-permute-done.22.khatri_ref.refs_11_
  132.4 1.8 %shard_map.108.kept_ref = f32[4,176,256]{2,1,0:T(8,128)S(1)} custom-call(bf16[1024,512]{1,0:T(8,128)(2,1)S(1)} %get-tuple-element.134.high_ref.refs_0_, bf16[1024,512]{1,0:T(8,128)(2,1)S(1)} %get-tuple-element.135.low_ref.refs_1_, bf16[1024,512]{1,0:T(8,128)(2,1)S(1)} %get-tuple-element.143.high_ref.refs_2_, ...), custom_call_target="tpu_custom_call" | custom-call | flops 1610612736 | bytes 8388608 | tf_op jit(solution)/shard_map/pallas_call | solution.py:26
  134.6 1.8 collective-permute-start.24
  137.1 2.6 %collective-permute-start.26 = (f32[176,256]{1,0:T(8,128)S(1)}, f32[176,256]{1,0:T(8,128)S(1)}, u32[]{:S(2)}, u32[]{:S(2)}) collective-permute-start(f32[176,256]{1,0:T(8,128)S(1)} %get-tuple-element.158), channel_id=1, source_target_pairs={{0,6},{1,7},{2,0},{3,1},{4,2},{5,3},{6,4},{7,5},{8,14},{9,15},{10,... | collective-permute-start | bytes 540680 | tf_op jit(solution)/shard_map/ppermute | solution.py:376
  139.7 4.0 %collective-permute-done.24.b = f32[176,256]{1,0:T(8,128)S(1)} collective-permute-done((f32[176,256]{1,0:T(8,128)S(1)}, f32[176,256]{1,0:T(8,128)S(1)}, u32[]{:S(2)}, u32[]{:S(2)}) %collective-permute-start.24) | collective-permute-done | bytes 180256 | tf_op jit(solution)/shard_map/ppermute | solution.py:376
  143.7 3.0 %collective-permute-done.25.c = f32[176,256]{1,0:T(8,128)S(1)} collective-permute-done((f32[176,256]{1,0:T(8,128)S(1)}, f32[176,256]{1,0:T(8,128)S(1)}, u32[]{:S(2)}, u32[]{:S(2)}) %collective-permute-start.25) | collective-permute-done | bytes 180256 | tf_op jit(solution)/shard_map/ppermute | solution.py:376
  146.7 1.5 collective-permute-start.29
  148.3 1.1 collective-permute-start.28
  149.9 2.7 %collective-permute-start.32 = (f32[128,256]{1,0:T(8,128)S(1)}, f32[128,256]{1,0:T(8,128)S(1)}, u32[]{:S(2)}, u32[]{:S(2)}) collective-permute-start(f32[128,256]{1,0:T(8,128)S(1)} %get-tuple-element.164.refs_0_), channel_id=1, source_target_pairs={{0,6},{1,7},{2,0},{3,1},{4,2},{5,3},{6,4},{7,5},{8,14},{9,15},{10,... | collective-permute-start | bytes 393224 | tf_op jit(solution)/shard_map/ppermute | solution.py:340
  152.6 1.2 collective-permute-start.31
  154.7 4.6 %shard_map.111 = (f32[128,128]{1,0:T(8,128)S(1)}, f32[128,128]{1,0:T(8,128)S(1)}, f32[128,128]{1,0:T(8,128)S(1)}) custom-call(f32[48,256]{1,0:T(8,128)S(1)} %get-tuple-element.159.refs_0_, f32[48,256]{1,0:T(8,128)S(1)} %collective-permute-done.27.refs_1_, f32[48,256]{1,0:T(8,128)S(1)} %collective-permute-done.28.refs_2_, ...), custom_call_target="tpu_custom_call" | custom-call | flops 99999997952 | bytes 524288 | tf_op jit(solution)/shard_map/pallas_call | solution.py:26
  159.9 1.3 collective-permute-done.30.refs_1_
  161.6 4.7 %shard_map.113.inverse_ref = f32[256,256]{1,0:T(8,128)S(1)} custom-call(f32[128,128]{1,0:T(8,128)S(1)} %get-tuple-element.168.a_ref, f32[128,128]{1,0:T(8,128)S(1)} %get-tuple-element.169.w_ref, f32[128,128]{1,0:T(8,128)S(1)} %get-tuple-element.170.rest_ref), custom_call_target="tpu_custom_call" | custom-call | flops 99999997952 | bytes 524288 | tf_op jit(solution)/shard_map/pallas_call | solution.py:26
  167.1 10.9 %all_to_all.17.got_ref = f32[16,1,256]{2,1,0:T(1,128)S(1)} all-to-all(f32[16,1,256]{2,1,0:T(1,128)S(1)} %get-tuple-element.172), channel_id=1, replica_groups=mesh['row'=16,'samp'=8] {'row'}, dimensions={0} | all-to-all | bytes 32768 | tf_op jit(solution)/shard_map/all_to_all | solution.py:430
  178.0 1.1 shard_map.115
  (62 shorter events, 18.8 us)
Async XLA Ops:
  0.6 41.3 %copy-start = (s32[2048,2]{0,1:T(2,128)S(1)}, s32[2048,2]{0,1:T(2,128)}, u32[]{:S(2)}) copy-start(s32[2048,2]{0,1:T(2,128)} %param.9) | copy-start | bytes 49156
  0.6 41.3 %copy-start.2 = (f32[1024,256]{1,0:T(8,128)S(1)}, f32[1024,256]{1,0:T(8,128)}, u32[]{:S(2)}) copy-start(f32[1024,256]{1,0:T(8,128)} %c_ref) | copy-start | bytes 3145732
  22.3 8.6 %collective-permute-start.2 = (f32[128,256]{1,0:T(8,128)S(1)}, f32[128,256]{1,0:T(8,128)S(1)}, u32[]{:S(2)}, u32[]{:S(2)}) collective-permute-start(f32[128,256]{1,0:T(8,128)S(1)} %shard_map.86.refs_0_), channel_id=1, source_target_pairs={{0,112},{8,120},{16,96},{24,104},{32,16},{40,24},{48,0},{56,8},{64... | collective-permute-start | bytes 393224 | tf_op jit(solution)/shard_map/ppermute | solution.py:349
  23.8 7.9 %collective-permute-start.1 = (f32[128,256]{1,0:T(8,128)S(1)}, f32[128,256]{1,0:T(8,128)S(1)}, u32[]{:S(2)}, u32[]{:S(2)}) collective-permute-start(f32[128,256]{1,0:T(8,128)S(1)} %shard_map.86.refs_0_), channel_id=1, source_target_pairs={{0,64},{8,72},{16,80},{24,88},{32,96},{40,104},{48,112},{56,120},{... | collective-permute-start | bytes 393224 | tf_op jit(solution)/shard_map/ppermute | solution.py:349
  25.4 8.6 %collective-permute-start = (f32[128,256]{1,0:T(8,128)S(1)}, f32[128,256]{1,0:T(8,128)S(1)}, u32[]{:S(2)}, u32[]{:S(2)}) collective-permute-start(f32[128,256]{1,0:T(8,128)S(1)} %shard_map.86.refs_0_), channel_id=1, source_target_pairs={{0,48},{8,56},{16,32},{24,40},{32,80},{40,88},{48,64},{56,72},{64,... | collective-permute-start | bytes 393224 | tf_op jit(solution)/shard_map/ppermute | solution.py:349
  34.0 12.1 %collective-permute-start.3 = (f32[512,256]{1,0:T(8,128)S(1)}, f32[512,256]{1,0:T(8,128)S(1)}, u32[]{:S(2)}, u32[]{:S(2)}) collective-permute-start(f32[512,256]{1,0:T(8,128)S(1)} %shard_map.87.khatri_ref.refs_8_), channel_id=1, source_target_pairs={{0,8},{8,16},{16,24},{24,0},{32,40},{40,48},{48,56},{56,32},{64,72... | collective-permute-start | bytes 1572872 | tf_op jit(solution)/shard_map/ppermute | solution.py:354
  34.5 12.2 %collective-permute-start.4 = (f32[512,256]{1,0:T(8,128)S(1)}, f32[512,256]{1,0:T(8,128)S(1)}, u32[]{:S(2)}, u32[]{:S(2)}) collective-permute-start(f32[512,256]{1,0:T(8,128)S(1)} %shard_map.87.khatri_ref.refs_8_), channel_id=1, source_target_pairs={{0,24},{8,0},{16,8},{24,16},{32,56},{40,32},{48,40},{56,48},{64,88... | collective-permute-start | bytes 1572872 | tf_op jit(solution)/shard_map/ppermute | solution.py:354
  37.3 11.4 %collective-permute-start.5 = (f32[512,256]{1,0:T(8,128)S(1)}, f32[512,256]{1,0:T(8,128)S(1)}, u32[]{:S(2)}, u32[]{:S(2)}) collective-permute-start(f32[512,256]{1,0:T(8,128)S(1)} %shard_map.87.khatri_ref.refs_8_), channel_id=1, source_target_pairs={{0,32},{8,40},{16,48},{24,56},{32,64},{40,72},{48,80},{56,88},{64,... | collective-permute-start | bytes 1572872 | tf_op jit(solution)/shard_map/ppermute | solution.py:354
  49.5 2.3 %collective-permute-start.6 = (f32[4,176,256]{2,1,0:T(8,128)S(1)}, f32[4,176,256]{2,1,0:T(8,128)S(1)}, u32[]{:S(2)}, u32[]{:S(2)}) collective-permute-start(f32[4,176,256]{2,1,0:T(8,128)S(1)} %shard_map.93.refs_12_), channel_id=1, source_target_pairs={{0,1},{1,0},{2,3},{3,2},{4,5},{5,4},{6,7},{7,6},{8,9},{9,8},{10,11... | collective-permute-start | bytes 2162696 | tf_op jit(solution)/shard_map/ppermute | solution.py:367
  51.8 9.3 %collective-permute-start.7 = (f32[176,256]{1,0:T(8,128)S(1)}, f32[176,256]{1,0:T(8,128)S(1)}, u32[]{:S(2)}, u32[]{:S(2)}) collective-permute-start(f32[176,256]{1,0:T(8,128)S(1)} %get-tuple-element.114), channel_id=1, source_target_pairs={{0,4},{1,5},{2,6},{3,7},{4,0},{5,1},{6,2},{7,3},{8,12},{9,13},{10,... | collective-permute-start | bytes 540680 | tf_op jit(solution)/shard_map/ppermute | solution.py:376
  55.8 8.7 %collective-permute-start.8 = (f32[176,256]{1,0:T(8,128)S(1)}, f32[176,256]{1,0:T(8,128)S(1)}, u32[]{:S(2)}, u32[]{:S(2)}) collective-permute-start(f32[176,256]{1,0:T(8,128)S(1)} %get-tuple-element.115), channel_id=1, source_target_pairs={{0,2},{1,3},{2,4},{3,5},{4,6},{5,7},{6,0},{7,1},{8,10},{9,11},{10,... | collective-permute-start | bytes 540680 | tf_op jit(solution)/shard_map/ppermute | solution.py:376
  56.8 8.4 %collective-permute-start.9 = (f32[176,256]{1,0:T(8,128)S(1)}, f32[176,256]{1,0:T(8,128)S(1)}, u32[]{:S(2)}, u32[]{:S(2)}) collective-permute-start(f32[176,256]{1,0:T(8,128)S(1)} %get-tuple-element.116), channel_id=1, source_target_pairs={{0,6},{1,7},{2,0},{3,1},{4,2},{5,3},{6,4},{7,5},{8,14},{9,15},{10,... | collective-permute-start | bytes 540680 | tf_op jit(solution)/shard_map/ppermute | solution.py:376
  65.3 8.3 %collective-permute-start.12 = (f32[48,256]{1,0:T(8,128)S(1)}, f32[48,256]{1,0:T(8,128)S(1)}, u32[]{:S(2)}, u32[]{:S(2)}) collective-permute-start(f32[48,256]{1,0:T(8,128)S(1)} %get-tuple-element.117.refs_0_), channel_id=1, source_target_pairs={{0,6},{1,7},{2,0},{3,1},{4,2},{5,3},{6,4},{7,5},{8,14},{9,15},{10,... | collective-permute-start | bytes 147464 | tf_op jit(solution)/shard_map/ppermute | solution.py:340
  68.0 5.6 %collective-permute-start.11 = (f32[48,256]{1,0:T(8,128)S(1)}, f32[48,256]{1,0:T(8,128)S(1)}, u32[]{:S(2)}, u32[]{:S(2)}) collective-permute-start(f32[48,256]{1,0:T(8,128)S(1)} %get-tuple-element.117.refs_0_), channel_id=1, source_target_pairs={{0,4},{1,5},{2,6},{3,7},{4,0},{5,1},{6,2},{7,3},{8,12},{9,13},{10,... | collective-permute-start | bytes 147464 | tf_op jit(solution)/shard_map/ppermute | solution.py:340
  68.5 5.7 %collective-permute-start.10 = (f32[48,256]{1,0:T(8,128)S(1)}, f32[48,256]{1,0:T(8,128)S(1)}, u32[]{:S(2)}, u32[]{:S(2)}) collective-permute-start(f32[48,256]{1,0:T(8,128)S(1)} %get-tuple-element.117.refs_0_), channel_id=1, source_target_pairs={{0,2},{1,3},{2,4},{3,5},{4,6},{5,7},{6,0},{7,1},{8,10},{9,11},{10,... | collective-permute-start | bytes 147464 | tf_op jit(solution)/shard_map/ppermute | solution.py:340
  69.1 9.6 %collective-permute-start.15 = (f32[128,256]{1,0:T(8,128)S(1)}, f32[128,256]{1,0:T(8,128)S(1)}, u32[]{:S(2)}, u32[]{:S(2)}) collective-permute-start(f32[128,256]{1,0:T(8,128)S(1)} %get-tuple-element.122.refs_0_), channel_id=1, source_target_pairs={{0,6},{1,7},{2,0},{3,1},{4,2},{5,3},{6,4},{7,5},{8,14},{9,15},{10,... | collective-permute-start | bytes 393224 | tf_op jit(solution)/shard_map/ppermute | solution.py:340
  71.7 7.1 %collective-permute-start.14 = (f32[128,256]{1,0:T(8,128)S(1)}, f32[128,256]{1,0:T(8,128)S(1)}, u32[]{:S(2)}, u32[]{:S(2)}) collective-permute-start(f32[128,256]{1,0:T(8,128)S(1)} %get-tuple-element.122.refs_0_), channel_id=1, source_target_pairs={{0,4},{1,5},{2,6},{3,7},{4,0},{5,1},{6,2},{7,3},{8,12},{9,13},{10,... | collective-permute-start | bytes 393224 | tf_op jit(solution)/shard_map/ppermute | solution.py:340
  73.6 6.5 %collective-permute-start.13 = (f32[128,256]{1,0:T(8,128)S(1)}, f32[128,256]{1,0:T(8,128)S(1)}, u32[]{:S(2)}, u32[]{:S(2)}) collective-permute-start(f32[128,256]{1,0:T(8,128)S(1)} %get-tuple-element.122.refs_0_), channel_id=1, source_target_pairs={{0,2},{1,3},{2,4},{3,5},{4,6},{5,7},{6,0},{7,1},{8,10},{9,11},{10,... | collective-permute-start | bytes 393224 | tf_op jit(solution)/shard_map/ppermute | solution.py:340
  80.1 23.5 %copy-start.1 = (s32[2048,2]{0,1:T(2,128)S(1)}, s32[2048,2]{0,1:T(2,128)}, u32[]{:S(2)}) copy-start(s32[2048,2]{0,1:T(2,128)} %param.9) | copy-start | bytes 49156
  80.1 4.8 %collective-permute-start.16 = (f32[512,256]{1,0:T(8,128)S(1)}, f32[512,256]{1,0:T(8,128)S(1)}, u32[]{:S(2)}, u32[]{:S(2)}) collective-permute-start(f32[512,256]{1,0:T(8,128)S(1)} %shard_map.98.mine_ref), channel_id=1, source_target_pairs={{0,1},{1,0},{2,3},{3,2},{4,5},{5,4},{6,7},{7,6},{8,9},{9,8},{10,11... | collective-permute-start | bytes 1572872 | tf_op jit(solution)/shard_map/ppermute | solution.py:389
  104.1 7.7 %collective-permute-start.19 = (f32[128,256]{1,0:T(8,128)S(1)}, f32[128,256]{1,0:T(8,128)S(1)}, u32[]{:S(2)}, u32[]{:S(2)}) collective-permute-start(f32[128,256]{1,0:T(8,128)S(1)} %get-tuple-element.132.refs_0_), channel_id=1, source_target_pairs={{0,112},{8,120},{16,96},{24,104},{32,16},{40,24},{48,0},{56,8},{64... | collective-permute-start | bytes 393224 | tf_op jit(solution)/shard_map/ppermute | solution.py:349
  106.0 6.5 %collective-permute-start.18 = (f32[128,256]{1,0:T(8,128)S(1)}, f32[128,256]{1,0:T(8,128)S(1)}, u32[]{:S(2)}, u32[]{:S(2)}) collective-permute-start(f32[128,256]{1,0:T(8,128)S(1)} %get-tuple-element.132.refs_0_), channel_id=1, source_target_pairs={{0,64},{8,72},{16,80},{24,88},{32,96},{40,104},{48,112},{56,120},{... | collective-permute-start | bytes 393224 | tf_op jit(solution)/shard_map/ppermute | solution.py:349
  107.5 8.6 %collective-permute-start.17 = (f32[128,256]{1,0:T(8,128)S(1)}, f32[128,256]{1,0:T(8,128)S(1)}, u32[]{:S(2)}, u32[]{:S(2)}) collective-permute-start(f32[128,256]{1,0:T(8,128)S(1)} %get-tuple-element.132.refs_0_), channel_id=1, source_target_pairs={{0,48},{8,56},{16,32},{24,40},{32,80},{40,88},{48,64},{56,72},{64,... | collective-permute-start | bytes 393224 | tf_op jit(solution)/shard_map/ppermute | solution.py:349
  116.1 12.8 %collective-permute-start.20 = (f32[512,256]{1,0:T(8,128)S(1)}, f32[512,256]{1,0:T(8,128)S(1)}, u32[]{:S(2)}, u32[]{:S(2)}) collective-permute-start(f32[512,256]{1,0:T(8,128)S(1)} %shard_map.102.khatri_ref.refs_8_), channel_id=1, source_target_pairs={{0,8},{8,16},{16,24},{24,0},{32,40},{40,48},{48,56},{56,32},{64,72... | collective-permute-start | bytes 1572872 | tf_op jit(solution)/shard_map/ppermute | solution.py:354
  116.8 12.9 %collective-permute-start.21 = (f32[512,256]{1,0:T(8,128)S(1)}, f32[512,256]{1,0:T(8,128)S(1)}, u32[]{:S(2)}, u32[]{:S(2)}) collective-permute-start(f32[512,256]{1,0:T(8,128)S(1)} %shard_map.102.khatri_ref.refs_8_), channel_id=1, source_target_pairs={{0,24},{8,0},{16,8},{24,16},{32,56},{40,32},{48,40},{56,48},{64,88... | collective-permute-start | bytes 1572872 | tf_op jit(solution)/shard_map/ppermute | solution.py:354
  119.4 12.2 %collective-permute-start.22 = (f32[512,256]{1,0:T(8,128)S(1)}, f32[512,256]{1,0:T(8,128)S(1)}, u32[]{:S(2)}, u32[]{:S(2)}) collective-permute-start(f32[512,256]{1,0:T(8,128)S(1)} %shard_map.102.khatri_ref.refs_8_), channel_id=1, source_target_pairs={{0,32},{8,40},{16,48},{24,56},{32,64},{40,72},{48,80},{56,88},{64,... | collective-permute-start | bytes 1572872 | tf_op jit(solution)/shard_map/ppermute | solution.py:354
  132.3 2.3 %collective-permute-start.23 = (f32[4,176,256]{2,1,0:T(8,128)S(1)}, f32[4,176,256]{2,1,0:T(8,128)S(1)}, u32[]{:S(2)}, u32[]{:S(2)}) collective-permute-start(f32[4,176,256]{2,1,0:T(8,128)S(1)} %shard_map.107.refs_12_), channel_id=1, source_target_pairs={{0,1},{1,0},{2,3},{3,2},{4,5},{5,4},{6,7},{7,6},{8,9},{9,8},{10,11... | collective-permute-start | bytes 2162696 | tf_op jit(solution)/shard_map/ppermute | solution.py:367
  134.6 9.0 %collective-permute-start.24 = (f32[176,256]{1,0:T(8,128)S(1)}, f32[176,256]{1,0:T(8,128)S(1)}, u32[]{:S(2)}, u32[]{:S(2)}) collective-permute-start(f32[176,256]{1,0:T(8,128)S(1)} %get-tuple-element.156), channel_id=1, source_target_pairs={{0,4},{1,5},{2,6},{3,7},{4,0},{5,1},{6,2},{7,3},{8,12},{9,13},{10,... | collective-permute-start | bytes 540680 | tf_op jit(solution)/shard_map/ppermute | solution.py:376
  136.4 10.3 %collective-permute-start.25 = (f32[176,256]{1,0:T(8,128)S(1)}, f32[176,256]{1,0:T(8,128)S(1)}, u32[]{:S(2)}, u32[]{:S(2)}) collective-permute-start(f32[176,256]{1,0:T(8,128)S(1)} %get-tuple-element.157), channel_id=1, source_target_pairs={{0,2},{1,3},{2,4},{3,5},{4,6},{5,7},{6,0},{7,1},{8,10},{9,11},{10,... | collective-permute-start | bytes 540680 | tf_op jit(solution)/shard_map/ppermute | solution.py:376
  137.1 9.6 %collective-permute-start.26 = (f32[176,256]{1,0:T(8,128)S(1)}, f32[176,256]{1,0:T(8,128)S(1)}, u32[]{:S(2)}, u32[]{:S(2)}) collective-permute-start(f32[176,256]{1,0:T(8,128)S(1)} %get-tuple-element.158), channel_id=1, source_target_pairs={{0,6},{1,7},{2,0},{3,1},{4,2},{5,3},{6,4},{7,5},{8,14},{9,15},{10,... | collective-permute-start | bytes 540680 | tf_op jit(solution)/shard_map/ppermute | solution.py:376
  146.7 7.1 %collective-permute-start.29 = (f32[48,256]{1,0:T(8,128)S(1)}, f32[48,256]{1,0:T(8,128)S(1)}, u32[]{:S(2)}, u32[]{:S(2)}) collective-permute-start(f32[48,256]{1,0:T(8,128)S(1)} %get-tuple-element.159.refs_0_), channel_id=1, source_target_pairs={{0,6},{1,7},{2,0},{3,1},{4,2},{5,3},{6,4},{7,5},{8,14},{9,15},{10,... | collective-permute-start | bytes 147464 | tf_op jit(solution)/shard_map/ppermute | solution.py:340
  148.3 6.1 %collective-permute-start.28 = (f32[48,256]{1,0:T(8,128)S(1)}, f32[48,256]{1,0:T(8,128)S(1)}, u32[]{:S(2)}, u32[]{:S(2)}) collective-permute-start(f32[48,256]{1,0:T(8,128)S(1)} %get-tuple-element.159.refs_0_), channel_id=1, source_target_pairs={{0,4},{1,5},{2,6},{3,7},{4,0},{5,1},{6,2},{7,3},{8,12},{9,13},{10,... | collective-permute-start | bytes 147464 | tf_op jit(solution)/shard_map/ppermute | solution.py:340
  149.4 5.3 %collective-permute-start.27 = (f32[48,256]{1,0:T(8,128)S(1)}, f32[48,256]{1,0:T(8,128)S(1)}, u32[]{:S(2)}, u32[]{:S(2)}) collective-permute-start(f32[48,256]{1,0:T(8,128)S(1)} %get-tuple-element.159.refs_0_), channel_id=1, source_target_pairs={{0,2},{1,3},{2,4},{3,5},{4,6},{5,7},{6,0},{7,1},{8,10},{9,11},{10,... | collective-permute-start | bytes 147464 | tf_op jit(solution)/shard_map/ppermute | solution.py:340
  149.9 9.4 %collective-permute-start.32 = (f32[128,256]{1,0:T(8,128)S(1)}, f32[128,256]{1,0:T(8,128)S(1)}, u32[]{:S(2)}, u32[]{:S(2)}) collective-permute-start(f32[128,256]{1,0:T(8,128)S(1)} %get-tuple-element.164.refs_0_), channel_id=1, source_target_pairs={{0,6},{1,7},{2,0},{3,1},{4,2},{5,3},{6,4},{7,5},{8,14},{9,15},{10,... | collective-permute-start | bytes 393224 | tf_op jit(solution)/shard_map/ppermute | solution.py:340
  152.6 7.3 %collective-permute-start.31 = (f32[128,256]{1,0:T(8,128)S(1)}, f32[128,256]{1,0:T(8,128)S(1)}, u32[]{:S(2)}, u32[]{:S(2)}) collective-permute-start(f32[128,256]{1,0:T(8,128)S(1)} %get-tuple-element.164.refs_0_), channel_id=1, source_target_pairs={{0,4},{1,5},{2,6},{3,7},{4,0},{5,1},{6,2},{7,3},{8,12},{9,13},{10,... | collective-permute-start | bytes 393224 | tf_op jit(solution)/shard_map/ppermute | solution.py:340
  153.8 7.4 %collective-permute-start.30 = (f32[128,256]{1,0:T(8,128)S(1)}, f32[128,256]{1,0:T(8,128)S(1)}, u32[]{:S(2)}, u32[]{:S(2)}) collective-permute-start(f32[128,256]{1,0:T(8,128)S(1)} %get-tuple-element.164.refs_0_), channel_id=1, source_target_pairs={{0,2},{1,3},{2,4},{3,5},{4,6},{5,7},{6,0},{7,1},{8,10},{9,11},{10,... | collective-permute-start | bytes 393224 | tf_op jit(solution)/shard_map/ppermute | solution.py:340
  161.3 5.0 %collective-permute-start.33 = (f32[512,256]{1,0:T(8,128)S(1)}, f32[512,256]{1,0:T(8,128)S(1)}, u32[]{:S(2)}, u32[]{:S(2)}) collective-permute-start(f32[512,256]{1,0:T(8,128)S(1)} %shard_map.112.mine_ref), channel_id=1, source_target_pairs={{0,1},{1,0},{2,3},{3,2},{4,5},{5,4},{6,7},{7,6},{8,9},{9,8},{10,11... | collective-permute-start | bytes 1572872 | tf_op jit(solution)/shard_map/ppermute | solution.py:389
